TPU v7x, 128 devices: a whole 4x4x4 slice. The times are simulated.
128 devices in a mesh: col: 16 (over y_hi, x, core), band: 8 (over z, y_lo).
Axes of the slice: x: 4, y: 4 (y_hi: 2, y_lo: 2; y = y_hi * 2 + y_lo), z: 4, core: 2. Of those that a mesh axis runs over, the one named last changes fastest.
Arguments:
- left_view: bfloat16 [320, 8, 4096], P(None, 'band', 'col'), may hold values from -6 to 6
- right_view: bfloat16 [320, 8, 4096], P(None, 'band', 'col'), may hold values from -6 to 6
- first_weight: bfloat16 [3, 3, 320, 320], replicated, may hold values from -0.109375 to 0.109375
- second_weight: bfloat16 [3, 3, 320, 320], replicated, may hold values from -0.109375 to 0.109375
- agg_weight: bfloat16 [3, 3, 32, 3, 40], replicated, may hold values from -0.1875 to 0.1875
Outputs:
- aggregated: bfloat16 [32, 192, 8, 4096], P(None, 'band', None, 'col')
All inputs are finite; a program needn't handle non-finite values.
Results may differ from a plain program's by a relative error of at most 0.0067.
Values may be sent and summed in bfloat16 or wider, within the bound.
No kernel may reach another device: no remote copies, remote signals or barrier semaphores. Data moves between devices by JAX's collectives and lax.ppermute only.
A program may use at most 256 MiB of HBM per device.

v0:
```python
import jax
import jax.numpy as jnp
from jax import lax
from jax.sharding import PartitionSpec as P

G = 40
D = 192


def padded_2(shard, sides, width):
    for axis, dim in sides:
        devices, length = (lax.axis_size(axis), shard.shape[dim])
        up = [(i, (i + 1) % devices) for i in range(devices - 1)]
        down = [(j, i) for i, j in up]
        last = lax.slice_in_dim(shard, length - width, length, axis=dim)
        initial = lax.slice_in_dim(shard, 0, width, axis=dim)
        before = lax.ppermute(last, axis, up)
        after = lax.ppermute(initial, axis, down)
        shard = jnp.concatenate([before, shard, after], axis=dim)
    return shard


def from_behind(shard, axis, by):
    devices = lax.axis_size(axis)
    pairs = [(i, i + by) for i in range(devices) if 0 <= i + by < devices]
    return lax.ppermute(shard, axis, pairs)


def conv_plane(views, weight):
    height = views.shape[2]
    width = views.shape[3]
    padded = padded_2(views, (("col", 3), ("band", 2)), 1)
    summed = jnp.zeros((views.shape[0], weight.shape[2], height, width), jnp.float32)
    for row_tap in range(3):
        for col_tap in range(3):
            summed = summed + jnp.einsum(
                "oc,vchw->vohw",
                weight[row_tap, col_tap],
                padded[:, :, row_tap : row_tap + height, col_tap : col_tap + width],
                preferred_element_type=jnp.float32,
            )
    return summed


def aggregate(padded, weight):
    depth = padded.shape[0] - 2
    height = padded.shape[2] - 2
    width = padded.shape[3] - 2
    summed = jnp.zeros((weight.shape[2], depth, height, width), jnp.float32)
    for row_tap in range(3):
        stacked = jnp.stack(
            [
                padded[:, :, row_tap : row_tap + height, col_tap : col_tap + width]
                for col_tap in range(3)
            ],
            axis=1,
        )
        for disp_tap in range(3):
            summed = summed + jnp.einsum(
                "fkg,dkghw->fdhw",
                weight[disp_tap, row_tap],
                stacked[disp_tap : disp_tap + depth],
                preferred_element_type=jnp.float32,
            )
    return summed


def shards(left_view, right_view, first_weight, second_weight, agg_weight):
    views = jnp.stack([left_view, right_view])
    hidden = jax.nn.relu(conv_plane(views, first_weight)).astype(jnp.bfloat16)
    features = (views.astype(jnp.float32) + conv_plane(hidden, second_weight)).astype(jnp.bfloat16)
    left_feat = features[0]
    right_feat = features[1]
    col_count = right_feat.shape[2]
    right_strip = from_behind(right_feat[:, :, col_count - D :], "col", 1)
    extended = jnp.concatenate([right_strip, right_feat], axis=2)
    left_all, right_all = (
        lax.all_gather(left_feat, "band", axis=1, tiled=True),
        lax.all_gather(extended, "band", axis=1, tiled=True),
    )
    channels = left_all.shape[0]
    row_count = left_all.shape[1]
    band_size = D // lax.axis_size("band")
    band_first = lax.axis_index("band") * band_size
    left_wide = left_all.astype(jnp.float32)

    def one_disp(offset):
        disparity = band_first - 1 + offset
        inside = ((disparity >= 0) & (disparity < D)).astype(jnp.float32)
        clipped = jnp.clip(disparity, 0, D - 1)
        shifted = lax.dynamic_slice_in_dim(right_all, D - clipped, col_count, 2)
        products = left_wide * shifted.astype(jnp.float32)
        return (
            products.reshape(G, channels // G, row_count, col_count).mean(axis=1) * inside
        ).astype(jnp.bfloat16)

    volume = lax.map(one_disp, jnp.arange(band_size + 2, dtype=jnp.int32))
    padded = padded_2(volume, (("col", 3),), 1)
    padded = jnp.pad(padded, ((0, 0), (0, 0), (1, 1), (0, 0)))
    return jax.nn.relu(aggregate(padded, agg_weight)).astype(jnp.bfloat16)


def solution(mesh):
    return jax.shard_map(
        shards,
        mesh=mesh,
        in_specs=(P(None, "band", "col"), P(None, "band", "col"), P(), P(), P()),
        out_specs=P(None, "band", None, "col"),
        check_vma=False,
    )
```

profile of v0, /device:TPU:20, one launch (start us, length us, event | category | flops | bytes accessed | tf_op | source)
XLA Modules:
  0.0 519.1 jit_solution(2958290667865594828)
XLA Ops:
  9.7 2.4 collective-permute-start
  12.6 3.8 collective-permute-done
  20.6 4.6 collective-permute-start.2
  26.7 7.2 %collective-permute-done.3 = bf16[2,320,1,258]{3,1,0,2:T(8,128)(2,1)S(1)} collective-permute-done((bf16[2,320,1,258]{3,1,0,2:T(8,128)(2,1)S(1)}, bf16[2,320,1,258]{3,1,0,2:T(8,128)(2,1)S(1)}, u32[]{:S(2)}, u32[]{:S(2)}) %collective-permute-start.3) | collective-permute-done | bytes 330272 | tf_op jit(solution)/shard_map/ppermute | solution.py:18
  40.8 2.4 collective-permute-start.4
  43.6 3.8 collective-permute-done.4
  49.4 7.6 %collective-permute-start.6 = (bf16[2,320,1,258]{3,1,0,2:T(8,128)(2,1)S(1)}, bf16[2,320,1,258]{3,1,0,2:T(8,128)(2,1)S(1)}, u32[]{:S(2)}, u32[]{:S(2)}) collective-permute-start(bf16[2,320,1,258]{3,1,0,2:T(8,128)(2,1)S(1)} %pad_maximum_fusion.6), channel_id=1, source_target_pairs={{0,1},{1,2},{2,3},{3,4},{4,5},{5,6},{6,7},{8,9},{9,10},{10,11},{11... | collective-permute-start | bytes 990728 | tf_op jit(solution)/shard_map/ppermute | solution.py:17
  57.4 9.4 %collective-permute-done.7 = bf16[2,320,1,258]{3,1,0,2:T(8,128)(2,1)S(1)} collective-permute-done((bf16[2,320,1,258]{3,1,0,2:T(8,128)(2,1)S(1)}, bf16[2,320,1,258]{3,1,0,2:T(8,128)(2,1)S(1)}, u32[]{:S(2)}, u32[]{:S(2)}) %collective-permute-start.7) | collective-permute-done | bytes 330272 | tf_op jit(solution)/shard_map/ppermute | solution.py:18
  72.6 4.7 collective-permute-done.8
  78.2 44.9 %all-gather.6.cloned.1.call-done = bf16[1,320,8,256]{3,1,0,2:T(8,128)(2,1)} async-done(((bf16[1,320,1,256]{3,1,0,2:T(8,128)(2,1)}), bf16[1,320,8,256]{3,1,0,2:T(8,128)(2,1)}) %all-gather.6.cloned.1.call-update) | async-done | bytes 1310736 | tf_op jit(solution)/shard_map/all_gather | solution.py:78
  124.7 3.0 copy.21
  127.7 58.4 %all-gather.4.cloned.1.call-done = bf16[320,8,448]{2,0,1:T(8,128)(2,1)} async-done(((bf16[320,1,448]{2,0,1:T(8,128)(2,1)}), bf16[320,8,448]{2,0,1:T(8,128)(2,1)}) %all-gather.4.cloned.1.call-update) | async-done | bytes 2293776 | tf_op jit(solution)/shard_map/all_gather | solution.py:79
  186.1 178.5 %while.12 = (s32[]{:T(128)}, bf16[26,40,8,256]{3,2,1,0:T(8,128)(2,1)}, s32[26]{0:T(128)S(1)}, s32[]{:T(128)}, bf16[320,8,448]{2,0,1:T(8,128)(2,1)}, /*index=5*/f...) while((s32[]{:T(128)}, ...), condition=%wide.region_2.3_spmd, body=%wide.region_0.2_spmd.sunk | while | flops 2048013 | bytes 12615957 | solution.py:97
  187.2 2.2 constant_dynamic-slice_fusion.2
  189.4 2.6 convert_multiply_fusion.2
  194.1 2.2 constant_dynamic-slice_fusion.2
  196.2 2.6 convert_multiply_fusion.2
  200.9 2.2 constant_dynamic-slice_fusion.2
  203.1 2.6 convert_multiply_fusion.2
  207.8 2.2 constant_dynamic-slice_fusion.2
  210.0 2.6 convert_multiply_fusion.2
  214.7 2.2 constant_dynamic-slice_fusion.2
  216.8 2.6 convert_multiply_fusion.2
  223.7 2.6 convert_multiply_fusion.2
  230.6 2.6 convert_multiply_fusion.2
  237.4 2.6 convert_multiply_fusion.2
  244.3 2.6 convert_multiply_fusion.2
  251.2 2.6 convert_multiply_fusion.2
  258.0 2.6 convert_multiply_fusion.2
  264.9 2.6 convert_multiply_fusion.2
  271.7 2.6 convert_multiply_fusion.2
  278.6 2.6 convert_multiply_fusion.2
  285.5 2.6 convert_multiply_fusion.2
  292.3 2.6 convert_multiply_fusion.2
  299.2 2.6 convert_multiply_fusion.2
  306.1 2.6 convert_multiply_fusion.2
  312.9 2.6 convert_multiply_fusion.2
  319.8 2.6 convert_multiply_fusion.2
  326.7 2.6 convert_multiply_fusion.2
  333.6 2.6 convert_multiply_fusion.2
  340.4 2.6 convert_multiply_fusion.2
  347.3 2.6 convert_multiply_fusion.2
  354.1 2.6 convert_multiply_fusion.2
  361.0 2.6 convert_multiply_fusion.2
  364.6 14.9 %copy.22 = bf16[26,40,8,256]{1,2,3,0:T(8,128)(2,1)} copy(bf16[26,40,8,256]{3,2,1,0:T(8,128)(2,1)} %get-tuple-element.85) | data formatting | bytes 8519680 | tf_op jit(solution)/shard_map/while | solution.py:97
  382.3 2.4 collective-permute-start.9
  384.7 5.4 %copy.81 = bf16[26,40,8,256]{3,1,2,0:T(8,128)(2,1)} copy(bf16[26,40,8,256]{3,2,1,0:T(8,128)(2,1)} %get-tuple-element.85) | data formatting | bytes 8519680 | tf_op jit(solution)/shard_map/while | solution.py:97
  390.2 2.4 copy.26
  392.5 2.4 copy.24
  395.0 9.9 %fusion.13 = bf16[26,40,10,258]{3,1,2,0:T(8,128)(2,1)S(1)} fusion(bf16[26,40,8,1]{3,1,2,0:T(8,128)(2,1)} %copy.26, bf16[26,40,8,256]{3,1,2,0:T(8,128)(2,1)} %copy.81, bf16[26,40,8,1]{3,1,2,0:T(8,128)(2,1)} %copy.24), kind=kLoop, calls=%fused_computation.21 | loop fusion | flops 32198400 | bytes 9659520 | tf_op jit(solution)/shard_map/concatenate | solution.py:19
  404.9 4.5 fusion.17
  409.4 5.9 %fusion.106 = f32[24,8,256,32,1]{2,3,4,1,0:T(8,128)} fusion(bf16[3,3,32,3,40]{4,2,3,1,0:T(8,128)(2,1)S(1)} %copy-done.11, bf16[26,1,40,8,256]{4,2,1,3,0:T(8,128)(2,1)S(1)} %get-tuple-element.122, bf16[26,1,40,8,256]{4,2,1,3,0:T(8,128)(2,1)S(1)} %bitcast.326, bf16[26,1,40,8,256]{4,2,1,3,0:T(8,128)(2,1)S(1)} %get-tuple-element.121), kind=kOutput, calls=%fused_computation.158 | convolution fusion | flops 415825920 | bytes 19095552 | tf_op jit(solution)/shard_map/fkg,dkghw->fdhw/dot_general | solution.py:59
  415.3 5.2 fusion.108
  420.5 8.9 %slice_bitcast_fusion.5 = (bf16[26,1,40,8,256]{4,2,1,3,0:T(8,128)(2,1)}, bf16[26,1,40,8,256]{4,2,3,0,1:T(8,128)(2,1)S(1)}, bf16[26,1,40,8,256]{4,2,3,0,1:T(8,128...) fusion(bf16[26,40,10,258]{3,1,2,0:T(8,128)(2,1)S(1)} %fusion.13), kind=kLoop, calls=%fused_computation.41 | loop fusion | bytes 51118080 | tf_op jit(solution)/shard_map/stack | solution.py:51
  429.4 7.4 %fusion.110 = f32[24,8,256,32,1]{2,3,4,1,0:T(8,128)} fusion(bf16[3,3,32,3,40]{4,2,3,1,0:T(8,128)(2,1)S(1)} %copy-done.11, bf16[26,1,40,8,256]{4,2,1,3,0:T(8,128)(2,1)} %get-tuple-element.118, bf16[26,1,40,8,256]{4,2,1,3,0:T(8,128)(2,1)} %get-tuple-element.119, bf16[26,1,40,8,256]{4,2,1,3,0:T(8,128)(2,1)} %get-tuple-element.115), kind=kOutput, calls=%fused_computation.162 | convolution fusion | flops 415825920 | bytes 19095552 | tf_op jit(solution)/shard_map/fkg,dkghw->fdhw/dot_general | solution.py:59
  439.8 5.1 fusion.112
  444.9 5.2 %fusion.114 = f32[24,8,256,32,1]{2,3,4,1,0:T(8,128)} fusion(bf16[3,3,32,3,40]{4,2,3,1,0:T(8,128)(2,1)S(1)} %copy-done.11, bf16[26,1,40,8,256]{4,2,1,3,0:T(8,128)(2,1)S(1)} %copy-done.7, bf16[26,1,40,8,256]{4,2,1,3,0:T(8,128)(2,1)S(1)} %copy-done.8, bf16[26,1,40,8,256]{4,2,1,3,0:T(8,128)(2,1)S(1)} %copy-done.6), kind=kOutput, calls=%fused_computation.166 | convolution fusion | flops 415825920 | bytes 19095552 | tf_op jit(solution)/shard_map/fkg,dkghw->fdhw/dot_general | solution.py:59
  450.1 4.6 pad_maximum_fusion.2
  454.7 9.1 %fusion.131 = (bf16[24,3,40,8,256]{4,2,3,0,1:T(8,128)(2,1)S(1)}, bf16[24,3,40,8,256]{4,2,3,0,1:T(8,128)(2,1)}, bf16[24,3,40,8,256]{4,2,3,0,1:T(8,128)(2,1)}) fusion(bf16[26,3,40,8,256]{4,2,3,0,1:T(8,128)(2,1)S(1)} %pad_maximum_fusion.2), kind=kLoop, calls=%fused_computation.184 | loop fusion | bytes 70778880 | tf_op jit(solution)/shard_map/slice | solution.py:62
  463.8 8.7 %fusion.3 = f32[24,8,256,32,1]{2,3,0,1,4:T(8,128)} fusion(bf16[24,3,40,8,256]{4,2,3,0,1:T(8,128)(2,1)} %get-tuple-element.113, bf16[3,3,32,3,40]{4,2,3,1,0:T(8,128)(2,1)} %param.11), kind=kOutput, calls=%fused_computation.11 | convolution fusion | flops 377487360 | bytes 18112512 | tf_op jit(solution)/shard_map/fkg,dkghw->fdhw/dot_general | solution.py:59
  472.5 8.7 %fusion.5 = f32[24,8,256,32,1]{2,3,0,1,4:T(8,128)} fusion(bf16[24,3,40,8,256]{4,2,3,0,1:T(8,128)(2,1)} %get-tuple-element.114, bf16[3,3,32,3,40]{4,2,3,1,0:T(8,128)(2,1)} %param.11), kind=kOutput, calls=%fused_computation.13 | convolution fusion | flops 377487360 | bytes 18112512 | tf_op jit(solution)/shard_map/fkg,dkghw->fdhw/dot_general | solution.py:59
  481.3 4.4 fusion.7
  485.6 21.3 %fusion.18 = bf16[32,24,8,256]{3,0,2,1:T(8,128)(2,1)} fusion(f32[24,8,256,32,1]{2,3,0,1,4:T(8,128)} %fusion.3, f32[24,8,256,32,1]{2,3,0,1,4:T(8,128)} %fusion.5, f32[24,8,256,32,1]{2,3,0,1,4:T(8,128)} %fusion.7, f32[24,8,256,32,1]{2,3,4,1,0:T(8,128)} %fusion.106, f32[24,8,256,32,1]{2,3,4,1,0:T(8,128)} %fusion.108, f32[24,8,256,32,1]{2,3,4,1,0:T(8,128)} %fusion.110, ...), kind=kOutput, calls=%fused_computation.42 | convolution fusion | flops 431554560 | bytes 66281472 | tf_op jit(solution)/shard_map/fkg,dkghw->fdhw/dot_general | solution.py:59
  507.0 5.3 %copy.37 = bf16[32,24,8,256]{3,2,1,0:T(8,128)(2,1)} copy(bf16[32,24,8,256]{3,0,2,1:T(8,128)(2,1)} %fusion.18) | data formatting | bytes 6291456 | tf_op jit(solution)/shard_map/convert_element_type | solution.py:100
  (173 shorter events, 116.3 us)
Async XLA Ops:
  6.5 30.1 %copy-start.9 = (bf16[3,3,320,320]{3,2,1,0:T(8,128)(2,1)S(1)}, bf16[3,3,320,320]{3,2,1,0:T(8,128)(2,1)}, u32[]{:S(2)}) copy-start(bf16[3,3,320,320]{3,2,1,0:T(8,128)(2,1)} %param.9) | copy-start | bytes 5529604
  6.5 116.6 %all-gather.6.cloned.1.call-start = ((), (), s32[]{:S(2)}) async-start(), calls=%async_computation.1 | async-start | bytes 1474560 | tf_op jit(solution)/shard_map/all_gather | solution.py:78
  7.8 4.7 collective-permute-start.1
  9.7 6.6 %collective-permute-start = (bf16[2,320,1,1]{3,1,0,2:T(8,128)(2,1)S(1)}, bf16[2,320,1,1]{3,1,0,2:T(8,128)(2,1)S(1)}, u32[]{:S(2)}, u32[]{:S(2)}) collective-permute-start(bf16[2,320,1,1]{3,1,0,2:T(8,128)(2,1)S(1)} %get-tuple-element.129), channel_id=1, source_target_pairs={{0,8},{8,16},{16,24},{24,32},{32,40},{40,48},{48,56},{56,64},{64,7... | collective-permute-start | bytes 3848 | tf_op jit(solution)/shard_map/ppermute | solution.py:17
  17.7 20.6 %copy-start.4 = (bf16[320,1,256]{2,0,1:T(8,128)(2,1)S(1)}, bf16[320,1,256]{2,0,1:T(8,128)(2,1)}, u32[]{:S(2)}) copy-start(bf16[320,1,256]{2,0,1:T(8,128)(2,1)} %param.7) | copy-start | bytes 491524
  17.7 20.6 %copy-start.5 = (bf16[320,1,256]{2,0,1:T(8,128)(2,1)S(1)}, bf16[320,1,256]{2,0,1:T(8,128)(2,1)}, u32[]{:S(2)}) copy-start(bf16[320,1,256]{2,0,1:T(8,128)(2,1)} %param.8) | copy-start | bytes 491524
  17.7 16.2 %collective-permute-start.3 = (bf16[2,320,1,258]{3,1,0,2:T(8,128)(2,1)S(1)}, bf16[2,320,1,258]{3,1,0,2:T(8,128)(2,1)S(1)}, u32[]{:S(2)}, u32[]{:S(2)}) collective-permute-start(bf16[2,320,1,258]{3,1,0,2:T(8,128)(2,1)S(1)} %pad_maximum_fusion.5), channel_id=1, source_target_pairs={{1,0},{2,1},{3,2},{4,3},{5,4},{6,5},{7,6},{9,8},{10,9},{11,10},{12... | collective-permute-start | bytes 990728 | tf_op jit(solution)/shard_map/ppermute | solution.py:18
  20.6 16.4 %collective-permute-start.2 = (bf16[2,320,1,258]{3,1,0,2:T(8,128)(2,1)S(1)}, bf16[2,320,1,258]{3,1,0,2:T(8,128)(2,1)S(1)}, u32[]{:S(2)}, u32[]{:S(2)}) collective-permute-start(bf16[2,320,1,258]{3,1,0,2:T(8,128)(2,1)S(1)} %pad_maximum_fusion.5), channel_id=1, source_target_pairs={{0,1},{1,2},{2,3},{3,4},{4,5},{5,6},{6,7},{8,9},{9,10},{10,11},{11... | collective-permute-start | bytes 990728 | tf_op jit(solution)/shard_map/ppermute | solution.py:17
  36.6 12.4 %copy-start.10 = (bf16[3,3,320,320]{3,2,1,0:T(8,128)(2,1)S(1)}, bf16[3,3,320,320]{3,2,1,0:T(8,128)(2,1)}, u32[]{:S(2)}) copy-start(bf16[3,3,320,320]{3,2,1,0:T(8,128)(2,1)} %param.10) | copy-start | bytes 5529604
  38.9 4.7 collective-permute-start.5
  40.8 6.6 %collective-permute-start.4 = (bf16[2,320,1,1]{3,1,0,2:T(8,128)(2,1)S(1)}, bf16[2,320,1,1]{3,1,0,2:T(8,128)(2,1)S(1)}, u32[]{:S(2)}, u32[]{:S(2)}) collective-permute-start(bf16[2,320,1,1]{3,1,0,2:T(8,128)(2,1)S(1)} %get-tuple-element.127), channel_id=1, source_target_pairs={{0,8},{8,16},{16,24},{24,32},{32,40},{40,48},{48,56},{56,64},{64,7... | collective-permute-start | bytes 3848 | tf_op jit(solution)/shard_map/ppermute | solution.py:17
  47.7 19.1 %collective-permute-start.7 = (bf16[2,320,1,258]{3,1,0,2:T(8,128)(2,1)S(1)}, bf16[2,320,1,258]{3,1,0,2:T(8,128)(2,1)S(1)}, u32[]{:S(2)}, u32[]{:S(2)}) collective-permute-start(bf16[2,320,1,258]{3,1,0,2:T(8,128)(2,1)S(1)} %pad_maximum_fusion.6), channel_id=1, source_target_pairs={{1,0},{2,1},{3,2},{4,3},{5,4},{6,5},{7,6},{9,8},{10,9},{11,10},{12... | collective-permute-start | bytes 990728 | tf_op jit(solution)/shard_map/ppermute | solution.py:18
  49.4 18.6 %collective-permute-start.6 = (bf16[2,320,1,258]{3,1,0,2:T(8,128)(2,1)S(1)}, bf16[2,320,1,258]{3,1,0,2:T(8,128)(2,1)S(1)}, u32[]{:S(2)}, u32[]{:S(2)}) collective-permute-start(bf16[2,320,1,258]{3,1,0,2:T(8,128)(2,1)S(1)} %pad_maximum_fusion.6), channel_id=1, source_target_pairs={{0,1},{1,2},{2,3},{3,4},{4,5},{5,6},{6,7},{8,9},{9,10},{10,11},{11... | collective-permute-start | bytes 990728 | tf_op jit(solution)/shard_map/ppermute | solution.py:17
  70.5 115.6 %all-gather.4.cloned.1.call-start = ((), (), s32[]{:S(2)}) async-start(), calls=%async_computation | async-start | bytes 2949120 | tf_op jit(solution)/shard_map/all_gather | solution.py:79
  70.7 6.6 %collective-permute-start.8 = (bf16[320,1,192]{2,0,1:T(8,128)(2,1)S(1)}, bf16[320,1,192]{2,0,1:T(8,128)(2,1)S(1)}, u32[]{:S(2)}, u32[]{:S(2)}) collective-permute-start(bf16[320,1,192]{2,0,1:T(8,128)(2,1)S(1)} %slice.305), channel_id=1, source_target_pairs={{0,8},{8,16},{16,24},{24,32},{32,40},{40,48},{48,56},{56,64},{64,7... | collective-permute-start | bytes 368648 | tf_op jit(solution)/shard_map/ppermute | solution.py:26
  380.4 9.8 %collective-permute-start.10 = (bf16[26,40,8,1]{1,2,3,0:T(8,128)(2,1)S(1)}, bf16[26,40,8,1]{1,2,3,0:T(8,128)(2,1)S(1)}, u32[]{:S(2)}, u32[]{:S(2)}) collective-permute-start(bf16[26,40,8,1]{1,2,3,0:T(8,128)(2,1)S(1)} %get-tuple-element.111), channel_id=1, source_target_pairs={{8,0},{16,8},{24,16},{32,24},{40,32},{48,40},{56,48},{64,56},{72,6... | collective-permute-start | bytes 49928 | tf_op jit(solution)/shard_map/ppermute | solution.py:18
  382.3 10.3 %collective-permute-start.9 = (bf16[26,40,8,1]{1,2,3,0:T(8,128)(2,1)S(1)}, bf16[26,40,8,1]{1,2,3,0:T(8,128)(2,1)S(1)}, u32[]{:S(2)}, u32[]{:S(2)}) collective-permute-start(bf16[26,40,8,1]{1,2,3,0:T(8,128)(2,1)S(1)} %get-tuple-element.110), channel_id=1, source_target_pairs={{0,8},{8,16},{16,24},{24,32},{32,40},{40,48},{48,56},{56,64},{64,7... | collective-permute-start | bytes 49928 | tf_op jit(solution)/shard_map/ppermute | solution.py:17
  392.5 12.3 %slice-start = ((s8[4259840]{0:T(1024)(128)(4,1)}), s8[65536]{0:T(1024)(128)(4,1)S(1)}, s32[]{:S(2)}) async-start(s8[4259840]{0:T(1024)(128)(4,1)} %bitcast.324), calls=%async_computation.2 | async-start | bytes 131072
  395.0 9.9 %slice-start.1 = ((s8[4259840]{0:T(1024)(128)(4,1)}), s8[4194304]{0:T(1024)(128)(4,1)S(1)}, s32[]{:S(2)}) async-start(s8[4259840]{0:T(1024)(128)(4,1)} %bitcast.324), calls=%async_computation.3 | async-start | bytes 8388608
  395.0 9.9 %copy-start = (bf16[26,40,8,1]{3,1,2,0:T(8,128)(2,1)S(1)}, bf16[26,40,8,1]{3,1,2,0:T(8,128)(2,1)}, u32[]{:S(2)}) copy-start(bf16[26,40,8,1]{3,1,2,0:T(8,128)(2,1)} %copy.26) | copy-start | bytes 49924
  395.0 9.9 %copy-start.1 = (bf16[26,40,8,1]{3,1,2,0:T(8,128)(2,1)S(1)}, bf16[26,40,8,1]{3,1,2,0:T(8,128)(2,1)}, u32[]{:S(2)}) copy-start(bf16[26,40,8,1]{3,1,2,0:T(8,128)(2,1)} %copy.24) | copy-start | bytes 49924
  404.9 4.5 copy-start.11
  409.4 5.9 %copy-start.2 = (bf16[26,1,40,8,256]{4,2,1,3,0:T(8,128)(2,1)}, bf16[26,1,40,8,256]{4,2,1,3,0:T(8,128)(2,1)S(1)}, u32[]{:S(2)}) copy-start(bf16[26,1,40,8,256]{4,2,1,3,0:T(8,128)(2,1)S(1)} %get-tuple-element.121) | copy-start | bytes 12779524
  409.4 5.9 %copy-start.3 = (bf16[26,1,40,8,256]{4,2,1,3,0:T(8,128)(2,1)}, bf16[26,1,40,8,256]{4,2,1,3,0:T(8,128)(2,1)S(1)}, u32[]{:S(2)}) copy-start(bf16[26,1,40,8,256]{4,2,1,3,0:T(8,128)(2,1)S(1)} %get-tuple-element.122) | copy-start | bytes 12779524
  429.4 7.4 %copy-start.6 = (bf16[26,1,40,8,256]{4,2,1,3,0:T(8,128)(2,1)S(1)}, bf16[26,1,40,8,256]{4,2,1,3,0:T(8,128)(2,1)}, u32[]{:S(2)}) copy-start(bf16[26,1,40,8,256]{4,2,1,3,0:T(8,128)(2,1)} %get-tuple-element.115) | copy-start | bytes 12779524
  429.4 9.2 %copy-start.7 = (bf16[26,1,40,8,256]{4,2,1,3,0:T(8,128)(2,1)S(1)}, bf16[26,1,40,8,256]{4,2,1,3,0:T(8,128)(2,1)}, u32[]{:S(2)}) copy-start(bf16[26,1,40,8,256]{4,2,1,3,0:T(8,128)(2,1)} %get-tuple-element.118) | copy-start | bytes 12779524
  429.4 10.4 %copy-start.8 = (bf16[26,1,40,8,256]{4,2,1,3,0:T(8,128)(2,1)S(1)}, bf16[26,1,40,8,256]{4,2,1,3,0:T(8,128)(2,1)}, u32[]{:S(2)}) copy-start(bf16[26,1,40,8,256]{4,2,1,3,0:T(8,128)(2,1)} %get-tuple-element.119) | copy-start | bytes 12779524
Sparse Core Ops, SparseCore 0:
  70.6 52.4 all-gather.5
  124.7 61.2 all-gather.3
where the time goes:
time: 527 us; the launch traced here: 519 us
  waiting for transfers between devices  133 us (25%)
  local copies, waits for them, and re-layouts  127 us (24%)
  other arithmetic  116 us (22%)
  matrix products  83.3 us (16%)
  starting transfers between devices  29.8 us (6%)
  loops' own time  15.5 us (3%)
  between operations  13.9 us (3%)
    dot_general x9, matrix products, aggregate(): jnp.einsum('fkg,dkghw->fdhw', weight[disp_tap, row_tap], stacked[disp_tap...  71.9 us
    mul x26, other arithmetic, one_disp(): products = left_wide * shifted.astype(jnp.float32)  68.8 us
    all_gather x1, waiting for transfers between devices, shards(): lax.all_gather(extended, 'band', axis=1, tiled=True)  58.4 us
    dynamic_slice x26, local copies, waits for them, and re-layouts, one_disp(): shifted = lax.dynamic_slice_in_dim(right_all, D - clipped, col_count, 2)  55.9 us
    all_gather x1, waiting for transfers between devices, shards(): lax.all_gather(left_feat, 'band', axis=1, tiled=True)  44.9 us
    while x3, local copies, waits for them, and re-layouts, shards(): volume = lax.map(one_disp, jnp.arange(band_size + 2, dtype=jnp.int32))  23.4 us
    ppermute x5, starting transfers between devices, padded_2(): before = lax.ppermute(last, axis, up)  19.4 us
    dynamic_update_slice x26, other arithmetic, shards(): volume = lax.map(one_disp, jnp.arange(band_size + 2, dtype=jnp.int32))  18.1 us
  transfers between devices with their start and end apart: 13, of which 9 were waited for; matrix products, arithmetic and copies ran while one was open for 4% of the time, Pallas kernels for 0%

commit v1 on v0

v1 whole, which is shorter than its diff:
```python
import functools

import jax
import jax.numpy as jnp
from jax import lax
from jax.experimental import pallas as pl
from jax.experimental.pallas import tpu as pltpu
from jax.sharding import PartitionSpec as P

G, J, D, F, H, WL, BD, C, W = 40, 8, 192, 32, 8, 256, 24, 320, 4096
CH = J * H * G
REM = 144
ML, MR = 272, 288
LR, RR = 272, 296
NT = BD + 2
KT = 3 * 384

def build(dst, slot, src, m):
    for n in range(2):
        for e in range(3):
            dst[slot, :, (n * 3 + e) * 128:(n * 3 + e + 1) * 128] = src(n, e).astype(jnp.bfloat16)
    lane = lax.broadcasted_iota(jnp.int32, (m, 128), 1)
    pair = jnp.where(lane < 64, src(2, 0), pltpu.roll(src(2, 1), 64, 1))
    dst[slot, :, 768:896] = pair.astype(jnp.bfloat16)
    dst[slot, :, 896:960] = src(2, 2)[:, :64].astype(jnp.bfloat16)

def conv_kernel(m, s_ref, *refs):
    xin = refs[:8]
    wm1, wr1, wm2, wr2, out_ref, raw, xs, hs, ts, z, feat = refs[8:]
    k, base = s_ref[0], s_ref[1]
    for d in range(8):
        h = jnp.bitwise_xor(k, d)
        for n in range(2):
            raw[h, n, 0:m, :] = xin[d][n * m:n * m + m, :].astype(jnp.float32)
        rem = xin[d][2 * m:2 * m + REM, :].astype(jnp.float32)
        raw[h, 2, 0:REM, :] = rem
        raw[h, 2, m - REM:m, :] = pltpu.roll(rem, 64, 1)
    for slot in (0, 9):
        xs[slot] = jnp.zeros((m, 960), jnp.bfloat16)
        hs[slot] = jnp.zeros((m, 960), jnp.bfloat16)
        z[slot] = jnp.zeros((2, m, 128), jnp.float32)
    col = base + lax.broadcasted_iota(jnp.int32, (m, 128), 0)

    def rest(x, wr, h):
        y = jnp.dot(x[h + 1], wr[...], preferred_element_type=jnp.float32)
        z[h + 1, 0] = y[:, :128]
        z[h + 1, 1, :, 0:64] = y[:, 128:192]

    def conv(x, wm, h):
        y = jnp.dot(x[h], wm[0], preferred_element_type=jnp.float32)
        y += jnp.dot(x[h + 1], wm[1], preferred_element_type=jnp.float32)
        y += jnp.dot(x[h + 2], wm[2], preferred_element_type=jnp.float32)
        return y[:, :128], y[:, 128:], z[h, 0] + pltpu.roll(z[h + 1, 0], 64, 1) + z[h + 2, 1]

    def load(h, c):
        build(xs, h + 1, lambda n, e: raw[h, n, e:e + m, :], m)
        rest(xs, wr1, h)
        return c
    lax.fori_loop(0, H, load, 0)
    def first(h, c):
        ok = jnp.logical_and(col + 1 >= 0, col + 1 < W)
        for n, y in enumerate(conv(xs, wm1, h)):
            ts[n, 0:m, :] = jnp.where(ok, jnp.maximum(y, 0.0), 0.0)
        build(hs, h + 1, lambda n, e: ts[n, e:e + m, :], m)
        return c
    lax.fori_loop(0, H, first, 0)
    def rest2(h, c):
        rest(hs, wr2, h)
        return c
    lax.fori_loop(0, H, rest2, 0)
    def second(h, c):
        ok = jnp.logical_and(col + 2 >= 0, col + 2 < W)
        for n, y in enumerate(conv(hs, wm2, h)):
            y = jnp.where(ok, y + raw[h, n, 2:2 + m, :], 0.0)
            feat[h, n] = y.astype(jnp.bfloat16).astype(jnp.float32)
        return c
    lax.fori_loop(0, H, second, 0)

    lane = lax.broadcasted_iota(jnp.int32, (16, 128), 1)
    def place(i, c):
        row = pl.multiple_of(i * 16, 16)
        for q in range(20):
            got = None
            for j in range(J):
                for h in range(H):
                    t0 = j * H * G + h * G
                    lo, hi = max(t0, q * 128), min(t0 + G, q * 128 + 128)
                    if lo >= hi:
                        continue
                    s_lo = lo - t0 + j * G
                    while lo < hi:
                        n = s_lo // 128
                        length = min(hi - lo, (n + 1) * 128 - s_lo)
                        x = feat[h, n, pl.ds(row, 16), :]
                        sh = (lo - s_lo) % 128
                        if sh:
                            x = pltpu.roll(x, sh, 1)
                        got = x if got is None else jnp.where(lane >= lo - q * 128, x, got)
                        lo, s_lo = lo + length, s_lo + length
            out_ref[pl.ds(row, 16), q * 128:q * 128 + 128] = got.astype(jnp.bfloat16)
        return c
    lax.fori_loop(0, m // 16, place, 0)

def conv_call(m, scal, xs, weights):
    return pl.pallas_call(
        functools.partial(conv_kernel, m),
        out_shape=jax.ShapeDtypeStruct((m, CH), jnp.bfloat16),
        in_specs=[pl.BlockSpec(memory_space=pltpu.SMEM)] + [pl.BlockSpec(memory_space=pltpu.VMEM)] * 12,
        out_specs=pl.BlockSpec(memory_space=pltpu.VMEM),
        scratch_shapes=[pltpu.VMEM((8, 3, m + 8, 128), jnp.float32), pltpu.VMEM((10, m, 960), jnp.bfloat16),
                        pltpu.VMEM((10, m, 960), jnp.bfloat16), pltpu.VMEM((3, m + 8, 128), jnp.float32),
                        pltpu.VMEM((10, 2, m, 128), jnp.float32), pltpu.VMEM((8, 3, m, 128), jnp.float32)],
        compiler_params=pltpu.CompilerParams(vmem_limit_bytes=56 * 2**20),
        name="feature_block",
    )(scal, *xs, *weights)

def group_major(x, axis):
    shape = x.shape
    x = x.reshape(shape[:axis] + (G, J) + shape[axis + 1:])
    return jnp.swapaxes(x, axis, axis + 1).reshape(shape)

def conv_weights(w):
    a = w.transpose(0, 1, 3, 2)
    main = a[:, :, :256].reshape(3, 3, 2, 128, C).transpose(0, 2, 1, 3, 4).reshape(3, 768, C)
    full = jnp.concatenate([main, a[:, :, 256:].reshape(3, 192, C)], axis=1)
    return full[:, :, :256], full[:, :, 256:].transpose(1, 0, 2).reshape(960, 192)

def pack(a):
    m = a.shape[0]
    return jnp.concatenate([a[:, :128], a[:, 128:256],
        jnp.concatenate([a[:REM, 256:], a[m - REM:, 256:]], axis=1)], axis=0)

def corr2(l_ref, r_ref, v_ref, p):
    def tile(i, c):
        row = pl.multiple_of(i * 8, 8)
        q = [[None] * 5 for _ in range(2)]
        for m in range(4):
            for n in range(5):
                lt = l_ref[m * 5 + n, pl.ds(row, 8), :]
                for u in range(2):
                    pr = lt * r_ref[m * 5 + n, pl.ds(row + (25 - u) - 2 * p, 8), :]
                    q[u][n] = pr if m == 0 else q[u][n] + pr
        for u in range(2):
            x = jnp.concatenate(q[u], axis=1)
            x = x + pltpu.roll(x, 320, 1)
            for n in range(3):
                v_ref[u, n, pl.ds(row, 8), :] = x[:, n * 128:n * 128 + 128]
        return c
    lax.fori_loop(0, 33, tile, 0, unroll=3)

def agg_kernel(k_ref, l_ref, r_ref, b_ref, out_ref, lf_ref, rf_ref, v_ref, vs_ref):
    k = k_ref[0]
    for n in range(20):
        lf_ref[n] = l_ref[:, n * 128:n * 128 + 128].astype(jnp.float32)
        rf_ref[n, 0:MR, :] = r_ref[:, n * 128:n * 128 + 128].astype(jnp.float32)
    def pair(p, c):
        corr2(lf_ref, rf_ref, v_ref, p)
        for u in range(2):
            t = 2 * p + u
            d = 24 * k - 1 + t
            ok = jnp.logical_and(d >= 0, d < D)
            m = jnp.where(ok, 1.0, 0.0).astype(jnp.float32)
            for e in range(3):
                for n in range(3):
                    vs_ref[t, :, e * 384 + n * 128:e * 384 + n * 128 + 128] = (v_ref[u, n, e:e + WL, :] * m).astype(jnp.bfloat16)
        return c
    lax.fori_loop(0, NT // 2, pair, 0)
    def out(d, c):
        y = jnp.dot(vs_ref[d], b_ref[0], preferred_element_type=jnp.float32)
        y += jnp.dot(vs_ref[d + 1], b_ref[1], preferred_element_type=jnp.float32)
        y += jnp.dot(vs_ref[d + 2], b_ref[2], preferred_element_type=jnp.float32)
        y = jnp.maximum(y, 0.0).T.reshape(F, H, WL)
        out_ref[:, d] = y.astype(jnp.bfloat16)
        return c
    lax.fori_loop(0, BD, out, 0)

def agg_rhs(w):
    w = w * jnp.asarray(0.125, w.dtype)
    z = jnp.zeros((3, F, 3, G), w.dtype)
    cols = []
    for hi in range(H):
        rows = [w[:, hi + 1 - ho] if 0 <= hi + 1 - ho <= 2 else z for ho in range(H)]
        cols.append(jnp.stack(rows, axis=2))
    full = jnp.stack(cols, axis=4)
    full = full.transpose(0, 3, 4, 5, 1, 2).reshape(3, 3, H * G, F * H)
    full = jnp.pad(full, ((0, 0), (0, 0), (0, 64), (0, 0)))
    return full.reshape(3, KT, F * H)

def agg_call(k, lx, rx, b):
    return pl.pallas_call(
        agg_kernel,
        out_shape=jax.ShapeDtypeStruct((F, BD, H, WL), jnp.bfloat16),
        in_specs=[pl.BlockSpec(memory_space=pltpu.SMEM)] + [pl.BlockSpec(memory_space=pltpu.VMEM)] * 3,
        out_specs=pl.BlockSpec(memory_space=pltpu.VMEM),
        scratch_shapes=[pltpu.VMEM((20, LR, 128), jnp.float32), pltpu.VMEM((20, RR, 128), jnp.float32),
                        pltpu.VMEM((2, 3, LR, 128), jnp.float32), pltpu.VMEM((NT, WL, KT), jnp.bfloat16)],
        compiler_params=pltpu.CompilerParams(vmem_limit_bytes=56 * 2**20),
        name="correlate_aggregate",
    )(k, lx, rx, b)


def from_col(x, by):
    n = lax.axis_size("col")
    return lax.ppermute(x, "col", [(i, i + by) for i in range(n) if 0 <= i + by < n])


def to_band(x, d):
    return lax.ppermute(x, "band", [(i, i ^ d) for i in range(lax.axis_size("band"))])


def shards(left_view, right_view, first_weight, second_weight, agg_weight):
    k = lax.axis_index("band")
    c = lax.axis_index("col")
    left = group_major(left_view[:, 0], 0).T
    right = group_major(right_view[:, 0], 0).T
    before = from_col(jnp.concatenate([left[WL - 16:], right[WL - 208:]], axis=0), 1)
    after = from_col(jnp.concatenate([left[:16], right[:16]], axis=0), -1)
    left = jnp.concatenate([before[13:16], left, after[:13]], axis=0)
    right = jnp.concatenate([before[16:], right, after[16:]], axis=0)
    packed = pack(left)
    lefts = [packed] + [to_band(packed, d) for d in range(1, 8)]

    def window(d):
        start = 181 - BD * jnp.bitwise_xor(k, d)
        return pack(lax.dynamic_slice_in_dim(right, start, MR, 0))

    rights = [window(0)] + [to_band(window(d), d) for d in range(1, 8)]
    weights = (*conv_weights(group_major(first_weight, 3)), *conv_weights(group_major(second_weight, 2)))
    base = c * WL
    lf = conv_call(ML, jnp.stack([k, base - 3]).astype(jnp.int32), lefts, weights)
    rf = conv_call(MR, jnp.stack([k, base - BD * k - 27]).astype(jnp.int32), rights, weights)
    return agg_call(k[None].astype(jnp.int32), lf, rf, agg_rhs(agg_weight))


def solution(mesh):
    return jax.shard_map(
        shards,
        mesh=mesh,
        in_specs=(P(None, "band", "col"), P(None, "band", "col"), P(), P(), P()),
        out_specs=P(None, "band", None, "col"),
        check_vma=False,
    )
```

time: 527 us -> 208 us (0.39); the launches traced: 519 us -> 206 us
  waiting for transfers between devices: 133 us -> 13.8 us
  other arithmetic: 116 us -> 10.2 us
  Pallas kernels: 0 us -> 88.4 us
  matrix products: 83.3 us -> 0 us
  local copies, waits for them, and re-layouts: 127 us -> 64.5 us
  loops' own time: 15.5 us -> 0 us
  between operations: 13.9 us -> 0.52 us
    all_gather x2 -> x0, waiting for transfers between devices: 103 us -> none  [the longest x1 58.4 us: shards(): lax.all_gather(extended, 'band', axis=1, tiled=True)]
    pallas_call x0 -> x3, Pallas kernels: none -> 88.4 us  [the longest x2 46.4 us: conv_call(): pl.pallas_call(functools.partial(conv_kernel, m), out_shape=jax.ShapeDtyp...]
    dot_general x27 -> x0, matrix products: 83.3 us -> none  [the longest x9 71.9 us: aggregate(): jnp.einsum('fkg,dkghw->fdhw', weight[disp_tap, row_tap], stacked[disp_tap...]
    dynamic_slice x52 -> x0, local copies, waits for them, and re-layouts: 71.1 us -> none  [the longest x26 55.9 us: one_disp(): shifted = lax.dynamic_slice_in_dim(right_all, D - clipped, col_count, 2)]
    mul x26 -> x1, other arithmetic: 68.8 us -> 0.02 us  [agg_rhs(): w = w * jnp.asarray(0.125, w.dtype)]
    while x3 -> x0, local copies, waits for them, and re-layouts: 23.4 us -> none  [shards(): volume = lax.map(one_disp, jnp.arange(band_size + 2, dtype=jnp.int32))]
    dynamic_update_slice x26 -> x0, other arithmetic: 18.1 us -> none  [shards(): volume = lax.map(one_disp, jnp.arange(band_size + 2, dtype=jnp.int32))]
    reshape x0 -> x8, local copies, waits for them, and re-layouts: none -> 17.1 us  [the longest x3 8.54 us: conv_weights(): a[:, :, :256].reshape(3, 3, 2, 128, C).transpose(0, 2, 1, 3, 4)]
  transfers between devices with their start and end apart: 13 -> 16, of which waited for: 9 -> 4; matrix products, arithmetic and copies ran while one was open for 4% -> 34% of each run, Pallas kernels for 0% -> 11%
where the time goes in v1:
time: 208 us; the launch traced here: 206 us
  Pallas kernels  88.4 us (42%)
  local copies, waits for them, and re-layouts  64.5 us (31%)
  starting transfers between devices  28.9 us (14%)
  waiting for transfers between devices  13.8 us (7%)
  other arithmetic  10.2 us (5%)
    pallas_call x2, Pallas kernels, conv_call(): pl.pallas_call(functools.partial(conv_kernel, m), out_shape=jax.ShapeDtyp...  46.4 us
    pallas_call x1, Pallas kernels, agg_call(): pl.pallas_call(agg_kernel, out_shape=jax.ShapeDtypeStruct((F, BD, H, WL),...  42.1 us
    ppermute x14, starting transfers between devices, to_band(): lax.ppermute(x, 'band', [(i, i ^ d) for i in range(lax.axis_size('band'))])  24.6 us
    another operation x10, local copies, waits for them, and re-layouts, agg_rhs(): cols.append(jnp.stack(rows, axis=2))  16.5 us
    ppermute x14, waiting for transfers between devices, to_band(): lax.ppermute(x, 'band', [(i, i ^ d) for i in range(lax.axis_size('band'))])  13.8 us
    unnamed x66, local copies, waits for them, and re-layouts  10.5 us
    reshape x3, local copies, waits for them, and re-layouts, conv_weights(): a[:, :, :256].reshape(3, 3, 2, 128, C).transpose(0, 2, 1, 3, 4)  8.54 us
    reshape x1, local copies, waits for them, and re-layouts, agg_rhs(): full = full.transpose(0, 3, 4, 5, 1, 2).reshape(3, 3, H * G, F * H)  6.25 us
  transfers between devices with their start and end apart: 16, of which 4 were waited for; matrix products, arithmetic and copies ran while one was open for 34% of the time, Pallas kernels for 11%

profile of v1, /device:TPU:20, one launch (start us, length us, event | category | flops | bytes accessed | tf_op | source)
XLA Modules:
  0.0 206.4 jit_solution(7393707372373364143)
XLA Ops:
  0.0 0.9 copy.127
  1.1 1.0 copy.125
  2.4 1.9 collective-permute-start.1
  4.3 0.7 pad_maximum_fusion.8
  5.0 2.4 %collective-permute-start = (bf16[224,320]{1,0:T(8,128)(2,1)}, bf16[224,320]{1,0:T(8,128)(2,1)}, u32[]{:S(2)}, u32[]{:S(2)}) collective-permute-start(bf16[224,320]{1,0:T(8,128)(2,1)} %pad_maximum_fusion.8), channel_id=1, source_target_pairs={{0,8},{8,16},{16,24},{24,32},{32,40},{40,48},{48,56},{56,64},{64,7... | collective-permute-start | bytes 430088 | tf_op jit(solution)/shard_map/ppermute | solution.py:204
  7.4 2.0 copy.133
  9.4 1.3 slice.251
  10.7 1.0 slice.252
  11.7 3.0 %copy.129 = bf16[3,3,320,320]{2,3,1,0:T(8,128)(2,1)S(1)} copy(bf16[3,3,320,320]{3,2,1,0:T(8,128)(2,1)} %param.7) | data formatting | bytes 3686400 | tf_op args[2]
  14.7 0.4 copy.130
  15.1 1.4 slice.247
  17.1 2.7 %stack.71 = bf16[3,32,8,3,40]{4,2,3,1,0:T(8,128)(2,1)} concatenate(bf16[3,32,1,3,40]{4,2,3,1,0:T(2,128)(2,1)S(1)} %copy.143, bf16[3,32,1,3,40]{4,2,3,1,0:T(2,128)(2,1)S(1)} %copy.141, bf16[3,32,1,3,40]{4,2,3,1,0:T(2,128)(2,1)S(1)} %copy.142, bf16[3,32,1,3,40]{4,2,3,1,0:T(2,128)(2,1)S(1)} %broadcast.13, bf16[3,32,4,3,40]{4,2,3,1,0:T(4,128)(2,1)S(1)} %broadcast.12), dimensions={2} | concatenate | bytes 368640 | tf_op jit(solution)/shard_map/stack | solution.py:183
  19.8 2.6 %stack.73 = bf16[3,32,8,3,40]{4,2,3,1,0:T(8,128)(2,1)} concatenate(bf16[3,32,1,3,40]{4,2,3,1,0:T(2,128)(2,1)S(1)} %broadcast.13, bf16[3,32,1,3,40]{4,2,3,1,0:T(2,128)(2,1)S(1)} %copy.143, bf16[3,32,1,3,40]{4,2,3,1,0:T(2,128)(2,1)S(1)} %copy.141, bf16[3,32,1,3,40]{4,2,3,1,0:T(2,128)(2,1)S(1)} %copy.142, bf16[3,32,4,3,40]{4,2,3,1,0:T(4,128)(2,1)S(1)} %broadcast.12), dimensions={2} | concatenate | bytes 368640 | tf_op jit(solution)/shard_map/stack | solution.py:183
  22.5 1.7 fusion.4
  24.2 2.8 %stack.75 = bf16[3,32,8,3,40]{4,2,3,1,0:T(8,128)(2,1)} concatenate(bf16[3,32,2,3,40]{4,2,3,1,0:T(2,128)(2,1)S(1)} %broadcast.11, bf16[3,32,1,3,40]{4,2,3,1,0:T(2,128)(2,1)S(1)} %copy.143, bf16[3,32,1,3,40]{4,2,3,1,0:T(2,128)(2,1)S(1)} %copy.141, bf16[3,32,1,3,40]{4,2,3,1,0:T(2,128)(2,1)S(1)} %copy.142, bf16[3,32,1,3,40]{4,2,3,1,0:T(2,128)(2,1)S(1)} %broadcast.13, ...), dimensions={2} | concatenate | bytes 368640 | tf_op jit(solution)/shard_map/stack | solution.py:183
  27.0 2.8 %stack.77 = bf16[3,32,8,3,40]{4,2,3,1,0:T(8,128)(2,1)} concatenate(bf16[3,32,1,3,40]{4,2,3,1,0:T(2,128)(2,1)S(1)} %broadcast.13, bf16[3,32,2,3,40]{4,2,3,1,0:T(2,128)(2,1)S(1)} %broadcast.11, bf16[3,32,1,3,40]{4,2,3,1,0:T(2,128)(2,1)S(1)} %copy.143, bf16[3,32,1,3,40]{4,2,3,1,0:T(2,128)(2,1)S(1)} %copy.141, bf16[3,32,1,3,40]{4,2,3,1,0:T(2,128)(2,1)S(1)} %copy.142, ...), dimensions={2} | concatenate | bytes 368640 | tf_op jit(solution)/shard_map/stack | solution.py:183
  29.8 2.6 %stack.79 = bf16[3,32,8,3,40]{4,2,3,1,0:T(8,128)(2,1)} concatenate(bf16[3,32,4,3,40]{4,2,3,1,0:T(4,128)(2,1)S(1)} %broadcast.12, bf16[3,32,1,3,40]{4,2,3,1,0:T(2,128)(2,1)S(1)} %copy.143, bf16[3,32,1,3,40]{4,2,3,1,0:T(2,128)(2,1)S(1)} %copy.141, bf16[3,32,1,3,40]{4,2,3,1,0:T(2,128)(2,1)S(1)} %copy.142, bf16[3,32,1,3,40]{4,2,3,1,0:T(2,128)(2,1)S(1)} %broadcast.13), dimensions={2} | concatenate | bytes 368640 | tf_op jit(solution)/shard_map/stack | solution.py:183
  32.5 2.6 %stack.81 = bf16[3,32,8,3,40]{4,2,3,1,0:T(8,128)(2,1)} concatenate(bf16[3,32,1,3,40]{4,2,3,1,0:T(2,128)(2,1)S(1)} %broadcast.13, bf16[3,32,4,3,40]{4,2,3,1,0:T(4,128)(2,1)S(1)} %broadcast.12, bf16[3,32,1,3,40]{4,2,3,1,0:T(2,128)(2,1)S(1)} %copy.143, bf16[3,32,1,3,40]{4,2,3,1,0:T(2,128)(2,1)S(1)} %copy.141, bf16[3,32,1,3,40]{4,2,3,1,0:T(2,128)(2,1)S(1)} %copy.142), dimensions={2} | concatenate | bytes 368640 | tf_op jit(solution)/shard_map/stack | solution.py:183
  35.1 1.3 reshape.58
  36.4 5.5 %copy.134 = bf16[3,3,2,128,320]{4,3,1,2,0:T(8,128)(2,1)S(1)} copy(bf16[3,3,2,128,320]{3,2,4,1,0:T(2,128)(2,1)} %reshape.58) | data formatting | bytes 2949120 | tf_op jit(solution)/shard_map/reshape | solution.py:124
  42.0 1.4 copy.135
  43.4 1.7 copy.131
  45.1 1.1 fusion.3
  46.2 1.9 fusion
  48.1 0.9 bitcast_dynamic-update-slice_fusion.4
  49.0 1.0 bitcast_dynamic-update-slice_fusion.3
  50.0 0.9 bitcast_dynamic-update-slice_fusion.2
  50.9 1.0 bitcast_dynamic-update-slice_fusion.1
  51.9 0.9 bitcast_dynamic-update-slice_fusion
  52.8 0.9 bitcast_dynamic-update-slice_fusion.5
  53.7 1.0 fusion.2
  54.8 1.7 fusion.5
  56.7 1.0 copy.137.refs_9_
  57.7 0.3 copy.136
  58.0 1.0 copy.138.refs_11_
  59.0 6.2 %copy.169 = bf16[3,3,8,40,32,8]{3,2,5,4,1,0:T(8,128)(2,1)} copy(bf16[3,3,8,40,32,8]{3,5,2,1,4,0:T(8,128)(2,1)} %bitcast.99) | data formatting | bytes 2949120 | tf_op jit(solution)/shard_map/transpose | solution.py:185
  65.2 6.3 %reshape.62 = bf16[3,3,320,256]{2,3,1,0:T(8,128)(2,1)S(1)} reshape(bf16[3,3,8,40,32,8]{3,2,5,4,1,0:T(8,128)(2,1)} %copy.169) | data formatting | bytes 2949120 | tf_op jit(solution)/shard_map/reshape | solution.py:185
  71.4 0.9 copy.171
  72.4 1.4 pad.4.clone
  73.8 0.7 slice.243
  74.6 1.4 collective-permute-start.2
  76.0 1.9 collective-permute-start.3
  77.9 0.3 collective-permute-start.4
  78.2 3.9 %collective-permute-start.5 = (bf16[688,128]{1,0:T(8,128)(2,1)S(1)}, bf16[688,128]{1,0:T(8,128)(2,1)S(1)}, u32[]{:S(2)}, u32[]{:S(2)}) collective-permute-start(bf16[688,128]{1,0:T(8,128)(2,1)S(1)} %fusion.13.refs_0_), channel_id=1, source_target_pairs={{0,4},{1,5},{2,6},{3,7},{4,0},{5,1},{6,2},{7,3},{8,12},{9,13},{10,... | collective-permute-start | bytes 528392 | tf_op jit(solution)/shard_map/ppermute | solution.py:208
  82.0 0.7 collective-permute-start.6
  82.8 0.9 slice.255
  83.8 0.4 constant_dynamic-slice_fusion.1
  84.2 0.4 fusion.15
  85.1 3.8 %collective-permute-start.7 = (bf16[688,128]{1,0:T(8,128)(2,1)S(1)}, bf16[688,128]{1,0:T(8,128)(2,1)S(1)}, u32[]{:S(2)}, u32[]{:S(2)}) collective-permute-start(bf16[688,128]{1,0:T(8,128)(2,1)S(1)} %fusion.13.refs_0_), channel_id=1, source_target_pairs={{0,6},{1,7},{2,4},{3,5},{4,2},{5,3},{6,0},{7,1},{8,14},{9,15},{10,... | collective-permute-start | bytes 528392 | tf_op jit(solution)/shard_map/ppermute | solution.py:208
  88.9 1.4 collective-permute-done.3.refs_2_
  90.3 4.8 %collective-permute-start.8 = (bf16[688,128]{1,0:T(8,128)(2,1)S(1)}, bf16[688,128]{1,0:T(8,128)(2,1)S(1)}, u32[]{:S(2)}, u32[]{:S(2)}) collective-permute-start(bf16[688,128]{1,0:T(8,128)(2,1)S(1)} %fusion.13.refs_0_), channel_id=1, source_target_pairs={{0,7},{1,6},{2,5},{3,4},{4,3},{5,2},{6,1},{7,0},{8,15},{9,14},{10,... | collective-permute-start | bytes 528392 | tf_op jit(solution)/shard_map/ppermute | solution.py:208
  95.1 1.3 collective-permute-start.9
  96.3 3.9 %collective-permute-done.5.refs_4_ = bf16[688,128]{1,0:T(8,128)(2,1)S(1)} collective-permute-done((bf16[688,128]{1,0:T(8,128)(2,1)S(1)}, bf16[688,128]{1,0:T(8,128)(2,1)S(1)}, u32[]{:S(2)}, u32[]{:S(2)}) %collective-permute-start.5) | collective-permute-done | bytes 176160 | tf_op jit(solution)/shard_map/ppermute | solution.py:208
  100.4 1.7 collective-permute-start.11
  102.2 2.1 %collective-permute-done.7.refs_6_ = bf16[688,128]{1,0:T(8,128)(2,1)S(1)} collective-permute-done((bf16[688,128]{1,0:T(8,128)(2,1)S(1)}, bf16[688,128]{1,0:T(8,128)(2,1)S(1)}, u32[]{:S(2)}, u32[]{:S(2)}) %collective-permute-start.7) | collective-permute-done | bytes 176160 | tf_op jit(solution)/shard_map/ppermute | solution.py:208
  104.3 3.9 %collective-permute-start.13 = (bf16[720,128]{1,0:T(8,128)(2,1)S(1)}, bf16[720,128]{1,0:T(8,128)(2,1)S(1)}, u32[]{:S(2)}, u32[]{:S(2)}) collective-permute-start(bf16[720,128]{1,0:T(8,128)(2,1)S(1)} %maximum_maximum_fusion.5), channel_id=1, source_target_pairs={{0,5},{1,4},{2,7},{3,6},{4,1},{5,0},{6,3},{7,2},{8,13},{9,12},{10,... | collective-permute-start | bytes 552968 | tf_op jit(solution)/shard_map/ppermute | solution.py:208
  108.2 1.0 collective-permute-start.14
  109.2 6.4 %collective-permute-done.10.refs_2_ = bf16[720,128]{1,0:T(8,128)(2,1)S(1)} collective-permute-done((bf16[720,128]{1,0:T(8,128)(2,1)S(1)}, bf16[720,128]{1,0:T(8,128)(2,1)S(1)}, u32[]{:S(2)}, u32[]{:S(2)}) %collective-permute-start.10) | collective-permute-done | bytes 184352 | tf_op jit(solution)/shard_map/ppermute | solution.py:208
  115.6 0.6 pad_add_fusion
  116.2 0.8 maximum_maximum_fusion.refs_0_
  117.0 22.8 %feature_block.2.l_ref = bf16[272,2560]{1,0:T(8,128)(2,1)} custom-call(s32[2]{0:T(128)} %get-tuple-element.42.s_ref, bf16[688,128]{1,0:T(8,128)(2,1)} %copy-done.13, bf16[688,128]{1,0:T(8,128)(2,1)} %copy-done.22, bf16[688,128]{1,0:T(8,128)(2,1)} %copy-done.23, bf16[688,128]{1,0:T(8,128)(2,1)} %copy-done.24, bf16[688,128]{1,0:T(8,128)(2,1)} %copy-done.25, ...), custom_call_target="tpu_custom_call" | custom-call | tf_op jit(solution)/shard_map/feature_block/pallas_call | solution.py:105
  139.9 0.6 copy-done.17
  140.8 23.5 %feature_block.3.r_ref = bf16[288,2560]{1,0:T(8,128)(2,1)} custom-call(s32[2]{0:T(128)} %get-tuple-element.43.s_ref, bf16[720,128]{1,0:T(8,128)(2,1)} %maximum_maximum_fusion.refs_0_, bf16[720,128]{1,0:T(8,128)(2,1)} %copy-done.15, bf16[720,128]{1,0:T(8,128)(2,1)} %copy-done.16, bf16[720,128]{1,0:T(8,128)(2,1)} %copy-done.17, bf16[720,128]{1,0:T(8,128)(2,1)} %copy-done.18, ...), custom_call_target="tpu_custom_call" | custom-call | tf_op jit(solution)/shard_map/feature_block/pallas_call | solution.py:105
  164.3 42.1 %correlate_aggregate.1 = bf16[32,24,8,256]{3,2,1,0:T(8,128)(2,1)} custom-call(s32[1]{0:T(128)} %bitcast.k_ref, bf16[272,2560]{1,0:T(8,128)(2,1)} %feature_block.2.l_ref, bf16[288,2560]{1,0:T(8,128)(2,1)} %feature_block.3.r_ref, bf16[3,1152,256]{2,1,0:T(8,128)(2,1)} %bitcast.98), custom_call_target="tpu_custom_call" | custom-call | tf_op jit(solution)/shard_map/correlate_aggregate/pallas_call | solution.py:190
  (99 shorter events, 2.4 us)
Async XLA Ops:
  1.1 8.3 %copy-start.9 = (bf16[320,256]{0,1:T(8,128)(2,1)}, bf16[320,256]{0,1:T(8,128)(2,1)S(1)}, u32[]{:S(2)}) copy-start(bf16[320,256]{0,1:T(8,128)(2,1)S(1)} %copy.128) | copy-start | bytes 491524
  2.3 7.1 %copy-start.11 = (bf16[320,256]{0,1:T(8,128)(2,1)}, bf16[320,256]{0,1:T(8,128)(2,1)S(1)}, u32[]{:S(2)}) copy-start(bf16[320,256]{0,1:T(8,128)(2,1)S(1)} %copy.126) | copy-start | bytes 491524
  2.4 71.4 %collective-permute-start.1 = (bf16[32,320]{1,0:T(8,128)(2,1)S(1)}, bf16[32,320]{1,0:T(8,128)(2,1)S(1)}, u32[]{:S(2)}, u32[]{:S(2)}) collective-permute-start(bf16[32,320]{1,0:T(8,128)(2,1)S(1)} %pad_maximum_fusion.9), channel_id=1, source_target_pairs={{8,0},{16,8},{24,16},{32,24},{40,32},{48,40},{56,48},{64,56},{72,6... | collective-permute-start | bytes 61448 | tf_op jit(solution)/shard_map/ppermute | solution.py:204
  5.0 68.8 %collective-permute-start = (bf16[224,320]{1,0:T(8,128)(2,1)}, bf16[224,320]{1,0:T(8,128)(2,1)}, u32[]{:S(2)}, u32[]{:S(2)}) collective-permute-start(bf16[224,320]{1,0:T(8,128)(2,1)} %pad_maximum_fusion.8), channel_id=1, source_target_pairs={{0,8},{8,16},{16,24},{24,32},{32,40},{40,48},{48,56},{56,64},{64,7... | collective-permute-start | bytes 430088 | tf_op jit(solution)/shard_map/ppermute | solution.py:204
  15.1 1.4 copy-start.14
  29.8 5.3 %copy-start = (bf16[3,3,256,320]{2,3,1,0:T(8,128)(2,1)S(1)}, bf16[3,3,256,320]{2,3,1,0:T(8,128)(2,1)}, u32[]{:S(2)}) copy-start(bf16[3,3,256,320]{2,3,1,0:T(8,128)(2,1)} %slice.251) | copy-start | bytes 4423684
  46.2 1.9 copy-start.8
  46.2 2.9 %copy-start.6 = (bf16[3,32,8,3,40]{4,2,3,1,0:T(8,128)(2,1)S(1)}, bf16[3,32,8,3,40]{4,2,3,1,0:T(8,128)(2,1)}, u32[]{:S(2)}) copy-start(bf16[3,32,8,3,40]{4,2,3,1,0:T(8,128)(2,1)} %stack.73) | copy-start | bytes 552964
  48.1 1.9 copy-start.7
  48.1 2.8 %copy-start.5 = (bf16[3,32,8,3,40]{4,2,3,1,0:T(8,128)(2,1)S(1)}, bf16[3,32,8,3,40]{4,2,3,1,0:T(8,128)(2,1)}, u32[]{:S(2)}) copy-start(bf16[3,32,8,3,40]{4,2,3,1,0:T(8,128)(2,1)} %stack.77) | copy-start | bytes 552964
  49.0 2.9 %copy-start.4 = (bf16[3,32,8,3,40]{4,2,3,1,0:T(8,128)(2,1)S(1)}, bf16[3,32,8,3,40]{4,2,3,1,0:T(8,128)(2,1)}, u32[]{:S(2)}) copy-start(bf16[3,32,8,3,40]{4,2,3,1,0:T(8,128)(2,1)} %stack.79) | copy-start | bytes 552964
  50.0 2.8 %copy-start.3 = (bf16[3,32,8,3,40]{4,2,3,1,0:T(8,128)(2,1)S(1)}, bf16[3,32,8,3,40]{4,2,3,1,0:T(8,128)(2,1)}, u32[]{:S(2)}) copy-start(bf16[3,32,8,3,40]{4,2,3,1,0:T(8,128)(2,1)} %stack.81) | copy-start | bytes 552964
  54.8 1.7 copy-start.1
  54.8 2.9 %copy-start.2 = (bf16[960,3,64]{2,0,1:T(8,128)(2,1)S(1)}, bf16[960,3,64]{2,0,1:T(8,128)(2,1)}, u32[]{:S(2)}) copy-start(bf16[960,3,64]{2,0,1:T(8,128)(2,1)} %fusion.2) | copy-start | bytes 1105924
  72.3 2.1 %copy-start.12 = (bf16[320,256]{0,1:T(8,128)(2,1)S(1)}, bf16[320,256]{0,1:T(8,128)(2,1)}, u32[]{:S(2)}) copy-start(bf16[320,256]{0,1:T(8,128)(2,1)} %copy-done.11) | copy-start | bytes 491524
  72.4 11.3 %copy-start.10 = (bf16[320,256]{0,1:T(8,128)(2,1)S(1)}, bf16[320,256]{0,1:T(8,128)(2,1)}, u32[]{:S(2)}) copy-start(bf16[320,256]{0,1:T(8,128)(2,1)} %copy-done.9) | copy-start | bytes 491524
  74.6 15.7 %copy-start.13 = (bf16[688,128]{1,0:T(8,128)(2,1)}, bf16[688,128]{1,0:T(8,128)(2,1)S(1)}, u32[]{:S(2)}) copy-start(bf16[688,128]{1,0:T(8,128)(2,1)S(1)} %fusion.13.refs_0_) | copy-start | bytes 528388
  74.6 10.5 %collective-permute-start.2 = (bf16[688,128]{1,0:T(8,128)(2,1)S(1)}, bf16[688,128]{1,0:T(8,128)(2,1)S(1)}, u32[]{:S(2)}, u32[]{:S(2)}) collective-permute-start(bf16[688,128]{1,0:T(8,128)(2,1)S(1)} %fusion.13.refs_0_), channel_id=1, source_target_pairs={{0,1},{1,0},{2,3},{3,2},{4,5},{5,4},{6,7},{7,6},{8,9},{9,8},{10,11... | collective-permute-start | bytes 528392 | tf_op jit(solution)/shard_map/ppermute | solution.py:208
  76.0 14.3 %collective-permute-start.3 = (bf16[688,128]{1,0:T(8,128)(2,1)S(1)}, bf16[688,128]{1,0:T(8,128)(2,1)S(1)}, u32[]{:S(2)}, u32[]{:S(2)}) collective-permute-start(bf16[688,128]{1,0:T(8,128)(2,1)S(1)} %fusion.13.refs_0_), channel_id=1, source_target_pairs={{0,2},{1,3},{2,0},{3,1},{4,6},{5,7},{6,4},{7,5},{8,10},{9,11},{10,... | collective-permute-start | bytes 528392 | tf_op jit(solution)/shard_map/ppermute | solution.py:208
  77.9 17.2 %collective-permute-start.4 = (bf16[688,128]{1,0:T(8,128)(2,1)S(1)}, bf16[688,128]{1,0:T(8,128)(2,1)S(1)}, u32[]{:S(2)}, u32[]{:S(2)}) collective-permute-start(bf16[688,128]{1,0:T(8,128)(2,1)S(1)} %fusion.13.refs_0_), channel_id=1, source_target_pairs={{0,3},{1,2},{2,1},{3,0},{4,7},{5,6},{6,5},{7,4},{8,11},{9,10},{10,... | collective-permute-start | bytes 528392 | tf_op jit(solution)/shard_map/ppermute | solution.py:208
  78.2 22.0 %collective-permute-start.5 = (bf16[688,128]{1,0:T(8,128)(2,1)S(1)}, bf16[688,128]{1,0:T(8,128)(2,1)S(1)}, u32[]{:S(2)}, u32[]{:S(2)}) collective-permute-start(bf16[688,128]{1,0:T(8,128)(2,1)S(1)} %fusion.13.refs_0_), channel_id=1, source_target_pairs={{0,4},{1,5},{2,6},{3,7},{4,0},{5,1},{6,2},{7,3},{8,12},{9,13},{10,... | collective-permute-start | bytes 528392 | tf_op jit(solution)/shard_map/ppermute | solution.py:208
  82.0 18.4 %collective-permute-start.6 = (bf16[688,128]{1,0:T(8,128)(2,1)S(1)}, bf16[688,128]{1,0:T(8,128)(2,1)S(1)}, u32[]{:S(2)}, u32[]{:S(2)}) collective-permute-start(bf16[688,128]{1,0:T(8,128)(2,1)S(1)} %fusion.13.refs_0_), channel_id=1, source_target_pairs={{0,5},{1,4},{2,7},{3,6},{4,1},{5,0},{6,3},{7,2},{8,13},{9,12},{10,... | collective-permute-start | bytes 528392 | tf_op jit(solution)/shard_map/ppermute | solution.py:208
  85.1 31.9 %copy-start.22 = (bf16[688,128]{1,0:T(8,128)(2,1)}, bf16[688,128]{1,0:T(8,128)(2,1)S(1)}, u32[]{:S(2)}) copy-start(bf16[688,128]{1,0:T(8,128)(2,1)S(1)} %collective-permute-done.2.refs_1_) | copy-start | bytes 528388
  85.1 19.2 %collective-permute-start.7 = (bf16[688,128]{1,0:T(8,128)(2,1)S(1)}, bf16[688,128]{1,0:T(8,128)(2,1)S(1)}, u32[]{:S(2)}, u32[]{:S(2)}) collective-permute-start(bf16[688,128]{1,0:T(8,128)(2,1)S(1)} %fusion.13.refs_0_), channel_id=1, source_target_pairs={{0,6},{1,7},{2,4},{3,5},{4,2},{5,3},{6,0},{7,1},{8,14},{9,15},{10,... | collective-permute-start | bytes 528392 | tf_op jit(solution)/shard_map/ppermute | solution.py:208
  90.3 26.7 %copy-start.23 = (bf16[688,128]{1,0:T(8,128)(2,1)}, bf16[688,128]{1,0:T(8,128)(2,1)S(1)}, u32[]{:S(2)}) copy-start(bf16[688,128]{1,0:T(8,128)(2,1)S(1)} %collective-permute-done.3.refs_2_) | copy-start | bytes 528388
  90.3 14.0 %collective-permute-start.8 = (bf16[688,128]{1,0:T(8,128)(2,1)S(1)}, bf16[688,128]{1,0:T(8,128)(2,1)S(1)}, u32[]{:S(2)}, u32[]{:S(2)}) collective-permute-start(bf16[688,128]{1,0:T(8,128)(2,1)S(1)} %fusion.13.refs_0_), channel_id=1, source_target_pairs={{0,7},{1,6},{2,5},{3,4},{4,3},{5,2},{6,1},{7,0},{8,15},{9,14},{10,... | collective-permute-start | bytes 528392 | tf_op jit(solution)/shard_map/ppermute | solution.py:208
  95.1 21.9 %copy-start.24 = (bf16[688,128]{1,0:T(8,128)(2,1)}, bf16[688,128]{1,0:T(8,128)(2,1)S(1)}, u32[]{:S(2)}) copy-start(bf16[688,128]{1,0:T(8,128)(2,1)S(1)} %collective-permute-done.4.refs_3_) | copy-start | bytes 528388
  95.1 13.1 %collective-permute-start.9 = (bf16[720,128]{1,0:T(8,128)(2,1)S(1)}, bf16[720,128]{1,0:T(8,128)(2,1)S(1)}, u32[]{:S(2)}, u32[]{:S(2)}) collective-permute-start(bf16[720,128]{1,0:T(8,128)(2,1)S(1)} %maximum_maximum_fusion.1), channel_id=1, source_target_pairs={{0,1},{1,0},{2,3},{3,2},{4,5},{5,4},{6,7},{7,6},{8,9},{9,8},{10,11... | collective-permute-start | bytes 552968 | tf_op jit(solution)/shard_map/ppermute | solution.py:208
  100.2 16.8 %copy-start.25 = (bf16[688,128]{1,0:T(8,128)(2,1)}, bf16[688,128]{1,0:T(8,128)(2,1)S(1)}, u32[]{:S(2)}) copy-start(bf16[688,128]{1,0:T(8,128)(2,1)S(1)} %collective-permute-done.5.refs_4_) | copy-start | bytes 528388
  100.2 15.4 %collective-permute-start.10 = (bf16[720,128]{1,0:T(8,128)(2,1)S(1)}, bf16[720,128]{1,0:T(8,128)(2,1)S(1)}, u32[]{:S(2)}, u32[]{:S(2)}) collective-permute-start(bf16[720,128]{1,0:T(8,128)(2,1)S(1)} %maximum_maximum_fusion.2), channel_id=1, source_target_pairs={{0,2},{1,3},{2,0},{3,1},{4,6},{5,7},{6,4},{7,5},{8,10},{9,11},{10,... | collective-permute-start | bytes 552968 | tf_op jit(solution)/shard_map/ppermute | solution.py:208
  100.4 16.6 %copy-start.26 = (bf16[688,128]{1,0:T(8,128)(2,1)}, bf16[688,128]{1,0:T(8,128)(2,1)S(1)}, u32[]{:S(2)}) copy-start(bf16[688,128]{1,0:T(8,128)(2,1)S(1)} %collective-permute-done.6.refs_5_) | copy-start | bytes 528388
  100.4 39.4 %collective-permute-start.11 = (bf16[720,128]{1,0:T(8,128)(2,1)S(1)}, bf16[720,128]{1,0:T(8,128)(2,1)S(1)}, u32[]{:S(2)}, u32[]{:S(2)}) collective-permute-start(bf16[720,128]{1,0:T(8,128)(2,1)S(1)} %maximum_maximum_fusion.3), channel_id=1, source_target_pairs={{0,3},{1,2},{2,1},{3,0},{4,7},{5,6},{6,5},{7,4},{8,11},{9,10},{10,... | collective-permute-start | bytes 552968 | tf_op jit(solution)/shard_map/ppermute | solution.py:208
  104.3 12.7 %copy-start.27 = (bf16[688,128]{1,0:T(8,128)(2,1)}, bf16[688,128]{1,0:T(8,128)(2,1)S(1)}, u32[]{:S(2)}) copy-start(bf16[688,128]{1,0:T(8,128)(2,1)S(1)} %collective-permute-done.7.refs_6_) | copy-start | bytes 528388
  104.3 35.6 %collective-permute-start.12 = (bf16[720,128]{1,0:T(8,128)(2,1)S(1)}, bf16[720,128]{1,0:T(8,128)(2,1)S(1)}, u32[]{:S(2)}, u32[]{:S(2)}) collective-permute-start(bf16[720,128]{1,0:T(8,128)(2,1)S(1)} %maximum_maximum_fusion.4), channel_id=1, source_target_pairs={{0,4},{1,5},{2,6},{3,7},{4,0},{5,1},{6,2},{7,3},{8,12},{9,13},{10,... | collective-permute-start | bytes 552968 | tf_op jit(solution)/shard_map/ppermute | solution.py:208
  104.3 12.7 %copy-start.28 = (bf16[688,128]{1,0:T(8,128)(2,1)}, bf16[688,128]{1,0:T(8,128)(2,1)S(1)}, u32[]{:S(2)}) copy-start(bf16[688,128]{1,0:T(8,128)(2,1)S(1)} %collective-permute-done.8.refs_7_) | copy-start | bytes 528388
  104.3 35.6 %collective-permute-start.13 = (bf16[720,128]{1,0:T(8,128)(2,1)S(1)}, bf16[720,128]{1,0:T(8,128)(2,1)S(1)}, u32[]{:S(2)}, u32[]{:S(2)}) collective-permute-start(bf16[720,128]{1,0:T(8,128)(2,1)S(1)} %maximum_maximum_fusion.5), channel_id=1, source_target_pairs={{0,5},{1,4},{2,7},{3,6},{4,1},{5,0},{6,3},{7,2},{8,13},{9,12},{10,... | collective-permute-start | bytes 552968 | tf_op jit(solution)/shard_map/ppermute | solution.py:208
  108.2 31.6 %copy-start.15 = (bf16[720,128]{1,0:T(8,128)(2,1)}, bf16[720,128]{1,0:T(8,128)(2,1)S(1)}, u32[]{:S(2)}) copy-start(bf16[720,128]{1,0:T(8,128)(2,1)S(1)} %collective-permute-done.9.refs_1_) | copy-start | bytes 552964
  108.2 31.7 %collective-permute-start.14 = (bf16[720,128]{1,0:T(8,128)(2,1)S(1)}, bf16[720,128]{1,0:T(8,128)(2,1)S(1)}, u32[]{:S(2)}, u32[]{:S(2)}) collective-permute-start(bf16[720,128]{1,0:T(8,128)(2,1)S(1)} %maximum_maximum_fusion.6), channel_id=1, source_target_pairs={{0,6},{1,7},{2,4},{3,5},{4,2},{5,3},{6,0},{7,1},{8,14},{9,15},{10,... | collective-permute-start | bytes 552968 | tf_op jit(solution)/shard_map/ppermute | solution.py:208
  115.6 24.3 %copy-start.16 = (bf16[720,128]{1,0:T(8,128)(2,1)}, bf16[720,128]{1,0:T(8,128)(2,1)S(1)}, u32[]{:S(2)}) copy-start(bf16[720,128]{1,0:T(8,128)(2,1)S(1)} %collective-permute-done.10.refs_2_) | copy-start | bytes 552964
  115.6 24.3 %collective-permute-start.15 = (bf16[720,128]{1,0:T(8,128)(2,1)S(1)}, bf16[720,128]{1,0:T(8,128)(2,1)S(1)}, u32[]{:S(2)}, u32[]{:S(2)}) collective-permute-start(bf16[720,128]{1,0:T(8,128)(2,1)S(1)} %maximum_maximum_fusion.7), channel_id=1, source_target_pairs={{0,7},{1,6},{2,5},{3,4},{4,3},{5,2},{6,1},{7,0},{8,15},{9,14},{10,... | collective-permute-start | bytes 552968 | tf_op jit(solution)/shard_map/ppermute | solution.py:208
  139.8 0.7 copy-start.17
  139.9 0.7 copy-start.18
  139.9 0.8 copy-start.19
  139.9 0.8 copy-start.20
  139.9 0.9 copy-start.21

commit v2 on v1

v2 whole, which is shorter than its diff:
```python
import functools

import jax
import jax.numpy as jnp
import numpy as np
from jax import lax
from jax.experimental import pallas as pl
from jax.experimental.pallas import tpu as pltpu
from jax.sharding import PartitionSpec as P

G, J, D, F, H, WL, BD, C, W = 40, 8, 192, 32, 8, 256, 24, 320, 4096
CH = J * H * G
REM = 144
ML, MR = 272, 288
LR, RR = 272, 296
NT = BD + 2
KT = 3 * 384

def dot_nt(x, w):
    return lax.dot_general(x, w, (((1,), (1,)), ((), ())), preferred_element_type=jnp.float32)

def build(dst, slot, src, m):
    for n in range(2):
        for e in range(3):
            dst[slot, :, (n * 3 + e) * 128:(n * 3 + e + 1) * 128] = src(n, e).astype(jnp.bfloat16)
    lane = lax.broadcasted_iota(jnp.int32, (m, 128), 1)
    pair = jnp.where(lane < 64, src(2, 0), pltpu.roll(src(2, 1), 64, 1))
    dst[slot, :, 768:896] = pair.astype(jnp.bfloat16)
    dst[slot, :, 896:960] = src(2, 2)[:, :64].astype(jnp.bfloat16)

def conv_kernel(m, at, s_ref, *refs):
    xin = refs[:8]
    wm1, wr1, wm2, wr2, order, out_ref, raw, xs, hs, ts, z, fb, feat, wide = refs[8:]
    k, base = s_ref[0], s_ref[1]
    y = k & 1
    if at:
        start = window_start(k)
        formats = [(FULL, start)] * 2 + [(288, 0)] * 2 + [(PAIR, 24 - 24 * y), (288, 0), (288, 0), (PAIR, 24 - 24 * y)]
    else:
        formats = [(m, 0)] * 8
    source = [k, k ^ 1, (k + 6) & 7, (k + 2) & 7, (k + 4) & 7, ((k + 6) & 7) ^ 1, ((k + 2) & 7) ^ 1, ((k + 4) & 7) ^ 1]
    for d in range(8):
        h, (size, start) = source[d], formats[d]
        rem = REM if size == m else size // 2
        if size == m:
            uncut(raw.at[h], xin[d], at, m, rem)
        else:
            uncut(wide, xin[d], at, size, rem)
            for n in range(3):
                raw[h, n, 0:m, :] = wide[n, pl.ds(start, m), :]
    for slot in (0, 9):
        xs[slot] = jnp.zeros((m, 960), jnp.bfloat16)
        hs[slot] = jnp.zeros((m, 960), jnp.bfloat16)
        z[slot] = jnp.zeros((2, m, 128), jnp.float32)
    col = base + lax.broadcasted_iota(jnp.int32, (m, 128), 0)

    def rest(x, wr, h):
        y = dot_nt(x[h + 1], wr[...])
        z[h + 1, 0] = y[:, :128]
        z[h + 1, 1, :, 0:64] = y[:, 128:192]

    def conv(x, wm, h):
        y = dot_nt(x[h], wm[0])
        y += dot_nt(x[h + 1], wm[1])
        y += dot_nt(x[h + 2], wm[2])
        return y[:, :128], y[:, 128:], z[h, 0] + pltpu.roll(z[h + 1, 0], 64, 1) + z[h + 2, 1]

    def load(h, c):
        build(xs, h + 1, lambda n, e: raw[h, n, e:e + m, :], m)
        rest(xs, wr1, h)
        return c
    lax.fori_loop(0, H, load, 0)
    def first(h, c):
        ok = jnp.logical_and(col + 1 >= 0, col + 1 < W)
        for n, y in enumerate(conv(xs, wm1, h)):
            ts[n, 0:m, :] = jnp.where(ok, jnp.maximum(y, 0.0), 0.0)
        build(hs, h + 1, lambda n, e: ts[n, e:e + m, :], m)
        return c
    lax.fori_loop(0, H, first, 0)
    def rest2(h, c):
        rest(hs, wr2, h)
        return c
    lax.fori_loop(0, H, rest2, 0)
    def second(h, c):
        ok = jnp.logical_and(col + 2 >= 0, col + 2 < W)
        for n, y in enumerate(conv(hs, wm2, h)):
            y = jnp.where(ok, y + raw[h, n, 2:2 + m, :], 0.0)
            if n < 2:
                fb[:, n * 128:n * 128 + 128] = y.astype(jnp.bfloat16)
            else:
                fb[:, 256:320] = y[:, :64].astype(jnp.bfloat16)
        y = jnp.dot(fb[...], order[...], preferred_element_type=jnp.float32)
        for n in range(3):
            feat[h, n] = y[:, n * 128:n * 128 + 128]
        return c
    lax.fori_loop(0, H, second, 0)

    lane = lax.broadcasted_iota(jnp.int32, (16, 128), 1)
    def place(i, c):
        row = pl.multiple_of(i * 16, 16)
        for q in range(20):
            got = None
            for j in range(J):
                for h in range(H):
                    t0 = j * H * G + h * G
                    lo, hi = max(t0, q * 128), min(t0 + G, q * 128 + 128)
                    if lo >= hi:
                        continue
                    x = feat[h, j // 3, pl.ds(row, 16), :]
                    sh = (t0 - (j % 3) * G) % 128
                    if sh:
                        x = pltpu.roll(x, sh, 1)
                    got = x if got is None else jnp.where(lane >= lo - q * 128, x, got)
            out_ref[pl.ds(row, 16), q * 128:q * 128 + 128] = got.astype(jnp.bfloat16)
        return c
    lax.fori_loop(0, m // 16, place, 0)

def conv_call(m, at, scal, xs, weights):
    return pl.pallas_call(
        functools.partial(conv_kernel, m, at),
        out_shape=jax.ShapeDtypeStruct((m, CH), jnp.bfloat16),
        in_specs=[pl.BlockSpec(memory_space=pltpu.SMEM)] + [pl.BlockSpec(memory_space=pltpu.VMEM)] * 13,
        out_specs=pl.BlockSpec(memory_space=pltpu.VMEM),
        scratch_shapes=[pltpu.VMEM((8, 3, m + 8, 128), jnp.float32), pltpu.VMEM((10, m, 960), jnp.bfloat16),
                        pltpu.VMEM((10, m, 960), jnp.bfloat16), pltpu.VMEM((3, m + 8, 128), jnp.float32),
                        pltpu.VMEM((10, 2, m, 128), jnp.float32), pltpu.VMEM((m, C), jnp.bfloat16), pltpu.VMEM((8, 3, m, 128), jnp.float32), pltpu.VMEM((3, 480, 128), jnp.float32)],
        compiler_params=pltpu.CompilerParams(vmem_limit_bytes=56 * 2**20),
        cost_estimate=pl.CostEstimate(flops=2 * 18 * m * H * C * C * 2, bytes_accessed=6_000_000, transcendentals=0),
        name="feature_block",
    )(scal, *xs, *weights)

def order_matrix():
    lane = np.arange(384)
    j, g = 3 * (lane // 128) + (lane % 128) // G, (lane % 128) % G
    hit = (np.arange(C)[:, None] == (g * J + j)[None, :]) & (lane % 128 < 3 * G)[None, :] & (j < J)[None, :]
    return jnp.asarray(hit, jnp.bfloat16)

def weights_kernel(w1, w2, aw, wm1, wr1, wm2, wr2, bt, tmp):
    lane = lax.broadcasted_iota(jnp.int32, (C, 128), 1)
    for w, wm, wr in ((w1, wm1, wr1), (w2, wm2, wr2)):
        for b in range(3):
            def put(at, width, x, b=b, wm=wm, wr=wr):
                wm[b, :, at:at + width] = x[:256]
                wr[b * 64:b * 64 + 64, at:at + width] = x[256:]
            for e in range(3):
                for n in range(2):
                    put((n * 3 + e) * 128, 128, w[b * 3 + e, :, n * 128:n * 128 + 128])
            zero = jnp.zeros((C, 64), jnp.float32)
            last = [jnp.concatenate([w[b * 3 + e, :, 256:320].astype(jnp.float32), zero], axis=1) for e in range(3)]
            pair = jnp.where(lane < 64, last[0], pltpu.roll(last[1], 64, 1))
            put(768, 128, pair.astype(jnp.bfloat16))
            put(896, 64, w[b * 3 + 2, :, 256:320])
    wide = lax.broadcasted_iota(jnp.int32, (F, 384), 1)
    for a in range(3):
        for e in range(3):
            x = jnp.concatenate([aw[a * 3 + e].astype(jnp.float32), jnp.zeros((F, 264), jnp.float32)], axis=1) * 0.125
            for ho in range(H):
                y = x if ho == 1 else pltpu.roll(x, ((ho - 1) * G) % 384, 1)
                y = jnp.where(wide < H * G, y, 0.0)
                for n in range(3):
                    tmp[n, pl.ds(ho, F, stride=H), :] = y[:, n * 128:n * 128 + 128]
            for n in range(3):
                bt[a, :, e * 384 + n * 128:e * 384 + n * 128 + 128] = tmp[n].astype(jnp.bfloat16)

def weights_call(w1, w2, aw):
    aw = aw.transpose(0, 3, 2, 1, 4).reshape(9, F, 3 * G)
    bf = lambda *s: jax.ShapeDtypeStruct(s, jnp.bfloat16)
    return pl.pallas_call(
        weights_kernel,
        out_shape=[bf(3, 256, 960), bf(192, 960), bf(3, 256, 960), bf(192, 960), bf(3, F * H, 3 * 384)],
        scratch_shapes=[pltpu.VMEM((3, F * H, 128), jnp.float32)],
        compiler_params=pltpu.CompilerParams(vmem_limit_bytes=32 * 2**20),
        cost_estimate=pl.CostEstimate(flops=10_000_000, bytes_accessed=10_000_000, transcendentals=0),
        name="pack_weights",
    )(w1.reshape(9, C, C), w2.reshape(9, C, C), aw)

FULL, PAIR = 480, 320
LP = 2 * 272 + REM

def cut(dst, at, src, start, m, rem):
    for n in range(2):
        dst[at + n * m:at + n * m + m, :] = src[n, pl.ds(start, m), :].astype(jnp.bfloat16)
    lane = lax.broadcasted_iota(jnp.int32, (rem, 128), 1)
    pair = jnp.where(lane < 64, src[2, pl.ds(start, rem), :], pltpu.roll(src[2, pl.ds(start + m - rem, rem), :], 64, 1))
    dst[at + 2 * m:at + 2 * m + rem, :] = pair.astype(jnp.bfloat16)

def uncut(dst, src, at, m, rem):
    for n in range(2):
        dst[n, 0:m, :] = src[at + n * m:at + n * m + m, :].astype(jnp.float32)
    x = src[at + 2 * m:at + 2 * m + rem, :].astype(jnp.float32)
    dst[2, 0:rem, :] = x
    dst[2, m - rem:m, :] = pltpu.roll(x, 64, 1)

def window_start(k):
    return 181 - BD * k

def pack_kernel(k_ref, lt, rt, before, after, full, up, down, far, lext, rext):
    k = k_ref[0]
    f32 = lambda x: x.astype(jnp.float32)
    for n in range(3):
        w = 128 if n < 2 else 64
        col = slice(n * 128, n * 128 + w)
        lext[n, 0:16, :w] = f32(before[0:16, col])
        lext[n, 16:272, :w] = f32(lt[:, col])
        lext[n, 272:288, :w] = f32(after[0:16, col])
        rext[n, 0:208, :w] = f32(before[16:224, col])
        rext[n, 208:464, :w] = f32(rt[:, col])
        rext[n, 464:480, :w] = f32(after[16:32, col])
    for dst in (full, up, down, far):
        cut(dst, 0, lext, 13, 272, REM)
    cut(full, LP, rext, 0, FULL, FULL // 2)
    cut(up, LP, rext, window_start((k + 2) & 7), 288, REM)
    cut(down, LP, rext, window_start((k + 6) & 7), 288, REM)
    cut(far, LP, rext, window_start(((k + 4) & 7) | 1), PAIR, PAIR // 2)

def relay_kernel(k_ref, got, up, down, rext):
    k = k_ref[0]
    uncut(rext, got, LP, FULL, FULL // 2)
    for dst, to in ((up, (k + 2) & 7), (down, (k + 6) & 7)):
        dst[0:LP, :] = got[0:LP, :]
        cut(dst, LP, rext, window_start(to), 288, REM)

def rows_of(n):
    return jax.ShapeDtypeStruct((n, 128), jnp.bfloat16)

EXACT, WHOLE, TWO = LP + 720, LP + 1200, LP + 800

def small_call(kernel, k, args, outs, scratch, name):
    return pl.pallas_call(
        kernel,
        out_shape=[rows_of(n) for n in outs],
        in_specs=[pl.BlockSpec(memory_space=pltpu.SMEM)] + [pl.BlockSpec(memory_space=pltpu.VMEM)] * len(args),
        scratch_shapes=[pltpu.VMEM((3, n, 128), jnp.float32) for n in scratch],
        compiler_params=pltpu.CompilerParams(vmem_limit_bytes=32 * 2**20),
        cost_estimate=pl.CostEstimate(flops=2_000_000, bytes_accessed=3_000_000, transcendentals=0),
        name=name,
    )(k, *args)

def corr2(l_ref, r_ref, v_ref, p):
    def tile(i, c):
        row = pl.multiple_of(i * 8, 8)
        q = [[None] * 5 for _ in range(2)]
        for m in range(4):
            for n in range(5):
                lt = l_ref[m * 5 + n, pl.ds(row, 8), :]
                for u in range(2):
                    pr = lt * r_ref[m * 5 + n, pl.ds(row + (25 - u) - 2 * p, 8), :]
                    q[u][n] = pr if m == 0 else q[u][n] + pr
        for u in range(2):
            x = jnp.concatenate(q[u], axis=1)
            x = x + pltpu.roll(x, 320, 1)
            for n in range(3):
                v_ref[u, n, pl.ds(row, 8), :] = x[:, n * 128:n * 128 + 128]
        return c
    lax.fori_loop(0, 33, tile, 0, unroll=3)

def agg_kernel(k_ref, l_ref, r_ref, b_ref, out_ref, lf_ref, rf_ref, v_ref, vs_ref):
    k = k_ref[0]
    for n in range(20):
        lf_ref[n] = l_ref[:, n * 128:n * 128 + 128].astype(jnp.float32)
        rf_ref[n, 0:MR, :] = r_ref[:, n * 128:n * 128 + 128].astype(jnp.float32)
    def pair(p, c):
        corr2(lf_ref, rf_ref, v_ref, p)
        for u in range(2):
            t = 2 * p + u
            d = 24 * k - 1 + t
            ok = jnp.logical_and(d >= 0, d < D)
            m = jnp.where(ok, 1.0, 0.0).astype(jnp.float32)
            for e in range(3):
                for n in range(3):
                    vs_ref[t, :, e * 384 + n * 128:e * 384 + n * 128 + 128] = (v_ref[u, n, e:e + WL, :] * m).astype(jnp.bfloat16)
        return c
    lax.fori_loop(0, NT // 2, pair, 0)
    def out(d, c):
        y = dot_nt(vs_ref[d], b_ref[0])
        y += dot_nt(vs_ref[d + 1], b_ref[1])
        y += dot_nt(vs_ref[d + 2], b_ref[2])
        y = jnp.maximum(y, 0.0).T.reshape(F, H, WL)
        out_ref[:, d] = y.astype(jnp.bfloat16)
        return c
    lax.fori_loop(0, BD, out, 0)

def agg_call(k, lx, rx, b):
    return pl.pallas_call(
        agg_kernel,
        out_shape=jax.ShapeDtypeStruct((F, BD, H, WL), jnp.bfloat16),
        in_specs=[pl.BlockSpec(memory_space=pltpu.SMEM)] + [pl.BlockSpec(memory_space=pltpu.VMEM)] * 3,
        out_specs=pl.BlockSpec(memory_space=pltpu.VMEM),
        scratch_shapes=[pltpu.VMEM((20, LR, 128), jnp.float32), pltpu.VMEM((20, RR, 128), jnp.float32),
                        pltpu.VMEM((2, 3, LR, 128), jnp.float32), pltpu.VMEM((NT, WL, KT), jnp.bfloat16)],
        compiler_params=pltpu.CompilerParams(vmem_limit_bytes=56 * 2**20),
        name="correlate_aggregate",
    )(k, lx, rx, b)


def from_col(x, by):
    n = lax.axis_size("col")
    return lax.ppermute(x, "col", [(i, i + by) for i in range(n) if 0 <= i + by < n])


def to_band(x, z, y):
    n = lax.axis_size("band")
    return lax.ppermute(x, "band", [(i, ((i + 2 * z) % n) ^ y) for i in range(n)])


def shards(left_view, right_view, first_weight, second_weight, agg_weight):
    k = lax.axis_index("band").astype(jnp.int32)
    base = lax.axis_index("col").astype(jnp.int32) * WL
    left = left_view[:, 0].T
    right = right_view[:, 0].T
    before = from_col(jnp.concatenate([left[WL - 16:], right[WL - 208:]], axis=0), 1)
    after = from_col(jnp.concatenate([left[:16], right[:16]], axis=0), -1)
    full, up, down, far = small_call(pack_kernel, k[None], (left, right, before, after), (WHOLE, EXACT, EXACT, TWO), (288, FULL), "pack_rows")
    across = to_band(full, 0, 1)
    above, below, twice = to_band(up, 1, 0), to_band(down, 3, 0), to_band(far, 2, 0)
    up, down = small_call(relay_kernel, k[None], (across,), (EXACT, EXACT), (FULL,), "relay_rows")
    rows = [full, across, above, below, twice, to_band(up, 1, 0), to_band(down, 3, 0), to_band(twice, 0, 1)]
    *weights, taps = weights_call(first_weight, second_weight, agg_weight)
    weights = (*weights, order_matrix())
    lf = conv_call(ML, 0, jnp.stack([k, base - 3]), rows, weights)
    rf = conv_call(MR, LP, jnp.stack([k, base - BD * k - 27]), rows, weights)
    return agg_call(k[None], lf, rf, taps)


def solution(mesh):
    return jax.shard_map(
        shards,
        mesh=mesh,
        in_specs=(P(None, "band", "col"), P(None, "band", "col"), P(), P(), P()),
        out_specs=P(None, "band", None, "col"),
        check_vma=False,
    )
```

time: 208 us -> 145 us (0.70)
  local copies, waits for them, and re-layouts: 64.5 us -> 10.2 us
  Pallas kernels: 88.4 us -> 103 us
  starting transfers between devices: 28.9 us -> 18.7 us
  other arithmetic: 10.2 us -> 0.65 us
    reshape x8 -> x1, local copies, waits for them, and re-layouts: 17.1 us -> 0.16 us  [weights_call(): aw = aw.transpose(0, 3, 2, 1, 4).reshape(9, F, 3 * G)]
    another operation x13 -> x0, local copies, waits for them, and re-layouts: 16.8 us -> none  [the longest x10 16.5 us: agg_rhs(): cols.append(jnp.stack(rows, axis=2))]
    pallas_call x2 -> x5, Pallas kernels: 46.4 us -> 60.1 us  [the longest x2 56.1 us: conv_call(): pl.pallas_call(functools.partial(conv_kernel, m, at), out_shape=jax.Shape...]
    ppermute x14 -> x7, starting transfers between devices: 24.6 us -> 13.1 us  [to_band(): return lax.ppermute(x, 'band', [(i, (i + 2 * z) % n ^ y) for i in range(n)])]
    transpose x7 -> x1, local copies, waits for them, and re-layouts: 11.1 us -> 1.09 us  [weights_call(): aw = aw.transpose(0, 3, 2, 1, 4).reshape(9, F, 3 * G)]
    slice x12 -> x0, local copies, waits for them, and re-layouts: 7.64 us -> none  [the longest x2 2.66 us: conv_weights(): a[:, :, :256].reshape(3, 3, 2, 128, C).transpose(0, 2, 1, 3, 4)]
    concatenate x11 -> x0, other arithmetic: 3.44 us -> none  [the longest x1 1.92 us: conv_weights(): full = jnp.concatenate([main, a[:, :, 256:].reshape(3, 192, C)], axis=1)]
    ppermute x14 -> x7, waiting for transfers between devices: 13.8 us -> 11.2 us  [to_band(): return lax.ppermute(x, 'band', [(i, (i + 2 * z) % n ^ y) for i in range(n)])]
  transfers between devices with their start and end apart: 16 -> 9, of which waited for: 4 -> 3; matrix products, arithmetic and copies ran while one was open for 34% -> 1% of each run, Pallas kernels for 11% -> 2%
where the time goes in v2:
time: 145 us
  Pallas kernels  103 us (71%)
  starting transfers between devices  18.7 us (13%)
  waiting for transfers between devices  12.7 us (9%)
  local copies, waits for them, and re-layouts  10.2 us (7%)
    pallas_call x2, Pallas kernels, conv_call(): pl.pallas_call(functools.partial(conv_kernel, m, at), out_shape=jax.Shape...  56.1 us
    pallas_call x1, Pallas kernels, agg_call(): pl.pallas_call(agg_kernel, out_shape=jax.ShapeDtypeStruct((F, BD, H, WL),...  42.5 us
    ppermute x7, starting transfers between devices, to_band(): return lax.ppermute(x, 'band', [(i, (i + 2 * z) % n ^ y) for i in range(n)])  13.1 us
    ppermute x7, waiting for transfers between devices, to_band(): return lax.ppermute(x, 'band', [(i, (i + 2 * z) % n ^ y) for i in range(n)])  11.2 us
    unnamed x20, local copies, waits for them, and re-layouts  8.95 us
    ppermute x2, starting transfers between devices, from_col(): lax.ppermute(x, 'col', [(i, i + by) for i in range(n) if 0 <= i + by < n])  5.56 us
  transfers between devices with their start and end apart: 9, of which 3 were waited for; matrix products, arithmetic and copies ran while one was open for 1% of the time, Pallas kernels for 2%

profile of v2, /device:TPU:20, one launch (start us, length us, event | category | flops | bytes accessed | tf_op | source)
XLA Modules:
  0.0 145.0 jit_solution(17003546829186122373)
XLA Ops:
  0.0 0.0 copy-start
  0.0 1.2 copy.10
  1.2 1.1 copy.11
  2.4 1.9 %collective-permute-start = (bf16[224,320]{1,0:T(8,128)(2,1)S(1)}, bf16[224,320]{1,0:T(8,128)(2,1)S(1)}, u32[]{:S(2)}, u32[]{:S(2)}) collective-permute-start(bf16[224,320]{1,0:T(8,128)(2,1)S(1)} %pad_maximum_fusion), channel_id=1, source_target_pairs={{0,8},{8,16},{16,24},{24,32},{32,40},{40,48},{48,56},{56,64},{64,7... | collective-permute-start | bytes 430088 | tf_op jit(solution)/shard_map/ppermute | solution.py:298
  4.3 3.6 %collective-permute-start.1 = (bf16[32,320]{1,0:T(8,128)(2,1)S(1)}, bf16[32,320]{1,0:T(8,128)(2,1)S(1)}, u32[]{:S(2)}, u32[]{:S(2)}) collective-permute-start(bf16[32,320]{1,0:T(8,128)(2,1)S(1)} %pad_maximum_fusion.1), channel_id=1, source_target_pairs={{8,0},{16,8},{24,16},{32,24},{40,32},{48,40},{56,48},{64,56},{72,6... | collective-permute-start | bytes 61448 | tf_op jit(solution)/shard_map/ppermute | solution.py:298
  8.0 1.5 %collective-permute-done.1.after = bf16[32,320]{1,0:T(8,128)(2,1)S(1)} collective-permute-done((bf16[32,320]{1,0:T(8,128)(2,1)S(1)}, bf16[32,320]{1,0:T(8,128)(2,1)S(1)}, u32[]{:S(2)}, u32[]{:S(2)}) %collective-permute-start.1) | collective-permute-done | bytes 20512 | tf_op jit(solution)/shard_map/ppermute | solution.py:298
  9.5 0.0 collective-permute-done.before
  9.5 1.1 pack_rows.1
  10.6 0.0 copy-start.6
  10.6 1.3 collective-permute-start.2
  11.9 3.9 %collective-permute-start.5 = (bf16[1488,128]{1,0:T(8,128)(2,1)S(1)}, bf16[1488,128]{1,0:T(8,128)(2,1)}, u32[]{:S(2)}, u32[]{:S(2)}) collective-permute-start(bf16[1488,128]{1,0:T(8,128)(2,1)S(1)} %get-tuple-element.19), channel_id=1, source_target_pairs={{0,4},{1,5},{2,6},{3,7},{4,0},{5,1},{6,2},{7,3},{8,12},{9,13},{10,... | collective-permute-start | bytes 1142792 | tf_op jit(solution)/shard_map/ppermute | solution.py:303
  15.7 9.5 %collective-permute-done.5.refs_4_ = bf16[1488,128]{1,0:T(8,128)(2,1)} collective-permute-done((bf16[1488,128]{1,0:T(8,128)(2,1)S(1)}, bf16[1488,128]{1,0:T(8,128)(2,1)}, u32[]{:S(2)}, u32[]{:S(2)}) %collective-permute-start.5) | collective-permute-done | bytes 380960 | tf_op jit(solution)/shard_map/ppermute | solution.py:303
  25.2 0.7 collective-permute-start.8
  26.0 1.9 %collective-permute-start.3 = (bf16[1408,128]{1,0:T(8,128)(2,1)}, bf16[1408,128]{1,0:T(8,128)(2,1)}, u32[]{:S(2)}, u32[]{:S(2)}) collective-permute-start(bf16[1408,128]{1,0:T(8,128)(2,1)} %get-tuple-element.17), channel_id=1, source_target_pairs={{0,2},{1,3},{2,4},{3,5},{4,6},{5,7},{6,0},{7,1},{8,10},{9,11},{10,... | collective-permute-start | bytes 1081352 | tf_op jit(solution)/shard_map/ppermute | solution.py:303
  27.8 2.1 %collective-permute-start.4 = (bf16[1408,128]{1,0:T(8,128)(2,1)}, bf16[1408,128]{1,0:T(8,128)(2,1)}, u32[]{:S(2)}, u32[]{:S(2)}) collective-permute-start(bf16[1408,128]{1,0:T(8,128)(2,1)} %get-tuple-element.18), channel_id=1, source_target_pairs={{0,6},{1,7},{2,0},{3,1},{4,2},{5,3},{6,4},{7,5},{8,14},{9,15},{10,... | collective-permute-start | bytes 1081352 | tf_op jit(solution)/shard_map/ppermute | solution.py:303
  29.9 0.0 collective-permute-done.2.got.refs_1_
  29.9 0.0 copy-start.3
  29.9 1.1 relay_rows.1
  31.0 0.0 collective-permute-start.6
  31.0 3.2 %collective-permute-start.7 = (bf16[1408,128]{1,0:T(8,128)(2,1)}, bf16[1408,128]{1,0:T(8,128)(2,1)}, u32[]{:S(2)}, u32[]{:S(2)}) collective-permute-start(bf16[1408,128]{1,0:T(8,128)(2,1)} %get-tuple-element.21), channel_id=1, source_target_pairs={{0,6},{1,7},{2,0},{3,1},{4,2},{5,3},{6,4},{7,5},{8,14},{9,15},{10,... | collective-permute-start | bytes 1081352 | tf_op jit(solution)/shard_map/ppermute | solution.py:303
  34.2 1.1 copy.12
  35.3 0.2 reshape.11.aw
  35.5 0.0 copy-done
  35.5 0.0 copy-start.1
  35.5 1.6 %copy-done.1 = bf16[3,3,320,320]{3,2,1,0:T(8,128)(2,1)S(1)} copy-done((bf16[3,3,320,320]{3,2,1,0:T(8,128)(2,1)S(1)}, bf16[3,3,320,320]{3,2,1,0:T(8,128)(2,1)}, u32[]{:S(2)}) %copy-start.1) | copy-done | bytes 1843224
  37.1 1.9 %pack_weights.1 = (bf16[3,256,960]{2,1,0:T(8,128)(2,1)S(1)}, bf16[192,960]{1,0:T(8,128)(2,1)S(1)}, bf16[3,256,960]{2,1,0:T(8,128)(2,1)S(1)}, bf16[192,960]{1,0:T(8,128)(2,1)S(1)}, bf16[3,256,1152]{2,1,0:T(8,128)(2,1)S(1)}) custom-call(bf16[9,320,320]{2,1,0:T(8,128)(2,1)S(1)} %bitcast.12, bf16[9,320,320]{2,1,0:T(8,128)(2,1)S(1)} %bitcast.13, ...), custom_call_target="tpu_custom_call" | custom-call | flops 10000000 | bytes 10000000 | tf_op jit(solution)/shard_map/pack_weights/pallas_call | solution.py:168
  39.0 0.0 copy-done.6
  39.0 0.0 copy-done.3
  39.0 0.0 copy-start.2
  39.1 1.2 copy-done.2
  40.3 0.0 copy-start.4
  40.3 1.1 copy-done.4
  41.4 0.0 copy-start.5
  41.4 1.2 copy-done.5
  42.6 0.0 copy-start.7
  42.6 0.7 copy-done.7
  43.3 0.0 copy-start.8
  43.3 0.8 copy-done.8
  44.1 0.6 pad_add_fusion
  44.7 0.0 collective-permute-done.3.refs_2_
  44.7 0.0 collective-permute-done.4.refs_3_
  44.7 0.0 collective-permute-done.8.refs_7_
  44.7 1.7 %collective-permute-done.6.refs_5_ = bf16[1408,128]{1,0:T(8,128)(2,1)} collective-permute-done((bf16[1408,128]{1,0:T(8,128)(2,1)}, bf16[1408,128]{1,0:T(8,128)(2,1)}, u32[]{:S(2)}, u32[]{:S(2)}) %collective-permute-start.6) | collective-permute-done | bytes 360480 | tf_op jit(solution)/shard_map/ppermute | solution.py:303
  46.4 0.0 collective-permute-done.7.refs_6_
  46.4 27.6 %feature_block.2.l_ref = bf16[272,2560]{1,0:T(8,128)(2,1)} custom-call(s32[2]{0:T(128)} %get-tuple-element.29.s_ref, bf16[1888,128]{1,0:T(8,128)(2,1)} %copy-done.6, bf16[1888,128]{1,0:T(8,128)(2,1)} %copy-done.3, bf16[1408,128]{1,0:T(8,128)(2,1)} %collective-permute-done.3.refs_2_, bf16[1408,128]{1,0:T(8,128)(2,1)} %collective-permute-done.4.refs_3_, ...), custom_call_target="tpu_custom_call" | custom-call | flops 16043212800 | bytes 6000000 | tf_op jit(solution)/shard_map/feature_block/pallas_call | solution.py:119
  74.0 28.5 %feature_block.3.r_ref = bf16[288,2560]{1,0:T(8,128)(2,1)} custom-call(s32[2]{0:T(128)} %get-tuple-element.30.s_ref, bf16[1888,128]{1,0:T(8,128)(2,1)} %copy-done.6, bf16[1888,128]{1,0:T(8,128)(2,1)} %copy-done.3, bf16[1408,128]{1,0:T(8,128)(2,1)} %collective-permute-done.3.refs_2_, bf16[1408,128]{1,0:T(8,128)(2,1)} %collective-permute-done.4.refs_3_, ...), custom_call_target="tpu_custom_call" | custom-call | flops 16986931200 | bytes 6000000 | tf_op jit(solution)/shard_map/feature_block/pallas_call | solution.py:119
  102.5 42.5 %correlate_aggregate.1 = bf16[32,24,8,256]{3,2,1,0:T(8,128)(2,1)} custom-call(s32[1]{0:T(128)} %bitcast.k_ref, bf16[272,2560]{1,0:T(8,128)(2,1)} %feature_block.2.l_ref, bf16[288,2560]{1,0:T(8,128)(2,1)} %feature_block.3.r_ref, bf16[3,256,1152]{2,1,0:T(8,128)(2,1)} %copy-done.2), custom_call_target="tpu_custom_call" | custom-call | tf_op jit(solution)/shard_map/correlate_aggregate/pallas_call | solution.py:284
  (5 shorter events, 0.1 us)
Async XLA Ops:
  0.0 35.5 %copy-start = (bf16[3,3,320,320]{3,2,1,0:T(8,128)(2,1)S(1)}, bf16[3,3,320,320]{3,2,1,0:T(8,128)(2,1)}, u32[]{:S(2)}) copy-start(bf16[3,3,320,320]{3,2,1,0:T(8,128)(2,1)} %param.8) | copy-start | bytes 5529604
  2.4 7.1 %collective-permute-start = (bf16[224,320]{1,0:T(8,128)(2,1)S(1)}, bf16[224,320]{1,0:T(8,128)(2,1)S(1)}, u32[]{:S(2)}, u32[]{:S(2)}) collective-permute-start(bf16[224,320]{1,0:T(8,128)(2,1)S(1)} %pad_maximum_fusion), channel_id=1, source_target_pairs={{0,8},{8,16},{16,24},{24,32},{32,40},{40,48},{48,56},{56,64},{64,7... | collective-permute-start | bytes 430088 | tf_op jit(solution)/shard_map/ppermute | solution.py:298
  4.3 5.1 %collective-permute-start.1 = (bf16[32,320]{1,0:T(8,128)(2,1)S(1)}, bf16[32,320]{1,0:T(8,128)(2,1)S(1)}, u32[]{:S(2)}, u32[]{:S(2)}) collective-permute-start(bf16[32,320]{1,0:T(8,128)(2,1)S(1)} %pad_maximum_fusion.1), channel_id=1, source_target_pairs={{8,0},{16,8},{24,16},{32,24},{40,32},{48,40},{56,48},{64,56},{72,6... | collective-permute-start | bytes 61448 | tf_op jit(solution)/shard_map/ppermute | solution.py:298
  10.6 28.5 %copy-start.6 = (bf16[1888,128]{1,0:T(8,128)(2,1)}, bf16[1888,128]{1,0:T(8,128)(2,1)S(1)}, u32[]{:S(2)}) copy-start(bf16[1888,128]{1,0:T(8,128)(2,1)S(1)} %get-tuple-element.16.refs_0_) | copy-start | bytes 1449988
  10.6 19.4 %collective-permute-start.2 = (bf16[1888,128]{1,0:T(8,128)(2,1)S(1)}, bf16[1888,128]{1,0:T(8,128)(2,1)S(1)}, u32[]{:S(2)}, u32[]{:S(2)}) collective-permute-start(bf16[1888,128]{1,0:T(8,128)(2,1)S(1)} %get-tuple-element.16.refs_0_), channel_id=1, source_target_pairs={{0,1},{1,0},{2,3},{3,2},{4,5},{5,4},{6,7},{7,6},{8,9},{9,8},{10,11... | collective-permute-start | bytes 1449992 | tf_op jit(solution)/shard_map/ppermute | solution.py:303
  11.9 13.4 %collective-permute-start.5 = (bf16[1488,128]{1,0:T(8,128)(2,1)S(1)}, bf16[1488,128]{1,0:T(8,128)(2,1)}, u32[]{:S(2)}, u32[]{:S(2)}) collective-permute-start(bf16[1488,128]{1,0:T(8,128)(2,1)S(1)} %get-tuple-element.19), channel_id=1, source_target_pairs={{0,4},{1,5},{2,6},{3,7},{4,0},{5,1},{6,2},{7,3},{8,12},{9,13},{10,... | collective-permute-start | bytes 1142792 | tf_op jit(solution)/shard_map/ppermute | solution.py:303
  25.2 19.5 %collective-permute-start.8 = (bf16[1488,128]{1,0:T(8,128)(2,1)}, bf16[1488,128]{1,0:T(8,128)(2,1)}, u32[]{:S(2)}, u32[]{:S(2)}) collective-permute-start(bf16[1488,128]{1,0:T(8,128)(2,1)} %collective-permute-done.5.refs_4_), channel_id=1, source_target_pairs={{0,1},{1,0},{2,3},{3,2},{4,5},{5,4},{6,7},{7,6},{8,9},{9,8},{10,11... | collective-permute-start | bytes 1142792 | tf_op jit(solution)/shard_map/ppermute | solution.py:303
  26.0 18.7 %collective-permute-start.3 = (bf16[1408,128]{1,0:T(8,128)(2,1)}, bf16[1408,128]{1,0:T(8,128)(2,1)}, u32[]{:S(2)}, u32[]{:S(2)}) collective-permute-start(bf16[1408,128]{1,0:T(8,128)(2,1)} %get-tuple-element.17), channel_id=1, source_target_pairs={{0,2},{1,3},{2,4},{3,5},{4,6},{5,7},{6,0},{7,1},{8,10},{9,11},{10,... | collective-permute-start | bytes 1081352 | tf_op jit(solution)/shard_map/ppermute | solution.py:303
  27.8 16.9 %collective-permute-start.4 = (bf16[1408,128]{1,0:T(8,128)(2,1)}, bf16[1408,128]{1,0:T(8,128)(2,1)}, u32[]{:S(2)}, u32[]{:S(2)}) collective-permute-start(bf16[1408,128]{1,0:T(8,128)(2,1)} %get-tuple-element.18), channel_id=1, source_target_pairs={{0,6},{1,7},{2,0},{3,1},{4,2},{5,3},{6,4},{7,5},{8,14},{9,15},{10,... | collective-permute-start | bytes 1081352 | tf_op jit(solution)/shard_map/ppermute | solution.py:303
  29.9 9.1 %copy-start.3 = (bf16[1888,128]{1,0:T(8,128)(2,1)}, bf16[1888,128]{1,0:T(8,128)(2,1)S(1)}, u32[]{:S(2)}) copy-start(bf16[1888,128]{1,0:T(8,128)(2,1)S(1)} %collective-permute-done.2.got.refs_1_) | copy-start | bytes 1449988
  31.0 15.4 %collective-permute-start.6 = (bf16[1408,128]{1,0:T(8,128)(2,1)}, bf16[1408,128]{1,0:T(8,128)(2,1)}, u32[]{:S(2)}, u32[]{:S(2)}) collective-permute-start(bf16[1408,128]{1,0:T(8,128)(2,1)} %get-tuple-element.20), channel_id=1, source_target_pairs={{0,2},{1,3},{2,4},{3,5},{4,6},{5,7},{6,0},{7,1},{8,10},{9,11},{10,... | collective-permute-start | bytes 1081352 | tf_op jit(solution)/shard_map/ppermute | solution.py:303
  31.0 15.4 %collective-permute-start.7 = (bf16[1408,128]{1,0:T(8,128)(2,1)}, bf16[1408,128]{1,0:T(8,128)(2,1)}, u32[]{:S(2)}, u32[]{:S(2)}) collective-permute-start(bf16[1408,128]{1,0:T(8,128)(2,1)} %get-tuple-element.21), channel_id=1, source_target_pairs={{0,6},{1,7},{2,0},{3,1},{4,2},{5,3},{6,4},{7,5},{8,14},{9,15},{10,... | collective-permute-start | bytes 1081352 | tf_op jit(solution)/shard_map/ppermute | solution.py:303
  35.5 1.6 %copy-start.1 = (bf16[3,3,320,320]{3,2,1,0:T(8,128)(2,1)S(1)}, bf16[3,3,320,320]{3,2,1,0:T(8,128)(2,1)}, u32[]{:S(2)}) copy-start(bf16[3,3,320,320]{3,2,1,0:T(8,128)(2,1)} %param.9) | copy-start | bytes 5529604
  39.0 1.2 copy-start.2
  40.3 1.1 copy-start.4
  41.4 1.2 copy-start.5
  42.6 0.7 copy-start.7
  43.3 0.8 copy-start.8

commit v3 on v2

--- a/solution.py
+++ b/solution.py
@@ -14,10 +14,14 @@
 ML, MR = 272, 288
 LR, RR = 272, 296
 NT = BD + 2
-KT = 3 * 384
-
-def dot_nt(x, w):
-    return lax.dot_general(x, w, (((1,), (1,)), ((), ())), preferred_element_type=jnp.float32)
+KT = 1024
+UN = 4
+
+def dot(x, w):
+    return jnp.dot(x, w, preferred_element_type=jnp.float32)
+
+def dot_on(x, i, y, j):
+    return lax.dot_general(x, y, (((i,), (j,)), ((), ())), preferred_element_type=jnp.float32)
 
 def build(dst, slot, src, m):
     for n in range(2):
@@ -30,7 +34,7 @@
 
 def conv_kernel(m, at, s_ref, *refs):
     xin = refs[:8]
-    wm1, wr1, wm2, wr2, order, out_ref, raw, xs, hs, ts, z, fb, feat, wide = refs[8:]
+    wm1, wr1, wm2, wr2, out_ref, raw, xs, hs, ts, z, feat, wide = refs[8:]
     k, base = s_ref[0], s_ref[1]
     y = k & 1
     if at:
@@ -55,45 +59,42 @@
     col = base + lax.broadcasted_iota(jnp.int32, (m, 128), 0)
 
     def rest(x, wr, h):
-        y = dot_nt(x[h + 1], wr[...])
+        y = dot(x[h + 1], wr[...])
         z[h + 1, 0] = y[:, :128]
         z[h + 1, 1, :, 0:64] = y[:, 128:192]
 
     def conv(x, wm, h):
-        y = dot_nt(x[h], wm[0])
-        y += dot_nt(x[h + 1], wm[1])
-        y += dot_nt(x[h + 2], wm[2])
+        y = dot(x[h], wm[0])
+        y += dot(x[h + 1], wm[1])
+        y += dot(x[h + 2], wm[2])
         return y[:, :128], y[:, 128:], z[h, 0] + pltpu.roll(z[h + 1, 0], 64, 1) + z[h + 2, 1]
 
     def load(h, c):
         build(xs, h + 1, lambda n, e: raw[h, n, e:e + m, :], m)
         rest(xs, wr1, h)
         return c
-    lax.fori_loop(0, H, load, 0)
-    def first(h, c):
+    lax.fori_loop(0, H, load, 0, unroll=UN)
+    def first(i, c):
+        for u in range(UN):
+            first_row(UN * i + u, ts.at[u])
+        return c
+    def first_row(h, ts):
         ok = jnp.logical_and(col + 1 >= 0, col + 1 < W)
         for n, y in enumerate(conv(xs, wm1, h)):
             ts[n, 0:m, :] = jnp.where(ok, jnp.maximum(y, 0.0), 0.0)
         build(hs, h + 1, lambda n, e: ts[n, e:e + m, :], m)
-        return c
-    lax.fori_loop(0, H, first, 0)
+    lax.fori_loop(0, H // UN, first, 0)
     def rest2(h, c):
         rest(hs, wr2, h)
         return c
-    lax.fori_loop(0, H, rest2, 0)
+    lax.fori_loop(0, H, rest2, 0, unroll=UN)
     def second(h, c):
         ok = jnp.logical_and(col + 2 >= 0, col + 2 < W)
         for n, y in enumerate(conv(hs, wm2, h)):
             y = jnp.where(ok, y + raw[h, n, 2:2 + m, :], 0.0)
-            if n < 2:
-                fb[:, n * 128:n * 128 + 128] = y.astype(jnp.bfloat16)
-            else:
-                fb[:, 256:320] = y[:, :64].astype(jnp.bfloat16)
-        y = jnp.dot(fb[...], order[...], preferred_element_type=jnp.float32)
-        for n in range(3):
-            feat[h, n] = y[:, n * 128:n * 128 + 128]
-        return c
-    lax.fori_loop(0, H, second, 0)
+            feat[h, n] = y.astype(jnp.bfloat16).astype(jnp.float32)
+        return c
+    lax.fori_loop(0, H, second, 0, unroll=UN)
 
     lane = lax.broadcasted_iota(jnp.int32, (16, 128), 1)
     def place(i, c):
@@ -106,50 +107,55 @@
                     lo, hi = max(t0, q * 128), min(t0 + G, q * 128 + 128)
                     if lo >= hi:
                         continue
-                    x = feat[h, j // 3, pl.ds(row, 16), :]
-                    sh = (t0 - (j % 3) * G) % 128
-                    if sh:
-                        x = pltpu.roll(x, sh, 1)
-                    got = x if got is None else jnp.where(lane >= lo - q * 128, x, got)
+                    s_lo = lo - t0 + j * G
+                    while lo < hi:
+                        n = s_lo // 128
+                        length = min(hi - lo, (n + 1) * 128 - s_lo)
+                        x = feat[h, n, pl.ds(row, 16), :]
+                        sh = (lo - s_lo) % 128
+                        if sh:
+                            x = pltpu.roll(x, sh, 1)
+                        got = x if got is None else jnp.where(lane >= lo - q * 128, x, got)
+                        lo, s_lo = lo + length, s_lo + length
             out_ref[pl.ds(row, 16), q * 128:q * 128 + 128] = got.astype(jnp.bfloat16)
         return c
-    lax.fori_loop(0, m // 16, place, 0)
+    lax.fori_loop(0, m // 16, place, 0, unroll=2)
 
 def conv_call(m, at, scal, xs, weights):
     return pl.pallas_call(
         functools.partial(conv_kernel, m, at),
         out_shape=jax.ShapeDtypeStruct((m, CH), jnp.bfloat16),
-        in_specs=[pl.BlockSpec(memory_space=pltpu.SMEM)] + [pl.BlockSpec(memory_space=pltpu.VMEM)] * 13,
+        in_specs=[pl.BlockSpec(memory_space=pltpu.SMEM)] + [pl.BlockSpec(memory_space=pltpu.VMEM)] * 12,
         out_specs=pl.BlockSpec(memory_space=pltpu.VMEM),
         scratch_shapes=[pltpu.VMEM((8, 3, m + 8, 128), jnp.float32), pltpu.VMEM((10, m, 960), jnp.bfloat16),
-                        pltpu.VMEM((10, m, 960), jnp.bfloat16), pltpu.VMEM((3, m + 8, 128), jnp.float32),
-                        pltpu.VMEM((10, 2, m, 128), jnp.float32), pltpu.VMEM((m, C), jnp.bfloat16), pltpu.VMEM((8, 3, m, 128), jnp.float32), pltpu.VMEM((3, 480, 128), jnp.float32)],
+                        pltpu.VMEM((10, m, 960), jnp.bfloat16), pltpu.VMEM((UN, 3, m + 8, 128), jnp.float32),
+                        pltpu.VMEM((10, 2, m, 128), jnp.float32), pltpu.VMEM((8, 3, m, 128), jnp.float32), pltpu.VMEM((3, 480, 128), jnp.float32)],
         compiler_params=pltpu.CompilerParams(vmem_limit_bytes=56 * 2**20),
         cost_estimate=pl.CostEstimate(flops=2 * 18 * m * H * C * C * 2, bytes_accessed=6_000_000, transcendentals=0),
         name="feature_block",
     )(scal, *xs, *weights)
 
 def order_matrix():
-    lane = np.arange(384)
-    j, g = 3 * (lane // 128) + (lane % 128) // G, (lane % 128) % G
-    hit = (np.arange(C)[:, None] == (g * J + j)[None, :]) & (lane % 128 < 3 * G)[None, :] & (j < J)[None, :]
-    return jnp.asarray(hit, jnp.bfloat16)
-
-def weights_kernel(w1, w2, aw, wm1, wr1, wm2, wr2, bt, tmp):
+    to = np.arange(C)
+    return jnp.asarray(np.arange(C)[:, None] == ((to % G) * J + to // G)[None, :], jnp.bfloat16)
+
+def weights_kernel(w1, w2, aw, order, wm1, wr1, wm2, wr2, bt, tmp):
     lane = lax.broadcasted_iota(jnp.int32, (C, 128), 1)
-    for w, wm, wr in ((w1, wm1, wr1), (w2, wm2, wr2)):
-        for b in range(3):
-            def put(at, width, x, b=b, wm=wm, wr=wr):
-                wm[b, :, at:at + width] = x[:256]
-                wr[b * 64:b * 64 + 64, at:at + width] = x[256:]
-            for e in range(3):
-                for n in range(2):
-                    put((n * 3 + e) * 128, 128, w[b * 3 + e, :, n * 128:n * 128 + 128])
-            zero = jnp.zeros((C, 64), jnp.float32)
-            last = [jnp.concatenate([w[b * 3 + e, :, 256:320].astype(jnp.float32), zero], axis=1) for e in range(3)]
-            pair = jnp.where(lane < 64, last[0], pltpu.roll(last[1], 64, 1))
-            put(768, 128, pair.astype(jnp.bfloat16))
-            put(896, 64, w[b * 3 + 2, :, 256:320])
+    zero = jnp.zeros((C, 64), jnp.float32)
+    for e in range(3):
+        places = ((0, 128, e * 128), (128, 128, (3 + e) * 128), (256, 64, 768 + e * 64))
+        for w, wm, wr, first in ((w1, wm1, wr1, True), (w2, wm2, wr2, False)):
+            last = []
+            for b in range(3):
+                x = w[b * 3 + e]
+                x = dot_on(order[...], 0, x, 1) if first else dot_on(x, 0, order[...], 0)
+                for at, n, to in places:
+                    wm[b, to:to + n, :] = x[at:at + n, :256].astype(jnp.bfloat16)
+                last.append(jnp.concatenate([x[:, 256:320], zero], axis=1))
+            pair = jnp.where(lane < 64, last[0], pltpu.roll(last[1], 64, 1)).astype(jnp.bfloat16)
+            for at, n, to in places:
+                wr[to:to + n, 0:128] = pair[at:at + n]
+                wr[to:to + n, 128:192] = last[2][at:at + n, :64].astype(jnp.bfloat16)
     wide = lax.broadcasted_iota(jnp.int32, (F, 384), 1)
     for a in range(3):
         for e in range(3):
@@ -159,20 +165,23 @@
                 y = jnp.where(wide < H * G, y, 0.0)
                 for n in range(3):
                     tmp[n, pl.ds(ho, F, stride=H), :] = y[:, n * 128:n * 128 + 128]
-            for n in range(3):
-                bt[a, :, e * 384 + n * 128:e * 384 + n * 128 + 128] = tmp[n].astype(jnp.bfloat16)
-
-def weights_call(w1, w2, aw):
+            for n in range(2):
+                at = a * KT + (n * 3 + e) * 128
+                bt[at:at + 128, :] = tmp[n].T.astype(jnp.bfloat16)
+            at, n = a * KT + 768 + e * 64, 64 if e < 2 else 128
+            bt[at:at + n, :] = tmp[2].T[:n].astype(jnp.bfloat16)
+
+def weights_call(w1, w2, aw, order):
     aw = aw.transpose(0, 3, 2, 1, 4).reshape(9, F, 3 * G)
     bf = lambda *s: jax.ShapeDtypeStruct(s, jnp.bfloat16)
     return pl.pallas_call(
         weights_kernel,
-        out_shape=[bf(3, 256, 960), bf(192, 960), bf(3, 256, 960), bf(192, 960), bf(3, F * H, 3 * 384)],
+        out_shape=[bf(3, 960, 256), bf(960, 192), bf(3, 960, 256), bf(960, 192), bf(3 * KT, F * H)],
         scratch_shapes=[pltpu.VMEM((3, F * H, 128), jnp.float32)],
         compiler_params=pltpu.CompilerParams(vmem_limit_bytes=32 * 2**20),
         cost_estimate=pl.CostEstimate(flops=10_000_000, bytes_accessed=10_000_000, transcendentals=0),
         name="pack_weights",
-    )(w1.reshape(9, C, C), w2.reshape(9, C, C), aw)
+    )(w1.reshape(9, C, C), w2.reshape(9, C, C), aw, order)
 
 FULL, PAIR = 480, 320
 LP = 2 * 272 + REM
@@ -252,33 +261,51 @@
             for n in range(3):
                 v_ref[u, n, pl.ds(row, 8), :] = x[:, n * 128:n * 128 + 128]
         return c
-    lax.fori_loop(0, 33, tile, 0, unroll=3)
-
-def agg_kernel(k_ref, l_ref, r_ref, b_ref, out_ref, lf_ref, rf_ref, v_ref, vs_ref):
+    lax.fori_loop(0, 33, tile, 0, unroll=33)
+
+def agg_kernel(k_ref, l_ref, r_ref, b_ref, out_ref, lf_ref, rf_ref, v_ref, vs0, vs1, vs2):
     k = k_ref[0]
     for n in range(20):
         lf_ref[n] = l_ref[:, n * 128:n * 128 + 128].astype(jnp.float32)
-        rf_ref[n, 0:MR, :] = r_ref[:, n * 128:n * 128 + 128].astype(jnp.float32)
-    def pair(p, c):
+        rf_ref[n, 0:288, :] = r_ref[:, n * 128:n * 128 + 128].astype(jnp.float32)
+    wide = lax.broadcasted_iota(jnp.int32, (WL, 128), 1)
+    def pair(p, dst):
         corr2(lf_ref, rf_ref, v_ref, p)
         for u in range(2):
-            t = 2 * p + u
-            d = 24 * k - 1 + t
-            ok = jnp.logical_and(d >= 0, d < D)
-            m = jnp.where(ok, 1.0, 0.0).astype(jnp.float32)
-            for e in range(3):
-                for n in range(3):
-                    vs_ref[t, :, e * 384 + n * 128:e * 384 + n * 128 + 128] = (v_ref[u, n, e:e + WL, :] * m).astype(jnp.bfloat16)
-        return c
-    lax.fori_loop(0, NT // 2, pair, 0)
-    def out(d, c):
-        y = dot_nt(vs_ref[d], b_ref[0])
-        y += dot_nt(vs_ref[d + 1], b_ref[1])
-        y += dot_nt(vs_ref[d + 2], b_ref[2])
-        y = jnp.maximum(y, 0.0).T.reshape(F, H, WL)
-        out_ref[:, d] = y.astype(jnp.bfloat16)
-        return c
-    lax.fori_loop(0, BD, out, 0)
+            def put(i, x, u=u):
+                dst[:, u * KT + i * 128:u * KT + i * 128 + 128] = x.astype(jnp.bfloat16)
+            for n in range(2):
+                for e in range(3):
+                    put(n * 3 + e, v_ref[u, n, e:e + WL, :])
+            put(6, jnp.where(wide < 64, v_ref[u, 2, 0:WL, :], pltpu.roll(v_ref[u, 2, 1:1 + WL, :], 64, 1)))
+            put(7, v_ref[u, 2, 2:2 + WL, :])
+    def out(q, lo, hi):
+        for u in range(2):
+            if u == 0:
+                y = jnp.dot(lo[...], b_ref[0:2 * KT], preferred_element_type=jnp.float32)
+                y += jnp.dot(hi[:, 0:KT], b_ref[2 * KT:], preferred_element_type=jnp.float32)
+            else:
+                y = jnp.dot(lo[:, KT:], b_ref[0:KT], preferred_element_type=jnp.float32)
+                y += jnp.dot(hi[...], b_ref[KT:], preferred_element_type=jnp.float32)
+            y = jnp.maximum(y, 0.0).T.reshape(F, H, WL)
+            out_ref[:, jnp.maximum(2 * q + u, 0)] = y.astype(jnp.bfloat16)
+    bufs = (vs0, vs1, vs2)
+    pair(0, vs0)
+    @pl.when(k == 0)
+    def _():
+        vs0[:, 0:KT] = jnp.zeros((WL, KT), jnp.bfloat16)
+    def three(i, c):
+        for r in range(3):
+            p = 1 + 3 * i + r
+            new, lo, hi = bufs[(1 + r) % 3], bufs[(2 + r) % 3], bufs[r]
+            out(p - 2, lo, hi)
+            pair(p, new)
+        return c
+    lax.fori_loop(0, 4, three, 0)
+    @pl.when(k == 7)
+    def _():
+        vs0[:, KT:] = jnp.zeros((WL, KT), jnp.bfloat16)
+    out(11, vs2, vs0)
 
 def agg_call(k, lx, rx, b):
     return pl.pallas_call(
@@ -287,7 +314,7 @@
         in_specs=[pl.BlockSpec(memory_space=pltpu.SMEM)] + [pl.BlockSpec(memory_space=pltpu.VMEM)] * 3,
         out_specs=pl.BlockSpec(memory_space=pltpu.VMEM),
         scratch_shapes=[pltpu.VMEM((20, LR, 128), jnp.float32), pltpu.VMEM((20, RR, 128), jnp.float32),
-                        pltpu.VMEM((2, 3, LR, 128), jnp.float32), pltpu.VMEM((NT, WL, KT), jnp.bfloat16)],
+                        pltpu.VMEM((2, 3, LR, 128), jnp.float32), *[pltpu.VMEM((WL, 2 * KT), jnp.bfloat16)] * 3],
         compiler_params=pltpu.CompilerParams(vmem_limit_bytes=56 * 2**20),
         name="correlate_aggregate",
     )(k, lx, rx, b)
@@ -306,8 +333,9 @@
 def shards(left_view, right_view, first_weight, second_weight, agg_weight):
     k = lax.axis_index("band").astype(jnp.int32)
     base = lax.axis_index("col").astype(jnp.int32) * WL
-    left = left_view[:, 0].T
-    right = right_view[:, 0].T
+    order = order_matrix()
+    left = dot_on(left_view[:, 0], 0, order, 0).astype(jnp.bfloat16)
+    right = dot_on(right_view[:, 0], 0, order, 0).astype(jnp.bfloat16)
     before = from_col(jnp.concatenate([left[WL - 16:], right[WL - 208:]], axis=0), 1)
     after = from_col(jnp.concatenate([left[:16], right[:16]], axis=0), -1)
     full, up, down, far = small_call(pack_kernel, k[None], (left, right, before, after), (WHOLE, EXACT, EXACT, TWO), (288, FULL), "pack_rows")
@@ -315,8 +343,7 @@
     above, below, twice = to_band(up, 1, 0), to_band(down, 3, 0), to_band(far, 2, 0)
     up, down = small_call(relay_kernel, k[None], (across,), (EXACT, EXACT), (FULL,), "relay_rows")
     rows = [full, across, above, below, twice, to_band(up, 1, 0), to_band(down, 3, 0), to_band(twice, 0, 1)]
-    *weights, taps = weights_call(first_weight, second_weight, agg_weight)
-    weights = (*weights, order_matrix())
+    *weights, taps = weights_call(first_weight, second_weight, agg_weight, order)
     lf = conv_call(ML, 0, jnp.stack([k, base - 3]), rows, weights)
     rf = conv_call(MR, LP, jnp.stack([k, base - BD * k - 27]), rows, weights)
     return agg_call(k[None], lf, rf, taps)

time: 145 us -> 115 us (0.79)
  Pallas kernels: 103 us -> 69.6 us
  matrix products: 0 us -> 2.54 us
  waiting for transfers between devices: 12.7 us -> 11 us
    pallas_call x2, Pallas kernels: 56.1 us -> 37.6 us  [conv_call(): pl.pallas_call(functools.partial(conv_kernel, m, at), out_shape=jax.Shape...]
    pallas_call x1, Pallas kernels: 42.5 us -> 26.1 us  [agg_call(): pl.pallas_call(agg_kernel, out_shape=jax.ShapeDtypeStruct((F, BD, H, WL),...]
    dot_general x0 -> x2, matrix products: none -> 2.54 us  [dot_on(): lax.dot_general(x, y, (((i,), (j,)), ((), ())), preferred_element_type=jn...]
    pallas_call x1, Pallas kernels: 1.88 us -> 3.92 us  [weights_call(): pl.pallas_call(weights_kernel, out_shape=[bf(3, 960, 256), bf(960, 192),...]
    ppermute x7, waiting for transfers between devices: 11.2 us -> 9.49 us  [to_band(): return lax.ppermute(x, 'band', [(i, (i + 2 * z) % n ^ y) for i in range(n)])]
    unnamed x20 -> x22, local copies, waits for them, and re-layouts: 8.95 us -> 7.52 us
  transfers between devices with their start and end apart: 9 -> 9, of which waited for: 3 -> 2; matrix products, arithmetic and copies ran while one was open for 1% -> 3% of each run, Pallas kernels for 2% -> 4%
where the time goes in v3:
time: 115 us; the launch traced here: 114 us
  Pallas kernels  69.6 us (61%)
  starting transfers between devices  18.8 us (16%)
  waiting for transfers between devices  11 us (10%)
  local copies, waits for them, and re-layouts  10.8 us (9%)
  matrix products  2.54 us (2%)
    pallas_call x2, Pallas kernels, conv_call(): pl.pallas_call(functools.partial(conv_kernel, m, at), out_shape=jax.Shape...  37.6 us
    pallas_call x1, Pallas kernels, agg_call(): pl.pallas_call(agg_kernel, out_shape=jax.ShapeDtypeStruct((F, BD, H, WL),...  26.1 us
    ppermute x7, starting transfers between devices, to_band(): return lax.ppermute(x, 'band', [(i, (i + 2 * z) % n ^ y) for i in range(n)])  13.1 us
    ppermute x7, waiting for transfers between devices, to_band(): return lax.ppermute(x, 'band', [(i, (i + 2 * z) % n ^ y) for i in range(n)])  9.49 us
    unnamed x22, local copies, waits for them, and re-layouts  7.52 us
    ppermute x2, starting transfers between devices, from_col(): lax.ppermute(x, 'col', [(i, i + by) for i in range(n) if 0 <= i + by < n])  5.69 us
    pallas_call x1, Pallas kernels, weights_call(): pl.pallas_call(weights_kernel, out_shape=[bf(3, 960, 256), bf(960, 192),...  3.92 us
    dot_general x2, matrix products, dot_on(): lax.dot_general(x, y, (((i,), (j,)), ((), ())), preferred_element_type=jn...  2.54 us
  transfers between devices with their start and end apart: 9, of which 2 were waited for; matrix products, arithmetic and copies ran while one was open for 3% of the time, Pallas kernels for 4%

profile of v3, /device:TPU:20, one launch (start us, length us, event | category | flops | bytes accessed | tf_op | source)
XLA Modules:
  0.0 113.7 jit_solution(8602576718226151365)
XLA Ops:
  0.0 0.0 copy-start
  0.0 0.9 copy-done
  0.9 1.2 %convolution_convert_fusion.1 = bf16[320,256]{1,0:T(8,128)(2,1)S(1)} fusion(bf16[320,320]{1,0:T(8,128)(2,1)} %constant.21.clone.order, bf16[320,1,256]{2,0,1:T(8,128)(2,1)S(1)} %copy-done), kind=kOutput, calls=%fused_computation.1 | convolution fusion | flops 52510720 | bytes 532480 | tf_op jit(solution)/shard_map/dot_general | solution.py:24
  2.1 0.2 copy.13
  2.3 1.3 %convolution_convert_fusion = bf16[320,256]{1,0:T(8,128)(2,1)S(1)} fusion(bf16[320,320]{1,0:T(8,128)(2,1)} %constant.21.clone.order, bf16[320,1,256]{2,0,1:T(8,128)(2,1)} %param.7), kind=kOutput, calls=%fused_computation | convolution fusion | flops 52510720 | bytes 532480 | tf_op jit(solution)/shard_map/dot_general | solution.py:24
  3.7 0.0 copy-start.1
  3.7 0.0 copy-start.5
  3.7 0.2 copy.14
  3.9 2.1 %collective-permute-start = (bf16[224,320]{1,0:T(8,128)(2,1)S(1)}, bf16[224,320]{1,0:T(8,128)(2,1)S(1)}, u32[]{:S(2)}, u32[]{:S(2)}) collective-permute-start(bf16[224,320]{1,0:T(8,128)(2,1)S(1)} %pad_maximum_fusion), channel_id=1, source_target_pairs={{0,8},{8,16},{16,24},{24,32},{32,40},{40,48},{48,56},{56,64},{64,7... | collective-permute-start | bytes 430088 | tf_op jit(solution)/shard_map/ppermute | solution.py:325
  6.0 3.6 %collective-permute-start.1 = (bf16[32,320]{1,0:T(8,128)(2,1)S(1)}, bf16[32,320]{1,0:T(8,128)(2,1)S(1)}, u32[]{:S(2)}, u32[]{:S(2)}) collective-permute-start(bf16[32,320]{1,0:T(8,128)(2,1)S(1)} %pad_maximum_fusion.1), channel_id=1, source_target_pairs={{8,0},{16,8},{24,16},{32,24},{40,32},{48,40},{56,48},{64,56},{72,6... | collective-permute-start | bytes 61448 | tf_op jit(solution)/shard_map/ppermute | solution.py:325
  9.6 1.5 %collective-permute-done.1.after = bf16[32,320]{1,0:T(8,128)(2,1)S(1)} collective-permute-done((bf16[32,320]{1,0:T(8,128)(2,1)S(1)}, bf16[32,320]{1,0:T(8,128)(2,1)S(1)}, u32[]{:S(2)}, u32[]{:S(2)}) %collective-permute-start.1) | collective-permute-done | bytes 20512 | tf_op jit(solution)/shard_map/ppermute | solution.py:325
  11.1 0.0 collective-permute-done.before
  11.1 1.1 pack_rows.1
  12.2 0.0 copy-start.10
  12.2 1.3 %collective-permute-start.2 = (bf16[1888,128]{1,0:T(8,128)(2,1)S(1)}, bf16[1888,128]{1,0:T(8,128)(2,1)S(1)}, u32[]{:S(2)}, u32[]{:S(2)}) collective-permute-start(bf16[1888,128]{1,0:T(8,128)(2,1)S(1)} %get-tuple-element.16.refs_0_), channel_id=1, source_target_pairs={{0,1},{1,0},{2,3},{3,2},{4,5},{5,4},{6,7},{7,6},{8,9},{9,8},{10,11... | collective-permute-start | bytes 1449992 | tf_op jit(solution)/shard_map/ppermute | solution.py:330
  13.5 3.9 %collective-permute-start.5 = (bf16[1488,128]{1,0:T(8,128)(2,1)S(1)}, bf16[1488,128]{1,0:T(8,128)(2,1)}, u32[]{:S(2)}, u32[]{:S(2)}) collective-permute-start(bf16[1488,128]{1,0:T(8,128)(2,1)S(1)} %get-tuple-element.19), channel_id=1, source_target_pairs={{0,4},{1,5},{2,6},{3,7},{4,0},{5,1},{6,2},{7,3},{8,12},{9,13},{10,... | collective-permute-start | bytes 1142792 | tf_op jit(solution)/shard_map/ppermute | solution.py:330
  17.4 9.5 %collective-permute-done.5.refs_4_ = bf16[1488,128]{1,0:T(8,128)(2,1)} collective-permute-done((bf16[1488,128]{1,0:T(8,128)(2,1)S(1)}, bf16[1488,128]{1,0:T(8,128)(2,1)}, u32[]{:S(2)}, u32[]{:S(2)}) %collective-permute-start.5) | collective-permute-done | bytes 380960 | tf_op jit(solution)/shard_map/ppermute | solution.py:330
  26.9 0.7 collective-permute-start.8
  27.6 1.9 %collective-permute-start.3 = (bf16[1408,128]{1,0:T(8,128)(2,1)}, bf16[1408,128]{1,0:T(8,128)(2,1)}, u32[]{:S(2)}, u32[]{:S(2)}) collective-permute-start(bf16[1408,128]{1,0:T(8,128)(2,1)} %get-tuple-element.17), channel_id=1, source_target_pairs={{0,2},{1,3},{2,4},{3,5},{4,6},{5,7},{6,0},{7,1},{8,10},{9,11},{10,... | collective-permute-start | bytes 1081352 | tf_op jit(solution)/shard_map/ppermute | solution.py:330
  29.5 2.1 %collective-permute-start.4 = (bf16[1408,128]{1,0:T(8,128)(2,1)}, bf16[1408,128]{1,0:T(8,128)(2,1)}, u32[]{:S(2)}, u32[]{:S(2)}) collective-permute-start(bf16[1408,128]{1,0:T(8,128)(2,1)} %get-tuple-element.18), channel_id=1, source_target_pairs={{0,6},{1,7},{2,0},{3,1},{4,2},{5,3},{6,4},{7,5},{8,14},{9,15},{10,... | collective-permute-start | bytes 1081352 | tf_op jit(solution)/shard_map/ppermute | solution.py:330
  31.6 0.0 collective-permute-done.2.got.refs_1_
  31.6 0.0 copy-done.10
  31.6 0.0 copy-start.4
  31.6 0.9 relay_rows.1
  32.5 0.0 collective-permute-start.6
  32.5 3.2 %collective-permute-start.7 = (bf16[1408,128]{1,0:T(8,128)(2,1)S(1)}, bf16[1408,128]{1,0:T(8,128)(2,1)}, u32[]{:S(2)}, u32[]{:S(2)}) collective-permute-start(bf16[1408,128]{1,0:T(8,128)(2,1)S(1)} %get-tuple-element.21), channel_id=1, source_target_pairs={{0,6},{1,7},{2,0},{3,1},{4,2},{5,3},{6,4},{7,5},{8,14},{9,15},{10,... | collective-permute-start | bytes 1081352 | tf_op jit(solution)/shard_map/ppermute | solution.py:330
  35.8 1.8 %copy.15 = bf16[3,3,32,3,40]{4,3,2,1,0:T(4,128)(2,1)} copy(bf16[3,3,32,3,40]{4,2,1,3,0:T(8,128)(2,1)} %bitcast.23) | data formatting | bytes 138240 | tf_op jit(solution)/shard_map/transpose | solution.py:175
  37.6 1.1 %reshape.11.aw = bf16[9,32,120]{2,1,0:T(8,128)(2,1)S(1)} reshape(bf16[3,3,32,3,40]{4,3,2,1,0:T(4,128)(2,1)} %copy.15) | data formatting | bytes 138240 | tf_op jit(solution)/shard_map/reshape | solution.py:175
  38.7 0.0 copy-done.1
  38.7 0.0 copy-done.5
  38.7 0.0 copy-start.2
  38.8 1.6 %copy-done.2 = bf16[3,3,320,320]{3,2,1,0:T(8,128)(2,1)S(1)} copy-done((bf16[3,3,320,320]{3,2,1,0:T(8,128)(2,1)S(1)}, bf16[3,3,320,320]{3,2,1,0:T(8,128)(2,1)}, u32[]{:S(2)}) %copy-start.2) | copy-done | bytes 1843224
  40.4 3.9 %pack_weights.1 = (bf16[3,960,256]{2,1,0:T(8,128)(2,1)S(1)}, bf16[960,192]{1,0:T(8,128)(2,1)S(1)}, bf16[3,960,256]{2,1,0:T(8,128)(2,1)S(1)}, bf16[960,192]{1,0:T(8,128)(2,1)S(1)}, bf16[3072,256]{1,0:T(8,128)(2,1)S(1)}) custom-call(bf16[9,320,320]{2,1,0:T(8,128)(2,1)S(1)} %bitcast.16, bf16[9,320,320]{2,1,0:T(8,128)(2,1)S(1)} %bitcast.17, ...), custom_call_target="tpu_custom_call" | custom-call | flops 10000000 | bytes 10000000 | tf_op jit(solution)/shard_map/pack_weights/pallas_call | solution.py:177
  44.3 0.0 copy-done.4
  44.3 0.0 copy-start.3
  44.3 1.1 %copy-done.3 = bf16[3072,256]{1,0:T(8,128)(2,1)} copy-done((bf16[3072,256]{1,0:T(8,128)(2,1)}, bf16[3072,256]{1,0:T(8,128)(2,1)S(1)}, u32[]{:S(2)}) %copy-start.3) | copy-done | bytes 1572888
  45.5 0.0 copy-start.6
  45.5 1.1 copy-done.6
  46.6 0.0 copy-start.7
  46.6 1.1 copy-done.7
  47.7 0.0 copy-start.8
  47.7 0.8 copy-done.8
  48.5 0.0 copy-start.9
  48.5 0.8 copy-done.9
  49.3 0.7 pad_add_fusion
  49.9 0.0 collective-permute-done.3.refs_2_
  49.9 0.0 collective-permute-done.4.refs_3_
  50.0 0.0 collective-permute-done.8.refs_7_
  50.0 0.0 collective-permute-done.6.refs_5_
  50.0 0.0 collective-permute-done.7.refs_6_
  50.0 18.4 %feature_block.2.l_ref = bf16[272,2560]{1,0:T(8,128)(2,1)} custom-call(s32[2]{0:T(128)} %get-tuple-element.29.s_ref, bf16[1888,128]{1,0:T(8,128)(2,1)} %copy-done.10, bf16[1888,128]{1,0:T(8,128)(2,1)} %copy-done.4, bf16[1408,128]{1,0:T(8,128)(2,1)} %collective-permute-done.3.refs_2_, bf16[1408,128]{1,0:T(8,128)(2,1)} %collective-permute-done.4.refs_3_, ...), custom_call_target="tpu_custom_call" | custom-call | flops 16043212800 | bytes 6000000 | tf_op jit(solution)/shard_map/feature_block/pallas_call | solution.py:125
  68.4 19.2 %feature_block.3.r_ref = bf16[288,2560]{1,0:T(8,128)(2,1)} custom-call(s32[2]{0:T(128)} %get-tuple-element.30.s_ref, bf16[1888,128]{1,0:T(8,128)(2,1)} %copy-done.10, bf16[1888,128]{1,0:T(8,128)(2,1)} %copy-done.4, bf16[1408,128]{1,0:T(8,128)(2,1)} %collective-permute-done.3.refs_2_, bf16[1408,128]{1,0:T(8,128)(2,1)} %collective-permute-done.4.refs_3_, ...), custom_call_target="tpu_custom_call" | custom-call | flops 16986931200 | bytes 6000000 | tf_op jit(solution)/shard_map/feature_block/pallas_call | solution.py:125
  87.5 26.1 %correlate_aggregate.1 = bf16[32,24,8,256]{3,2,1,0:T(8,128)(2,1)} custom-call(s32[1]{0:T(128)} %bitcast.k_ref, bf16[272,2560]{1,0:T(8,128)(2,1)} %feature_block.2.l_ref, bf16[288,2560]{1,0:T(8,128)(2,1)} %feature_block.3.r_ref, bf16[3072,256]{1,0:T(8,128)(2,1)} %copy-done.3), custom_call_target="tpu_custom_call" | custom-call | tf_op jit(solution)/shard_map/correlate_aggregate/pallas_call | solution.py:311
  (5 shorter events, 0.1 us)
Async XLA Ops:
  0.0 0.9 copy-start
  3.7 35.1 %copy-start.1 = (bf16[3,3,320,320]{3,2,1,0:T(8,128)(2,1)S(1)}, bf16[3,3,320,320]{3,2,1,0:T(8,128)(2,1)}, u32[]{:S(2)}) copy-start(bf16[3,3,320,320]{3,2,1,0:T(8,128)(2,1)} %param.8) | copy-start | bytes 5529604
  3.7 35.1 %copy-start.5 = (bf16[320,320]{1,0:T(8,128)(2,1)S(1)}, bf16[320,320]{1,0:T(8,128)(2,1)}, u32[]{:S(2)}) copy-start(bf16[320,320]{1,0:T(8,128)(2,1)} %constant.21.clone.order) | copy-start | bytes 614404
  3.9 7.2 %collective-permute-start = (bf16[224,320]{1,0:T(8,128)(2,1)S(1)}, bf16[224,320]{1,0:T(8,128)(2,1)S(1)}, u32[]{:S(2)}, u32[]{:S(2)}) collective-permute-start(bf16[224,320]{1,0:T(8,128)(2,1)S(1)} %pad_maximum_fusion), channel_id=1, source_target_pairs={{0,8},{8,16},{16,24},{24,32},{32,40},{40,48},{48,56},{56,64},{64,7... | collective-permute-start | bytes 430088 | tf_op jit(solution)/shard_map/ppermute | solution.py:325
  6.0 5.1 %collective-permute-start.1 = (bf16[32,320]{1,0:T(8,128)(2,1)S(1)}, bf16[32,320]{1,0:T(8,128)(2,1)S(1)}, u32[]{:S(2)}, u32[]{:S(2)}) collective-permute-start(bf16[32,320]{1,0:T(8,128)(2,1)S(1)} %pad_maximum_fusion.1), channel_id=1, source_target_pairs={{8,0},{16,8},{24,16},{32,24},{40,32},{48,40},{56,48},{64,56},{72,6... | collective-permute-start | bytes 61448 | tf_op jit(solution)/shard_map/ppermute | solution.py:325
  12.2 19.4 %copy-start.10 = (bf16[1888,128]{1,0:T(8,128)(2,1)}, bf16[1888,128]{1,0:T(8,128)(2,1)S(1)}, u32[]{:S(2)}) copy-start(bf16[1888,128]{1,0:T(8,128)(2,1)S(1)} %get-tuple-element.16.refs_0_) | copy-start | bytes 1449988
  12.2 19.4 %collective-permute-start.2 = (bf16[1888,128]{1,0:T(8,128)(2,1)S(1)}, bf16[1888,128]{1,0:T(8,128)(2,1)S(1)}, u32[]{:S(2)}, u32[]{:S(2)}) collective-permute-start(bf16[1888,128]{1,0:T(8,128)(2,1)S(1)} %get-tuple-element.16.refs_0_), channel_id=1, source_target_pairs={{0,1},{1,0},{2,3},{3,2},{4,5},{5,4},{6,7},{7,6},{8,9},{9,8},{10,11... | collective-permute-start | bytes 1449992 | tf_op jit(solution)/shard_map/ppermute | solution.py:330
  13.5 13.4 %collective-permute-start.5 = (bf16[1488,128]{1,0:T(8,128)(2,1)S(1)}, bf16[1488,128]{1,0:T(8,128)(2,1)}, u32[]{:S(2)}, u32[]{:S(2)}) collective-permute-start(bf16[1488,128]{1,0:T(8,128)(2,1)S(1)} %get-tuple-element.19), channel_id=1, source_target_pairs={{0,4},{1,5},{2,6},{3,7},{4,0},{5,1},{6,2},{7,3},{8,12},{9,13},{10,... | collective-permute-start | bytes 1142792 | tf_op jit(solution)/shard_map/ppermute | solution.py:330
  26.9 23.1 %collective-permute-start.8 = (bf16[1488,128]{1,0:T(8,128)(2,1)}, bf16[1488,128]{1,0:T(8,128)(2,1)}, u32[]{:S(2)}, u32[]{:S(2)}) collective-permute-start(bf16[1488,128]{1,0:T(8,128)(2,1)} %collective-permute-done.5.refs_4_), channel_id=1, source_target_pairs={{0,1},{1,0},{2,3},{3,2},{4,5},{5,4},{6,7},{7,6},{8,9},{9,8},{10,11... | collective-permute-start | bytes 1142792 | tf_op jit(solution)/shard_map/ppermute | solution.py:330
  27.6 22.3 %collective-permute-start.3 = (bf16[1408,128]{1,0:T(8,128)(2,1)}, bf16[1408,128]{1,0:T(8,128)(2,1)}, u32[]{:S(2)}, u32[]{:S(2)}) collective-permute-start(bf16[1408,128]{1,0:T(8,128)(2,1)} %get-tuple-element.17), channel_id=1, source_target_pairs={{0,2},{1,3},{2,4},{3,5},{4,6},{5,7},{6,0},{7,1},{8,10},{9,11},{10,... | collective-permute-start | bytes 1081352 | tf_op jit(solution)/shard_map/ppermute | solution.py:330
  29.5 20.5 %collective-permute-start.4 = (bf16[1408,128]{1,0:T(8,128)(2,1)}, bf16[1408,128]{1,0:T(8,128)(2,1)}, u32[]{:S(2)}, u32[]{:S(2)}) collective-permute-start(bf16[1408,128]{1,0:T(8,128)(2,1)} %get-tuple-element.18), channel_id=1, source_target_pairs={{0,6},{1,7},{2,0},{3,1},{4,2},{5,3},{6,4},{7,5},{8,14},{9,15},{10,... | collective-permute-start | bytes 1081352 | tf_op jit(solution)/shard_map/ppermute | solution.py:330
  31.6 12.7 %copy-start.4 = (bf16[1888,128]{1,0:T(8,128)(2,1)}, bf16[1888,128]{1,0:T(8,128)(2,1)S(1)}, u32[]{:S(2)}) copy-start(bf16[1888,128]{1,0:T(8,128)(2,1)S(1)} %collective-permute-done.2.got.refs_1_) | copy-start | bytes 1449988
  32.5 17.4 %collective-permute-start.6 = (bf16[1408,128]{1,0:T(8,128)(2,1)}, bf16[1408,128]{1,0:T(8,128)(2,1)}, u32[]{:S(2)}, u32[]{:S(2)}) collective-permute-start(bf16[1408,128]{1,0:T(8,128)(2,1)} %get-tuple-element.20), channel_id=1, source_target_pairs={{0,2},{1,3},{2,4},{3,5},{4,6},{5,7},{6,0},{7,1},{8,10},{9,11},{10,... | collective-permute-start | bytes 1081352 | tf_op jit(solution)/shard_map/ppermute | solution.py:330
  32.5 17.4 %collective-permute-start.7 = (bf16[1408,128]{1,0:T(8,128)(2,1)S(1)}, bf16[1408,128]{1,0:T(8,128)(2,1)}, u32[]{:S(2)}, u32[]{:S(2)}) collective-permute-start(bf16[1408,128]{1,0:T(8,128)(2,1)S(1)} %get-tuple-element.21), channel_id=1, source_target_pairs={{0,6},{1,7},{2,0},{3,1},{4,2},{5,3},{6,4},{7,5},{8,14},{9,15},{10,... | collective-permute-start | bytes 1081352 | tf_op jit(solution)/shard_map/ppermute | solution.py:330
  38.7 1.6 %copy-start.2 = (bf16[3,3,320,320]{3,2,1,0:T(8,128)(2,1)S(1)}, bf16[3,3,320,320]{3,2,1,0:T(8,128)(2,1)}, u32[]{:S(2)}) copy-start(bf16[3,3,320,320]{3,2,1,0:T(8,128)(2,1)} %param.9) | copy-start | bytes 5529604
  44.3 1.2 %copy-start.3 = (bf16[3072,256]{1,0:T(8,128)(2,1)}, bf16[3072,256]{1,0:T(8,128)(2,1)S(1)}, u32[]{:S(2)}) copy-start(bf16[3072,256]{1,0:T(8,128)(2,1)S(1)} %get-tuple-element.26.b_ref) | copy-start | bytes 4718596
  45.5 1.1 copy-start.6
  46.6 1.1 copy-start.7
  47.7 0.8 copy-start.8
  48.5 0.8 copy-start.9

commit v4 on v3

v4 whole, which is shorter than its diff:
```python
import functools

import jax
import jax.numpy as jnp
import numpy as np
from jax import lax
from jax.experimental import pallas as pl
from jax.experimental.pallas import tpu as pltpu
from jax.sharding import PartitionSpec as P

G, J, D, F, H, WL, BD, C, W = 40, 8, 192, 32, 8, 256, 24, 320, 4096
CH = J * H * G
REM = 144
ML, MR = 272, 288
LR, RR = 272, 296
NT = BD + 2
KT = 1024
UN = 4


def dot(x, w):
    return jnp.dot(x, w, preferred_element_type=jnp.float32)


def dot_on(x, i, y, j):
    return lax.dot_general(x, y, (((i,), (j,)), ((), ())), preferred_element_type=jnp.float32)


def build(dst, slot, src, m):
    for n in range(2):
        for e in range(3):
            dst[slot, :, (n * 3 + e) * 128:(n * 3 + e + 1) * 128] = src(n, e).astype(jnp.bfloat16)
    lane = lax.broadcasted_iota(jnp.int32, (m, 128), 1)
    pair = jnp.where(lane < 64, src(2, 0), pltpu.roll(src(2, 1), 64, 1))
    dst[slot, :, 768:896] = pair.astype(jnp.bfloat16)
    dst[slot, :, 896:960] = src(2, 2)[:, :64].astype(jnp.bfloat16)


def feature_view(m, at, k, base, xin, wm1, wr1, wm2, wr2, target, raw, xs, hs, ts, z, feat, wide):
    y = k & 1
    if at:
        start = window_start(k)
        formats = [(FULL, start)] * 2 + [(288, 0)] * 2 + [(PAIR, 24 - 24 * y), (288, 0), (288, 0), (PAIR, 24 - 24 * y)]
    else:
        formats = [(m, 0)] * 8
    source = [k, k ^ 1, (k + 6) & 7, (k + 2) & 7, (k + 4) & 7, ((k + 6) & 7) ^ 1, ((k + 2) & 7) ^ 1, ((k + 4) & 7) ^ 1]
    for d in range(8):
        h, (size, start) = source[d], formats[d]
        rem = REM if size == m else size // 2
        if size == m:
            uncut(raw.at[h], xin[d], at, m, rem)
        else:
            uncut(wide, xin[d], at, size, rem)
            for n in range(3):
                raw[h, n, 0:m, :] = wide[n, pl.ds(start, m), :]
    xs, hs, z, feat = xs.at[:, 0:m], hs.at[:, 0:m], z.at[:, :, 0:m], feat.at[:, :, 0:m]
    col = base + lax.broadcasted_iota(jnp.int32, (m, 128), 0)

    def rest(x, wr, h):
        y = dot(x[h + 1], wr[...])
        z[h + 1, 0] = y[:, :128]
        z[h + 1, 1, :, 0:64] = y[:, 128:192]

    def conv(x, wm, h):
        y = dot(x[h], wm[0])
        y += dot(x[h + 1], wm[1])
        y += dot(x[h + 2], wm[2])
        return y[:, :128], y[:, 128:], z[h, 0] + pltpu.roll(z[h + 1, 0], 64, 1) + z[h + 2, 1]

    def load(h, c):
        build(xs, h + 1, lambda n, e: raw[h, n, e:e + m, :], m)
        rest(xs, wr1, h)
        return c
    lax.fori_loop(0, H, load, 0, unroll=UN)
    def first(i, c):
        for u in range(UN):
            first_row(UN * i + u, ts.at[u])
        return c
    def first_row(h, ts):
        ok = jnp.logical_and(col + 1 >= 0, col + 1 < W)
        for n, y in enumerate(conv(xs, wm1, h)):
            ts[n, 0:m, :] = jnp.where(ok, jnp.maximum(y, 0.0), 0.0)
        build(hs, h + 1, lambda n, e: ts[n, e:e + m, :], m)
    lax.fori_loop(0, H // UN, first, 0)
    def rest2(h, c):
        rest(hs, wr2, h)
        return c
    lax.fori_loop(0, H, rest2, 0, unroll=UN)
    def second(h, c):
        ok = jnp.logical_and(col + 2 >= 0, col + 2 < W)
        for n, y in enumerate(conv(hs, wm2, h)):
            y = jnp.where(ok, y + raw[h, n, 2:2 + m, :], 0.0)
            feat[h, n] = y.astype(jnp.bfloat16).astype(jnp.float32)
        return c
    lax.fori_loop(0, H, second, 0, unroll=UN)

    lane = lax.broadcasted_iota(jnp.int32, (16, 128), 1)
    def place(i, c):
        row = pl.multiple_of(i * 16, 16)
        for q in range(20):
            got = None
            for j in range(J):
                for h in range(H):
                    t0 = j * H * G + h * G
                    lo, hi = max(t0, q * 128), min(t0 + G, q * 128 + 128)
                    if lo >= hi:
                        continue
                    s_lo = lo - t0 + j * G
                    while lo < hi:
                        n = s_lo // 128
                        length = min(hi - lo, (n + 1) * 128 - s_lo)
                        x = feat[h, n, pl.ds(row, 16), :]
                        sh = (lo - s_lo) % 128
                        if sh:
                            x = pltpu.roll(x, sh, 1)
                        got = x if got is None else jnp.where(lane >= lo - q * 128, x, got)
                        lo, s_lo = lo + length, s_lo + length
            target[q, pl.ds(row, 16), :] = got
        return c
    lax.fori_loop(0, m // 16, place, 0, unroll=2)


def corr2(l_ref, r_ref, v_ref, p):
    def tile(i, c):
        row = pl.multiple_of(i * 8, 8)
        q = [[None] * 5 for _ in range(2)]
        for m in range(4):
            for n in range(5):
                lt = l_ref[m * 5 + n, pl.ds(row, 8), :]
                for u in range(2):
                    pr = lt * r_ref[m * 5 + n, pl.ds(row + (25 - u) - 2 * p, 8), :]
                    q[u][n] = pr if m == 0 else q[u][n] + pr
        for u in range(2):
            x = jnp.concatenate(q[u], axis=1)
            x = x + pltpu.roll(x, 320, 1)
            for n in range(3):
                v_ref[u, n, pl.ds(row, 8), :] = x[:, n * 128:n * 128 + 128]
        return c
    lax.fori_loop(0, 33, tile, 0, unroll=33)


def aggregate_views(k, b_ref, out_ref, lf_ref, rf_ref, v_ref, vs0, vs1, vs2):
    wide = lax.broadcasted_iota(jnp.int32, (WL, 128), 1)
    def pair(p, dst):
        corr2(lf_ref, rf_ref, v_ref, p)
        for u in range(2):
            def put(i, x, u=u):
                dst[:, u * KT + i * 128:u * KT + i * 128 + 128] = x.astype(jnp.bfloat16)
            for n in range(2):
                for e in range(3):
                    put(n * 3 + e, v_ref[u, n, e:e + WL, :])
            put(6, jnp.where(wide < 64, v_ref[u, 2, 0:WL, :], pltpu.roll(v_ref[u, 2, 1:1 + WL, :], 64, 1)))
            put(7, v_ref[u, 2, 2:2 + WL, :])
    def out(q, lo, hi):
        for u in range(2):
            if u == 0:
                y = jnp.dot(lo[...], b_ref[0:2 * KT], preferred_element_type=jnp.float32)
                y += jnp.dot(hi[:, 0:KT], b_ref[2 * KT:], preferred_element_type=jnp.float32)
            else:
                y = jnp.dot(lo[:, KT:], b_ref[0:KT], preferred_element_type=jnp.float32)
                y += jnp.dot(hi[...], b_ref[KT:], preferred_element_type=jnp.float32)
            y = jnp.maximum(y, 0.0).T.reshape(F, H, WL)
            out_ref[:, jnp.maximum(2 * q + u, 0)] = y.astype(jnp.bfloat16)
    bufs = (vs0, vs1, vs2)
    pair(0, vs0)
    @pl.when(k == 0)
    def _():
        vs0[:, 0:KT] = jnp.zeros((WL, KT), jnp.bfloat16)
    def three(i, c):
        for r in range(3):
            p = 1 + 3 * i + r
            new, lo, hi = bufs[(1 + r) % 3], bufs[(2 + r) % 3], bufs[r]
            out(p - 2, lo, hi)
            pair(p, new)
        return c
    lax.fori_loop(0, 4, three, 0)
    @pl.when(k == 7)
    def _():
        vs0[:, KT:] = jnp.zeros((WL, KT), jnp.bfloat16)
    out(11, vs2, vs0)


def order_matrix():
    to = np.arange(C)
    return jnp.asarray(np.arange(C)[:, None] == ((to % G) * J + to // G)[None, :], jnp.bfloat16)


def weights_kernel(w1, w2, aw, order, wm1, wr1, wm2, wr2, bt, tmp):
    lane = lax.broadcasted_iota(jnp.int32, (C, 128), 1)
    zero = jnp.zeros((C, 64), jnp.float32)
    for e in range(3):
        places = ((0, 128, e * 128), (128, 128, (3 + e) * 128), (256, 64, 768 + e * 64))
        for w, wm, wr, first in ((w1, wm1, wr1, True), (w2, wm2, wr2, False)):
            last = []
            for b in range(3):
                x = w[b * 3 + e]
                x = dot_on(order[...], 0, x, 1) if first else dot_on(x, 0, order[...], 0)
                for at, n, to in places:
                    wm[b, to:to + n, :] = x[at:at + n, :256].astype(jnp.bfloat16)
                last.append(jnp.concatenate([x[:, 256:320], zero], axis=1))
            pair = jnp.where(lane < 64, last[0], pltpu.roll(last[1], 64, 1)).astype(jnp.bfloat16)
            for at, n, to in places:
                wr[to:to + n, 0:128] = pair[at:at + n]
                wr[to:to + n, 128:192] = last[2][at:at + n, :64].astype(jnp.bfloat16)
    wide = lax.broadcasted_iota(jnp.int32, (F, 384), 1)
    for a in range(3):
        for e in range(3):
            x = [aw[(a * 3 + b) * 3 + e].astype(jnp.float32) for b in range(3)]
            x = jnp.concatenate(x + [jnp.zeros((F, 264), jnp.float32)], axis=1) * 0.125
            for ho in range(H):
                y = x if ho == 1 else pltpu.roll(x, ((ho - 1) * G) % 384, 1)
                y = jnp.where(wide < H * G, y, 0.0)
                for n in range(3):
                    tmp[n, pl.ds(ho, F, stride=H), :] = y[:, n * 128:n * 128 + 128]
            for n in range(2):
                at = a * KT + (n * 3 + e) * 128
                bt[at:at + 128, :] = tmp[n].T.astype(jnp.bfloat16)
            at, n = a * KT + 768 + e * 64, 64 if e < 2 else 128
            bt[at:at + n, :] = tmp[2].T[:n].astype(jnp.bfloat16)


def weights_call(w1, w2, aw, order):
    aw = aw.transpose(0, 1, 3, 2, 4).reshape(27, F, G)
    bf = lambda *s: jax.ShapeDtypeStruct(s, jnp.bfloat16)
    return pl.pallas_call(
        weights_kernel,
        out_shape=[bf(3, 960, 256), bf(960, 192), bf(3, 960, 256), bf(960, 192), bf(3 * KT, F * H)],
        scratch_shapes=[pltpu.VMEM((3, F * H, 128), jnp.float32)],
        compiler_params=pltpu.CompilerParams(vmem_limit_bytes=56 * 2**20),
        cost_estimate=pl.CostEstimate(flops=10_000_000, bytes_accessed=10_000_000, transcendentals=0),
        name="pack_weights",
    )(w1.reshape(9, C, C), w2.reshape(9, C, C), aw, order)

FULL, PAIR = 480, 320
LP = 2 * 272 + REM


def cut(dst, at, src, start, m, rem):
    for n in range(2):
        dst[at + n * m:at + n * m + m, :] = src[n, pl.ds(start, m), :].astype(jnp.bfloat16)
    lane = lax.broadcasted_iota(jnp.int32, (rem, 128), 1)
    pair = jnp.where(lane < 64, src[2, pl.ds(start, rem), :], pltpu.roll(src[2, pl.ds(start + m - rem, rem), :], 64, 1))
    dst[at + 2 * m:at + 2 * m + rem, :] = pair.astype(jnp.bfloat16)


def uncut(dst, src, at, m, rem):
    for n in range(2):
        dst[n, 0:m, :] = src[at + n * m:at + n * m + m, :].astype(jnp.float32)
    x = src[at + 2 * m:at + 2 * m + rem, :].astype(jnp.float32)
    dst[2, 0:rem, :] = x
    dst[2, m - rem:m, :] = pltpu.roll(x, 64, 1)


def window_start(k):
    return 181 - BD * k


def pack_kernel(k_ref, lt, rt, before, after, full, up, down, far, lext, rext):
    k = k_ref[0]
    f32 = lambda x: x.astype(jnp.float32)
    for n in range(3):
        w = 128 if n < 2 else 64
        col = slice(n * 128, n * 128 + w)
        lext[n, 0:16, :w] = f32(before[0:16, col])
        lext[n, 16:272, :w] = f32(lt[:, col])
        lext[n, 272:288, :w] = f32(after[0:16, col])
        rext[n, 0:208, :w] = f32(before[16:224, col])
        rext[n, 208:464, :w] = f32(rt[:, col])
        rext[n, 464:480, :w] = f32(after[16:32, col])
    for dst in (full, up, down, far):
        cut(dst, 0, lext, 13, 272, REM)
    cut(full, LP, rext, 0, FULL, FULL // 2)
    cut(up, LP, rext, window_start((k + 2) & 7), 288, REM)
    cut(down, LP, rext, window_start((k + 6) & 7), 288, REM)
    cut(far, LP, rext, window_start(((k + 4) & 7) | 1), PAIR, PAIR // 2)


def relay_kernel(k_ref, got, up, down, rext):
    k = k_ref[0]
    uncut(rext, got, LP, FULL, FULL // 2)
    for dst, to in ((up, (k + 2) & 7), (down, (k + 6) & 7)):
        dst[0:LP, :] = got[0:LP, :]
        cut(dst, LP, rext, window_start(to), 288, REM)


def rows_of(n):
    return jax.ShapeDtypeStruct((n, 128), jnp.bfloat16)

EXACT, WHOLE, TWO = LP + 720, LP + 1200, LP + 800


def small_call(kernel, k, args, outs, scratch, name):
    return pl.pallas_call(
        kernel,
        out_shape=[rows_of(n) for n in outs],
        in_specs=[pl.BlockSpec(memory_space=pltpu.SMEM)] + [pl.BlockSpec(memory_space=pltpu.VMEM)] * len(args),
        scratch_shapes=[pltpu.VMEM((3, n, 128), jnp.float32) for n in scratch],
        compiler_params=pltpu.CompilerParams(vmem_limit_bytes=56 * 2**20),
        cost_estimate=pl.CostEstimate(flops=2_000_000, bytes_accessed=3_000_000, transcendentals=0),
        name=name,
    )(k, *args)


def main_kernel(s_ref, *refs):
    xin, (wm1, wr1, wm2, wr2, taps, out_ref), scratch = refs[:8], refs[8:14], refs[14:]
    conv_scratch, (lf, rf, *others) = scratch[:7], scratch[7:]
    k, base = s_ref[0], s_ref[1]
    raw, xs, hs, ts, z = conv_scratch[:5]
    for slot in (0, 9):
        xs[slot] = jnp.zeros((MR, 960), jnp.bfloat16)
        hs[slot] = jnp.zeros((MR, 960), jnp.bfloat16)
        z[slot] = jnp.zeros((2, MR, 128), jnp.float32)
    feature_view(ML, 0, k, base - 3, xin, wm1, wr1, wm2, wr2, lf, *conv_scratch)
    feature_view(MR, LP, k, base - BD * k - 27, xin, wm1, wr1, wm2, wr2, rf, *conv_scratch)
    aggregate_views(k, taps, out_ref, lf, rf, *others)


def main_call(scal, rows, weights, taps):
    f32 = lambda *s: pltpu.VMEM(s, jnp.float32)
    b16 = lambda *s: pltpu.VMEM(s, jnp.bfloat16)
    return pl.pallas_call(
        main_kernel,
        out_shape=jax.ShapeDtypeStruct((F, BD, H, WL), jnp.bfloat16),
        in_specs=[pl.BlockSpec(memory_space=pltpu.SMEM)] + [pl.BlockSpec(memory_space=pltpu.VMEM)] * 13,
        out_specs=pl.BlockSpec(memory_space=pltpu.VMEM),
        scratch_shapes=[f32(8, 3, MR + 8, 128), b16(10, MR, 960), b16(10, MR, 960), f32(UN, 3, MR + 8, 128), f32(10, 2, MR, 128),
                        f32(8, 3, MR, 128), f32(3, FULL, 128), f32(20, LR, 128), f32(20, RR, 128), f32(2, 3, LR, 128),
                        b16(WL, 2 * KT), b16(WL, 2 * KT), b16(WL, 2 * KT)],
        compiler_params=pltpu.CompilerParams(vmem_limit_bytes=60 * 2**20),
        name="features_volume_aggregate",
    )(scal, *rows, *weights, taps)


def from_col(x, by):
    n = lax.axis_size("col")
    return lax.ppermute(x, "col", [(i, i + by) for i in range(n) if 0 <= i + by < n])


def to_band(x, z, y):
    n = lax.axis_size("band")
    return lax.ppermute(x, "band", [(i, ((i + 2 * z) % n) ^ y) for i in range(n)])


def shards(left_view, right_view, first_weight, second_weight, agg_weight):
    k = lax.axis_index("band").astype(jnp.int32)
    base = lax.axis_index("col").astype(jnp.int32) * WL
    order = order_matrix()
    left = dot_on(left_view[:, 0], 0, order, 0).astype(jnp.bfloat16)
    right = dot_on(right_view[:, 0], 0, order, 0).astype(jnp.bfloat16)
    before = from_col(jnp.concatenate([left[WL - 16:], right[WL - 208:]], axis=0), 1)
    after = from_col(jnp.concatenate([left[:16], right[:16]], axis=0), -1)
    *weights, taps = weights_call(first_weight, second_weight, agg_weight, order)
    full, up, down, far = small_call(pack_kernel, k[None], (left, right, before, after), (WHOLE, EXACT, EXACT, TWO), (288, FULL), "pack_rows")
    across = to_band(full, 0, 1)
    above, below, twice = to_band(up, 1, 0), to_band(down, 3, 0), to_band(far, 2, 0)
    up, down = small_call(relay_kernel, k[None], (across,), (EXACT, EXACT), (FULL,), "relay_rows")
    rows = [full, across, above, below, twice, to_band(up, 1, 0), to_band(down, 3, 0), to_band(twice, 0, 1)]
    return main_call(jnp.stack([k, base]), rows, weights, taps)


def solution(mesh):
    return jax.shard_map(
        shards,
        mesh=mesh,
        in_specs=(P(None, "band", "col"), P(None, "band", "col"), P(), P(), P()),
        out_specs=P(None, "band", None, "col"),
        check_vma=False,
    )
```

time: 115 us -> 110 us (0.957); the launches traced: 114 us -> 110 us
  local copies, waits for them, and re-layouts: 10.8 us -> 3.61 us
  Pallas kernels: 69.6 us -> 72.2 us
  waiting for transfers between devices: 11 us -> 12.2 us
    pallas_call x1, Pallas kernels: 3.92 us -> 8.41 us  [weights_call(): pl.pallas_call(weights_kernel, out_shape=[bf(3, 960, 256), bf(960, 192),...]
    pallas_call x3 -> x1, Pallas kernels: 63.7 us -> 59.3 us  [main_call(): pl.pallas_call(main_kernel, out_shape=jax.ShapeDtypeStruct((F, BD, H, WL)...]
    unnamed x22 -> x24, local copies, waits for them, and re-layouts: 7.52 us -> 3.26 us
    pallas_call x2, Pallas kernels: 2.02 us -> 4.53 us  [small_call(): pl.pallas_call(kernel, out_shape=[rows_of(n) for n in outs], in_specs=[pl...]
    transpose x1 -> x0, local copies, waits for them, and re-layouts: 1.8 us -> none  [weights_call(): aw = aw.transpose(0, 3, 2, 1, 4).reshape(9, F, 3 * G)]
    ppermute x7, waiting for transfers between devices: 9.49 us -> 10.7 us  [to_band(): return lax.ppermute(x, 'band', [(i, (i + 2 * z) % n ^ y) for i in range(n)])]
  transfers between devices with their start and end apart: 9 -> 9, of which waited for: 2 -> 3; matrix products, arithmetic and copies ran while one was open for 3% -> 1% of each run, Pallas kernels for 4% -> 10%
where the time goes in v4:
time: 110 us
  Pallas kernels  72.2 us (66%)
  starting transfers between devices  18.7 us (17%)
  waiting for transfers between devices  12.2 us (11%)
  local copies, waits for them, and re-layouts  3.61 us (3%)
  matrix products  2.6 us (2%)
    pallas_call x1, Pallas kernels, main_call(): pl.pallas_call(main_kernel, out_shape=jax.ShapeDtypeStruct((F, BD, H, WL)...  59.3 us
    ppermute x7, starting transfers between devices, to_band(): return lax.ppermute(x, 'band', [(i, (i + 2 * z) % n ^ y) for i in range(n)])  13.1 us
    ppermute x7, waiting for transfers between devices, to_band(): return lax.ppermute(x, 'band', [(i, (i + 2 * z) % n ^ y) for i in range(n)])  10.7 us
    pallas_call x1, Pallas kernels, weights_call(): pl.pallas_call(weights_kernel, out_shape=[bf(3, 960, 256), bf(960, 192),...  8.41 us
    ppermute x2, starting transfers between devices, from_col(): lax.ppermute(x, 'col', [(i, i + by) for i in range(n) if 0 <= i + by < n])  5.56 us
    pallas_call x2, Pallas kernels, small_call(): pl.pallas_call(kernel, out_shape=[rows_of(n) for n in outs], in_specs=[pl...  4.53 us
    unnamed x24, local copies, waits for them, and re-layouts  3.26 us
    dot_general x2, matrix products, dot_on(): lax.dot_general(x, y, (((i,), (j,)), ((), ())), preferred_element_type=jn...  2.6 us
  transfers between devices with their start and end apart: 9, of which 3 were waited for; matrix products, arithmetic and copies ran while one was open for 1% of the time, Pallas kernels for 10%

profile of v4, /device:TPU:20, one launch (start us, length us, event | category | flops | bytes accessed | tf_op | source)
XLA Modules:
  0.0 110.2 jit_solution(4087889723825636241)
XLA Ops:
  0.0 0.0 copy-start
  0.0 0.9 copy-done
  0.9 1.2 %convolution_convert_fusion.1 = bf16[320,256]{1,0:T(8,128)(2,1)S(1)} fusion(bf16[320,320]{1,0:T(8,128)(2,1)} %constant.13.clone.order, bf16[320,1,256]{2,0,1:T(8,128)(2,1)S(1)} %copy-done), kind=kOutput, calls=%fused_computation.1 | convolution fusion | flops 52510720 | bytes 532480 | tf_op jit(solution)/shard_map/dot_general | solution.py:26
  2.1 0.2 copy.9
  2.3 0.0 copy-start.3
  2.3 1.4 %convolution_convert_fusion = bf16[320,256]{1,0:T(8,128)(2,1)S(1)} fusion(bf16[320,320]{1,0:T(8,128)(2,1)} %constant.13.clone.order, bf16[320,1,256]{2,0,1:T(8,128)(2,1)} %param.7), kind=kOutput, calls=%fused_computation | convolution fusion | flops 52510720 | bytes 532480 | tf_op jit(solution)/shard_map/dot_general | solution.py:26
  3.7 0.2 copy.10
  3.9 0.0 copy-start.2
  4.0 1.9 %collective-permute-start = (bf16[224,320]{1,0:T(8,128)(2,1)S(1)}, bf16[224,320]{1,0:T(8,128)(2,1)S(1)}, u32[]{:S(2)}, u32[]{:S(2)}) collective-permute-start(bf16[224,320]{1,0:T(8,128)(2,1)S(1)} %pad_maximum_fusion), channel_id=1, source_target_pairs={{0,8},{8,16},{16,24},{24,32},{32,40},{40,48},{48,56},{56,64},{64,7... | collective-permute-start | bytes 430088 | tf_op jit(solution)/shard_map/ppermute | solution.py:336
  5.9 3.6 %collective-permute-start.1 = (bf16[32,320]{1,0:T(8,128)(2,1)S(1)}, bf16[32,320]{1,0:T(8,128)(2,1)S(1)}, u32[]{:S(2)}, u32[]{:S(2)}) collective-permute-start(bf16[32,320]{1,0:T(8,128)(2,1)S(1)} %pad_maximum_fusion.1), channel_id=1, source_target_pairs={{8,0},{16,8},{24,16},{32,24},{40,32},{48,40},{56,48},{64,56},{72,6... | collective-permute-start | bytes 61448 | tf_op jit(solution)/shard_map/ppermute | solution.py:336
  9.6 1.5 %collective-permute-done.1.after = bf16[32,320]{1,0:T(8,128)(2,1)S(1)} collective-permute-done((bf16[32,320]{1,0:T(8,128)(2,1)S(1)}, bf16[32,320]{1,0:T(8,128)(2,1)S(1)}, u32[]{:S(2)}, u32[]{:S(2)}) %collective-permute-start.1) | collective-permute-done | bytes 20512 | tf_op jit(solution)/shard_map/ppermute | solution.py:336
  11.1 0.0 copy-start.11
  11.1 0.0 collective-permute-done.before
  11.1 0.0 copy-start.10
  11.1 0.0 copy-done.3
  11.1 0.0 copy-done.2
  11.1 0.6 copy-done.11
  11.7 0.1 copy-done.10
  11.7 2.4 %pack_rows.1 = (bf16[1888,128]{1,0:T(8,128)(2,1)}, bf16[1408,128]{1,0:T(8,128)(2,1)}, bf16[1408,128]{1,0:T(8,128)(2,1)}, bf16[1488,128]{1,0:T(8,128)(2,1)}) custom-call(s32[1]{0:T(128)} %bitcast.k_ref, bf16[256,320]{1,0:T(8,128)(2,1)} %bitcast.23, bf16[256,320]{1,0:T(8,128)(2,1)} %bitcast.21, bf16[224,320]{1,0:T(8,128)(2,1)} %copy-done.10, ...), custom_call_target="tpu_custom_call" | custom-call | flops 2000000 | bytes 3000000 | tf_op jit(solution)/shard_map/pack_rows/pallas_call | solution.py:293
  14.2 1.3 %collective-permute-start.2 = (bf16[1888,128]{1,0:T(8,128)(2,1)}, bf16[1888,128]{1,0:T(8,128)(2,1)S(1)}, u32[]{:S(2)}, u32[]{:S(2)}) collective-permute-start(bf16[1888,128]{1,0:T(8,128)(2,1)} %get-tuple-element.16.refs_0_), channel_id=1, source_target_pairs={{0,1},{1,0},{2,3},{3,2},{4,5},{5,4},{6,7},{7,6},{8,9},{9,8},{10,11... | collective-permute-start | bytes 1449992 | tf_op jit(solution)/shard_map/ppermute | solution.py:341
  15.4 3.9 %collective-permute-start.5 = (bf16[1488,128]{1,0:T(8,128)(2,1)}, bf16[1488,128]{1,0:T(8,128)(2,1)S(1)}, u32[]{:S(2)}, u32[]{:S(2)}) collective-permute-start(bf16[1488,128]{1,0:T(8,128)(2,1)} %get-tuple-element.19), channel_id=1, source_target_pairs={{0,4},{1,5},{2,6},{3,7},{4,0},{5,1},{6,2},{7,3},{8,12},{9,13},{10,... | collective-permute-start | bytes 1142792 | tf_op jit(solution)/shard_map/ppermute | solution.py:341
  19.3 9.6 %collective-permute-done.5.refs_4_ = bf16[1488,128]{1,0:T(8,128)(2,1)S(1)} collective-permute-done((bf16[1488,128]{1,0:T(8,128)(2,1)}, bf16[1488,128]{1,0:T(8,128)(2,1)S(1)}, u32[]{:S(2)}, u32[]{:S(2)}) %collective-permute-start.5) | collective-permute-done | bytes 380960 | tf_op jit(solution)/shard_map/ppermute | solution.py:341
  28.9 0.0 copy-start.4
  28.9 0.7 collective-permute-start.8
  29.7 1.8 %collective-permute-start.3 = (bf16[1408,128]{1,0:T(8,128)(2,1)}, bf16[1408,128]{1,0:T(8,128)(2,1)S(1)}, u32[]{:S(2)}, u32[]{:S(2)}) collective-permute-start(bf16[1408,128]{1,0:T(8,128)(2,1)} %get-tuple-element.17), channel_id=1, source_target_pairs={{0,2},{1,3},{2,4},{3,5},{4,6},{5,7},{6,0},{7,1},{8,10},{9,11},{10,... | collective-permute-start | bytes 1081352 | tf_op jit(solution)/shard_map/ppermute | solution.py:341
  31.5 2.1 %collective-permute-start.4 = (bf16[1408,128]{1,0:T(8,128)(2,1)}, bf16[1408,128]{1,0:T(8,128)(2,1)S(1)}, u32[]{:S(2)}, u32[]{:S(2)}) collective-permute-start(bf16[1408,128]{1,0:T(8,128)(2,1)} %get-tuple-element.18), channel_id=1, source_target_pairs={{0,6},{1,7},{2,0},{3,1},{4,2},{5,3},{6,4},{7,5},{8,14},{9,15},{10,... | collective-permute-start | bytes 1081352 | tf_op jit(solution)/shard_map/ppermute | solution.py:341
  33.6 0.0 collective-permute-done.2.got.refs_1_
  33.6 0.0 copy-start.1
  33.6 0.8 copy-done.1
  34.4 2.1 %relay_rows.1 = (bf16[1408,128]{1,0:T(8,128)(2,1)}, bf16[1408,128]{1,0:T(8,128)(2,1)}) custom-call(s32[1]{0:T(128)} %bitcast.k_ref, bf16[1888,128]{1,0:T(8,128)(2,1)} %copy-done.1), custom_call_target="tpu_custom_call" | custom-call | flops 2000000 | bytes 3000000 | tf_op jit(solution)/shard_map/relay_rows/pallas_call | solution.py:293
  36.5 0.0 collective-permute-start.6
  36.5 3.2 %collective-permute-start.7 = (bf16[1408,128]{1,0:T(8,128)(2,1)}, bf16[1408,128]{1,0:T(8,128)(2,1)S(1)}, u32[]{:S(2)}, u32[]{:S(2)}) collective-permute-start(bf16[1408,128]{1,0:T(8,128)(2,1)} %get-tuple-element.21), channel_id=1, source_target_pairs={{0,6},{1,7},{2,0},{3,1},{4,2},{5,3},{6,4},{7,5},{8,14},{9,15},{10,... | collective-permute-start | bytes 1081352 | tf_op jit(solution)/shard_map/ppermute | solution.py:341
  39.8 8.4 %pack_weights.1 = (bf16[3,960,256]{2,1,0:T(8,128)(2,1)}, bf16[960,192]{1,0:T(8,128)(2,1)}, bf16[3,960,256]{2,1,0:T(8,128)(2,1)}, bf16[960,192]{1,0:T(8,128)(2,1)}, bf16[3072,256]{1,0:T(8,128)(2,1)}) custom-call(bf16[9,320,320]{2,1,0:T(8,128)(2,1)} %bitcast.17, bf16[9,320,320]{2,1,0:T(8,128)(2,1)} %bitcast.18, bf16[27,32,40]{2,1,0:T(8,128)(2,1)} %bitcast.24, ...), custom_call_target="tpu_custom_call" | custom-call | flops 10000000 | bytes 10000000 | tf_op jit(solution)/shard_map/pack_weights/pallas_call | solution.py:225
  48.2 0.6 pad_add_fusion.s_ref
  48.8 0.0 collective-permute-done.3.refs_2_
  48.8 0.0 copy-start.6
  48.8 0.0 collective-permute-done.4.refs_3_
  48.8 0.0 copy-start.7
  48.8 0.0 collective-permute-done.8.refs_7_
  48.8 0.0 copy-start.5
  48.8 1.1 %collective-permute-done.6.refs_5_ = bf16[1408,128]{1,0:T(8,128)(2,1)S(1)} collective-permute-done((bf16[1408,128]{1,0:T(8,128)(2,1)}, bf16[1408,128]{1,0:T(8,128)(2,1)S(1)}, u32[]{:S(2)}, u32[]{:S(2)}) %collective-permute-start.6) | collective-permute-done | bytes 360480 | tf_op jit(solution)/shard_map/ppermute | solution.py:341
  50.0 0.0 copy-start.8
  50.0 0.0 collective-permute-done.7.refs_6_
  50.0 0.0 copy-start.9
  50.0 0.0 copy-done.4
  50.0 0.0 copy-done.6
  50.0 0.0 copy-done.7
  50.0 0.0 copy-done.5
  50.0 0.7 copy-done.8
  50.7 0.1 copy-done.9
  50.9 59.3 %features_volume_aggregate.1 = bf16[32,24,8,256]{3,2,1,0:T(8,128)(2,1)} custom-call(s32[2]{0:T(128)} %pad_add_fusion.s_ref, bf16[1888,128]{1,0:T(8,128)(2,1)} %get-tuple-element.16.refs_0_, bf16[1888,128]{1,0:T(8,128)(2,1)} %copy-done.1, bf16[1408,128]{1,0:T(8,128)(2,1)} %copy-done.6, bf16[1408,128]{1,0:T(8,128)(2,1)} %copy-done.7, ...), custom_call_target="tpu_custom_call" | custom-call | tf_op jit(solution)/shard_map/features_volume_aggregate/pallas_call | solution.py:321
  (5 shorter events, 0.1 us)
Async XLA Ops:
  0.0 0.9 copy-start
  2.3 8.8 %copy-start.3 = (bf16[320,256]{0,1:T(8,128)(2,1)}, bf16[320,256]{0,1:T(8,128)(2,1)S(1)}, u32[]{:S(2)}) copy-start(bf16[320,256]{0,1:T(8,128)(2,1)S(1)} %copy.9) | copy-start | bytes 491524
  3.9 7.2 %copy-start.2 = (bf16[320,256]{0,1:T(8,128)(2,1)}, bf16[320,256]{0,1:T(8,128)(2,1)S(1)}, u32[]{:S(2)}) copy-start(bf16[320,256]{0,1:T(8,128)(2,1)S(1)} %copy.10) | copy-start | bytes 491524
  4.0 7.1 %collective-permute-start = (bf16[224,320]{1,0:T(8,128)(2,1)S(1)}, bf16[224,320]{1,0:T(8,128)(2,1)S(1)}, u32[]{:S(2)}, u32[]{:S(2)}) collective-permute-start(bf16[224,320]{1,0:T(8,128)(2,1)S(1)} %pad_maximum_fusion), channel_id=1, source_target_pairs={{0,8},{8,16},{16,24},{24,32},{32,40},{40,48},{48,56},{56,64},{64,7... | collective-permute-start | bytes 430088 | tf_op jit(solution)/shard_map/ppermute | solution.py:336
  5.9 5.1 %collective-permute-start.1 = (bf16[32,320]{1,0:T(8,128)(2,1)S(1)}, bf16[32,320]{1,0:T(8,128)(2,1)S(1)}, u32[]{:S(2)}, u32[]{:S(2)}) collective-permute-start(bf16[32,320]{1,0:T(8,128)(2,1)S(1)} %pad_maximum_fusion.1), channel_id=1, source_target_pairs={{8,0},{16,8},{24,16},{32,24},{40,32},{48,40},{56,48},{64,56},{72,6... | collective-permute-start | bytes 61448 | tf_op jit(solution)/shard_map/ppermute | solution.py:336
  11.1 0.6 copy-start.11
  11.1 0.7 copy-start.10
  14.2 19.5 %collective-permute-start.2 = (bf16[1888,128]{1,0:T(8,128)(2,1)}, bf16[1888,128]{1,0:T(8,128)(2,1)S(1)}, u32[]{:S(2)}, u32[]{:S(2)}) collective-permute-start(bf16[1888,128]{1,0:T(8,128)(2,1)} %get-tuple-element.16.refs_0_), channel_id=1, source_target_pairs={{0,1},{1,0},{2,3},{3,2},{4,5},{5,4},{6,7},{7,6},{8,9},{9,8},{10,11... | collective-permute-start | bytes 1449992 | tf_op jit(solution)/shard_map/ppermute | solution.py:341
  15.4 13.5 %collective-permute-start.5 = (bf16[1488,128]{1,0:T(8,128)(2,1)}, bf16[1488,128]{1,0:T(8,128)(2,1)S(1)}, u32[]{:S(2)}, u32[]{:S(2)}) collective-permute-start(bf16[1488,128]{1,0:T(8,128)(2,1)} %get-tuple-element.19), channel_id=1, source_target_pairs={{0,4},{1,5},{2,6},{3,7},{4,0},{5,1},{6,2},{7,3},{8,12},{9,13},{10,... | collective-permute-start | bytes 1142792 | tf_op jit(solution)/shard_map/ppermute | solution.py:341
  28.9 21.1 %copy-start.4 = (bf16[1488,128]{1,0:T(8,128)(2,1)}, bf16[1488,128]{1,0:T(8,128)(2,1)S(1)}, u32[]{:S(2)}) copy-start(bf16[1488,128]{1,0:T(8,128)(2,1)S(1)} %collective-permute-done.5.refs_4_) | copy-start | bytes 1142788
  28.9 19.9 %collective-permute-start.8 = (bf16[1488,128]{1,0:T(8,128)(2,1)S(1)}, bf16[1488,128]{1,0:T(8,128)(2,1)S(1)}, u32[]{:S(2)}, u32[]{:S(2)}) collective-permute-start(bf16[1488,128]{1,0:T(8,128)(2,1)S(1)} %collective-permute-done.5.refs_4_), channel_id=1, source_target_pairs={{0,1},{1,0},{2,3},{3,2},{4,5},{5,4},{6,7},{7,6},{8,9},{9,8},{10,11... | collective-permute-start | bytes 1142792 | tf_op jit(solution)/shard_map/ppermute | solution.py:341
  29.7 19.2 %collective-permute-start.3 = (bf16[1408,128]{1,0:T(8,128)(2,1)}, bf16[1408,128]{1,0:T(8,128)(2,1)S(1)}, u32[]{:S(2)}, u32[]{:S(2)}) collective-permute-start(bf16[1408,128]{1,0:T(8,128)(2,1)} %get-tuple-element.17), channel_id=1, source_target_pairs={{0,2},{1,3},{2,4},{3,5},{4,6},{5,7},{6,0},{7,1},{8,10},{9,11},{10,... | collective-permute-start | bytes 1081352 | tf_op jit(solution)/shard_map/ppermute | solution.py:341
  31.5 17.3 %collective-permute-start.4 = (bf16[1408,128]{1,0:T(8,128)(2,1)}, bf16[1408,128]{1,0:T(8,128)(2,1)S(1)}, u32[]{:S(2)}, u32[]{:S(2)}) collective-permute-start(bf16[1408,128]{1,0:T(8,128)(2,1)} %get-tuple-element.18), channel_id=1, source_target_pairs={{0,6},{1,7},{2,0},{3,1},{4,2},{5,3},{6,4},{7,5},{8,14},{9,15},{10,... | collective-permute-start | bytes 1081352 | tf_op jit(solution)/shard_map/ppermute | solution.py:341
  33.6 0.8 copy-start.1
  36.5 13.4 %collective-permute-start.6 = (bf16[1408,128]{1,0:T(8,128)(2,1)}, bf16[1408,128]{1,0:T(8,128)(2,1)S(1)}, u32[]{:S(2)}, u32[]{:S(2)}) collective-permute-start(bf16[1408,128]{1,0:T(8,128)(2,1)} %get-tuple-element.20), channel_id=1, source_target_pairs={{0,2},{1,3},{2,4},{3,5},{4,6},{5,7},{6,0},{7,1},{8,10},{9,11},{10,... | collective-permute-start | bytes 1081352 | tf_op jit(solution)/shard_map/ppermute | solution.py:341
  36.5 13.4 %collective-permute-start.7 = (bf16[1408,128]{1,0:T(8,128)(2,1)}, bf16[1408,128]{1,0:T(8,128)(2,1)S(1)}, u32[]{:S(2)}, u32[]{:S(2)}) collective-permute-start(bf16[1408,128]{1,0:T(8,128)(2,1)} %get-tuple-element.21), channel_id=1, source_target_pairs={{0,6},{1,7},{2,0},{3,1},{4,2},{5,3},{6,4},{7,5},{8,14},{9,15},{10,... | collective-permute-start | bytes 1081352 | tf_op jit(solution)/shard_map/ppermute | solution.py:341
  48.8 1.2 %copy-start.6 = (bf16[1408,128]{1,0:T(8,128)(2,1)}, bf16[1408,128]{1,0:T(8,128)(2,1)S(1)}, u32[]{:S(2)}) copy-start(bf16[1408,128]{1,0:T(8,128)(2,1)S(1)} %collective-permute-done.3.refs_2_) | copy-start | bytes 1081348
  48.8 1.2 %copy-start.7 = (bf16[1408,128]{1,0:T(8,128)(2,1)}, bf16[1408,128]{1,0:T(8,128)(2,1)S(1)}, u32[]{:S(2)}) copy-start(bf16[1408,128]{1,0:T(8,128)(2,1)S(1)} %collective-permute-done.4.refs_3_) | copy-start | bytes 1081348
  48.8 1.2 %copy-start.5 = (bf16[1488,128]{1,0:T(8,128)(2,1)}, bf16[1488,128]{1,0:T(8,128)(2,1)S(1)}, u32[]{:S(2)}) copy-start(bf16[1488,128]{1,0:T(8,128)(2,1)S(1)} %collective-permute-done.8.refs_7_) | copy-start | bytes 1142788
  50.0 0.8 copy-start.8
  50.0 0.9 copy-start.9

commit v5 on v4

--- a/solution.py
+++ b/solution.py
@@ -15,7 +15,7 @@
 LR, RR = 272, 296
 NT = BD + 2
 KT = 1024
-UN = 4
+UN = 8
 
 
 def dot(x, w):
@@ -62,16 +62,19 @@
         z[h + 1, 1, :, 0:64] = y[:, 128:192]
 
     def conv(x, wm, h):
-        y = dot(x[h], wm[0])
-        y += dot(x[h + 1], wm[1])
-        y += dot(x[h + 2], wm[2])
+        y = dot(x[h + 1], wm[1])
+        if h > 0:
+            y += dot(x[h], wm[0])
+        if h < H - 1:
+            y += dot(x[h + 2], wm[2])
         return y[:, :128], y[:, 128:], z[h, 0] + pltpu.roll(z[h + 1, 0], 64, 1) + z[h + 2, 1]
 
     def load(h, c):
         build(xs, h + 1, lambda n, e: raw[h, n, e:e + m, :], m)
         rest(xs, wr1, h)
         return c
-    lax.fori_loop(0, H, load, 0, unroll=UN)
+    for h in range(H):
+        load(h, 0)
     def first(i, c):
         for u in range(UN):
             first_row(UN * i + u, ts.at[u])
@@ -81,18 +84,20 @@
         for n, y in enumerate(conv(xs, wm1, h)):
             ts[n, 0:m, :] = jnp.where(ok, jnp.maximum(y, 0.0), 0.0)
         build(hs, h + 1, lambda n, e: ts[n, e:e + m, :], m)
-    lax.fori_loop(0, H // UN, first, 0)
+    first(0, 0)
     def rest2(h, c):
         rest(hs, wr2, h)
         return c
-    lax.fori_loop(0, H, rest2, 0, unroll=UN)
+    for h in range(H):
+        rest2(h, 0)
     def second(h, c):
         ok = jnp.logical_and(col + 2 >= 0, col + 2 < W)
         for n, y in enumerate(conv(hs, wm2, h)):
             y = jnp.where(ok, y + raw[h, n, 2:2 + m, :], 0.0)
             feat[h, n] = y.astype(jnp.bfloat16).astype(jnp.float32)
         return c
-    lax.fori_loop(0, H, second, 0, unroll=UN)
+    for h in range(H):
+        second(h, 0)
 
     lane = lax.broadcasted_iota(jnp.int32, (16, 128), 1)
     def place(i, c):
@@ -295,7 +300,7 @@
         out_shape=[rows_of(n) for n in outs],
         in_specs=[pl.BlockSpec(memory_space=pltpu.SMEM)] + [pl.BlockSpec(memory_space=pltpu.VMEM)] * len(args),
         scratch_shapes=[pltpu.VMEM((3, n, 128), jnp.float32) for n in scratch],
-        compiler_params=pltpu.CompilerParams(vmem_limit_bytes=56 * 2**20),
+        compiler_params=pltpu.CompilerParams(vmem_limit_bytes=32 * 2**20),
         cost_estimate=pl.CostEstimate(flops=2_000_000, bytes_accessed=3_000_000, transcendentals=0),
         name=name,
     )(k, *args)

time: 110 us -> 102 us (0.927)
  Pallas kernels: 72.2 us -> 64 us
  waiting for transfers between devices: 12.2 us -> 14.6 us
  local copies, waits for them, and re-layouts: 3.61 us -> 1.28 us
    pallas_call x1, Pallas kernels: 59.3 us -> 55.1 us  [main_call(): pl.pallas_call(main_kernel, out_shape=jax.ShapeDtypeStruct((F, BD, H, WL)...]
    pallas_call x2, Pallas kernels: 4.53 us -> 0.46 us  [small_call(): pl.pallas_call(kernel, out_shape=[rows_of(n) for n in outs], in_specs=[pl...]
    ppermute x7, waiting for transfers between devices: 10.7 us -> 13.1 us  [to_band(): return lax.ppermute(x, 'band', [(i, (i + 2 * z) % n ^ y) for i in range(n)])]
    unnamed x24 -> x10, local copies, waits for them, and re-layouts: 3.26 us -> 0.93 us
  transfers between devices with their start and end apart: 9 -> 9, of which waited for: 3 -> 3; matrix products, arithmetic and copies ran while one was open for 1% -> 1% of each run, Pallas kernels for 10% -> 8%
where the time goes in v5:
time: 102 us
  Pallas kernels  64 us (63%)
  starting transfers between devices  18.8 us (18%)
  waiting for transfers between devices  14.6 us (14%)
  matrix products  2.54 us (2%)
  local copies, waits for them, and re-layouts  1.28 us (1%)
    pallas_call x1, Pallas kernels, main_call(): pl.pallas_call(main_kernel, out_shape=jax.ShapeDtypeStruct((F, BD, H, WL)...  55.1 us
    ppermute x7, starting transfers between devices, to_band(): return lax.ppermute(x, 'band', [(i, (i + 2 * z) % n ^ y) for i in range(n)])  13.3 us
    ppermute x7, waiting for transfers between devices, to_band(): return lax.ppermute(x, 'band', [(i, (i + 2 * z) % n ^ y) for i in range(n)])  13.1 us
    pallas_call x1, Pallas kernels, weights_call(): pl.pallas_call(weights_kernel, out_shape=[bf(3, 960, 256), bf(960, 192),...  8.43 us
    ppermute x2, starting transfers between devices, from_col(): lax.ppermute(x, 'col', [(i, i + by) for i in range(n) if 0 <= i + by < n])  5.56 us
    dot_general x2, matrix products, dot_on(): lax.dot_general(x, y, (((i,), (j,)), ((), ())), preferred_element_type=jn...  2.54 us
  transfers between devices with their start and end apart: 9, of which 3 were waited for; matrix products, arithmetic and copies ran while one was open for 1% of the time, Pallas kernels for 8%

profile of v5, /device:TPU:20, one launch (start us, length us, event | category | flops | bytes accessed | tf_op | source)
XLA Modules:
  0.0 102.0 jit_solution(13216720691456459028)
XLA Ops:
  0.0 0.0 copy-start
  0.0 0.9 copy-done
  0.9 1.2 %convolution_convert_fusion.1 = bf16[320,256]{1,0:T(8,128)(2,1)S(1)} fusion(bf16[320,320]{1,0:T(8,128)(2,1)} %constant.13.clone.order, bf16[320,1,256]{2,0,1:T(8,128)(2,1)S(1)} %copy-done), kind=kOutput, calls=%fused_computation.1 | convolution fusion | flops 52510720 | bytes 532480 | tf_op jit(solution)/shard_map/dot_general | solution.py:26
  2.1 0.2 copy.9
  2.3 1.3 %convolution_convert_fusion = bf16[320,256]{1,0:T(8,128)(2,1)S(1)} fusion(bf16[320,320]{1,0:T(8,128)(2,1)} %constant.13.clone.order, bf16[320,1,256]{2,0,1:T(8,128)(2,1)} %param.7), kind=kOutput, calls=%fused_computation | convolution fusion | flops 52510720 | bytes 532480 | tf_op jit(solution)/shard_map/dot_general | solution.py:26
  3.7 0.2 copy.10
  3.9 1.9 %collective-permute-start = (bf16[224,320]{1,0:T(8,128)(2,1)S(1)}, bf16[224,320]{1,0:T(8,128)(2,1)S(1)}, u32[]{:S(2)}, u32[]{:S(2)}) collective-permute-start(bf16[224,320]{1,0:T(8,128)(2,1)S(1)} %pad_maximum_fusion), channel_id=1, source_target_pairs={{0,8},{8,16},{16,24},{24,32},{32,40},{40,48},{48,56},{56,64},{64,7... | collective-permute-start | bytes 430088 | tf_op jit(solution)/shard_map/ppermute | solution.py:341
  5.8 3.6 %collective-permute-start.1 = (bf16[32,320]{1,0:T(8,128)(2,1)S(1)}, bf16[32,320]{1,0:T(8,128)(2,1)S(1)}, u32[]{:S(2)}, u32[]{:S(2)}) collective-permute-start(bf16[32,320]{1,0:T(8,128)(2,1)S(1)} %pad_maximum_fusion.1), channel_id=1, source_target_pairs={{8,0},{16,8},{24,16},{32,24},{40,32},{48,40},{56,48},{64,56},{72,6... | collective-permute-start | bytes 61448 | tf_op jit(solution)/shard_map/ppermute | solution.py:341
  9.5 1.5 %collective-permute-done.1.after = bf16[32,320]{1,0:T(8,128)(2,1)S(1)} collective-permute-done((bf16[32,320]{1,0:T(8,128)(2,1)S(1)}, bf16[32,320]{1,0:T(8,128)(2,1)S(1)}, u32[]{:S(2)}, u32[]{:S(2)}) %collective-permute-start.1) | collective-permute-done | bytes 20512 | tf_op jit(solution)/shard_map/ppermute | solution.py:341
  11.0 0.0 collective-permute-done.before
  11.0 0.3 pack_rows.1
  11.3 0.0 copy-start.2
  11.3 1.4 %collective-permute-start.2 = (bf16[1888,128]{1,0:T(8,128)(2,1)S(1)}, bf16[1888,128]{1,0:T(8,128)(2,1)S(1)}, u32[]{:S(2)}, u32[]{:S(2)}) collective-permute-start(bf16[1888,128]{1,0:T(8,128)(2,1)S(1)} %get-tuple-element.16.refs_0_), channel_id=1, source_target_pairs={{0,1},{1,0},{2,3},{3,2},{4,5},{5,4},{6,7},{7,6},{8,9},{9,8},{10,11... | collective-permute-start | bytes 1449992 | tf_op jit(solution)/shard_map/ppermute | solution.py:346
  12.6 3.9 %collective-permute-start.5 = (bf16[1488,128]{1,0:T(8,128)(2,1)S(1)}, bf16[1488,128]{1,0:T(8,128)(2,1)S(1)}, u32[]{:S(2)}, u32[]{:S(2)}) collective-permute-start(bf16[1488,128]{1,0:T(8,128)(2,1)S(1)} %get-tuple-element.19), channel_id=1, source_target_pairs={{0,4},{1,5},{2,6},{3,7},{4,0},{5,1},{6,2},{7,3},{8,12},{9,13},{10,... | collective-permute-start | bytes 1142792 | tf_op jit(solution)/shard_map/ppermute | solution.py:346
  16.5 9.4 %collective-permute-done.5.refs_4_ = bf16[1488,128]{1,0:T(8,128)(2,1)S(1)} collective-permute-done((bf16[1488,128]{1,0:T(8,128)(2,1)S(1)}, bf16[1488,128]{1,0:T(8,128)(2,1)S(1)}, u32[]{:S(2)}, u32[]{:S(2)}) %collective-permute-start.5) | collective-permute-done | bytes 380960 | tf_op jit(solution)/shard_map/ppermute | solution.py:346
  25.9 0.0 copy-start.3
  25.9 0.7 collective-permute-start.8
  26.6 1.9 %collective-permute-start.3 = (bf16[1408,128]{1,0:T(8,128)(2,1)S(1)}, bf16[1408,128]{1,0:T(8,128)(2,1)}, u32[]{:S(2)}, u32[]{:S(2)}) collective-permute-start(bf16[1408,128]{1,0:T(8,128)(2,1)S(1)} %get-tuple-element.17), channel_id=1, source_target_pairs={{0,2},{1,3},{2,4},{3,5},{4,6},{5,7},{6,0},{7,1},{8,10},{9,11},{10,... | collective-permute-start | bytes 1081352 | tf_op jit(solution)/shard_map/ppermute | solution.py:346
  28.5 2.1 %collective-permute-start.4 = (bf16[1408,128]{1,0:T(8,128)(2,1)S(1)}, bf16[1408,128]{1,0:T(8,128)(2,1)}, u32[]{:S(2)}, u32[]{:S(2)}) collective-permute-start(bf16[1408,128]{1,0:T(8,128)(2,1)S(1)} %get-tuple-element.18), channel_id=1, source_target_pairs={{0,6},{1,7},{2,0},{3,1},{4,2},{5,3},{6,4},{7,5},{8,14},{9,15},{10,... | collective-permute-start | bytes 1081352 | tf_op jit(solution)/shard_map/ppermute | solution.py:346
  30.6 0.0 collective-permute-done.2.got.refs_1_
  30.6 0.0 copy-start.1
  30.6 0.2 relay_rows.1
  30.8 0.1 collective-permute-start.6
  30.9 3.2 %collective-permute-start.7 = (bf16[1408,128]{1,0:T(8,128)(2,1)S(1)}, bf16[1408,128]{1,0:T(8,128)(2,1)}, u32[]{:S(2)}, u32[]{:S(2)}) collective-permute-start(bf16[1408,128]{1,0:T(8,128)(2,1)S(1)} %get-tuple-element.21), channel_id=1, source_target_pairs={{0,6},{1,7},{2,0},{3,1},{4,2},{5,3},{6,4},{7,5},{8,14},{9,15},{10,... | collective-permute-start | bytes 1081352 | tf_op jit(solution)/shard_map/ppermute | solution.py:346
  34.1 8.4 %pack_weights.1 = (bf16[3,960,256]{2,1,0:T(8,128)(2,1)}, bf16[960,192]{1,0:T(8,128)(2,1)}, bf16[3,960,256]{2,1,0:T(8,128)(2,1)}, bf16[960,192]{1,0:T(8,128)(2,1)}, bf16[3072,256]{1,0:T(8,128)(2,1)}) custom-call(bf16[9,320,320]{2,1,0:T(8,128)(2,1)} %bitcast.22, bf16[9,320,320]{2,1,0:T(8,128)(2,1)} %bitcast.23, bf16[27,32,40]{2,1,0:T(8,128)(2,1)} %bitcast.24, ...), custom_call_target="tpu_custom_call" | custom-call | flops 10000000 | bytes 10000000 | tf_op jit(solution)/shard_map/pack_weights/pallas_call | solution.py:230
  42.5 0.0 copy-done.2
  42.5 0.0 copy-done.3
  42.5 0.0 copy-done.1
  42.5 0.6 pad_add_fusion.s_ref
  43.1 0.0 collective-permute-done.3.refs_2_
  43.1 0.0 collective-permute-done.4.refs_3_
  43.1 0.0 collective-permute-done.8.refs_7_
  43.1 0.0 copy-start.4
  43.2 3.7 %collective-permute-done.6.refs_5_ = bf16[1408,128]{1,0:T(8,128)(2,1)} collective-permute-done((bf16[1408,128]{1,0:T(8,128)(2,1)S(1)}, bf16[1408,128]{1,0:T(8,128)(2,1)}, u32[]{:S(2)}, u32[]{:S(2)}) %collective-permute-start.6) | collective-permute-done | bytes 360480 | tf_op jit(solution)/shard_map/ppermute | solution.py:346
  46.8 0.0 collective-permute-done.7.refs_6_
  46.8 0.0 copy-done.4
  46.9 55.1 %features_volume_aggregate.1 = bf16[32,24,8,256]{3,2,1,0:T(8,128)(2,1)} custom-call(s32[2]{0:T(128)} %pad_add_fusion.s_ref, bf16[1888,128]{1,0:T(8,128)(2,1)} %copy-done.2, bf16[1888,128]{1,0:T(8,128)(2,1)} %copy-done.1, bf16[1408,128]{1,0:T(8,128)(2,1)} %collective-permute-done.3.refs_2_, bf16[1408,128]{1,0:T(8,128)(2,1)} %collective-permute-done.4.refs_3_, ...), custom_call_target="tpu_custom_call" | custom-call | tf_op jit(solution)/shard_map/features_volume_aggregate/pallas_call | solution.py:326
  (5 shorter events, 0.1 us)
Async XLA Ops:
  0.0 0.9 copy-start
  3.9 7.1 %collective-permute-start = (bf16[224,320]{1,0:T(8,128)(2,1)S(1)}, bf16[224,320]{1,0:T(8,128)(2,1)S(1)}, u32[]{:S(2)}, u32[]{:S(2)}) collective-permute-start(bf16[224,320]{1,0:T(8,128)(2,1)S(1)} %pad_maximum_fusion), channel_id=1, source_target_pairs={{0,8},{8,16},{16,24},{24,32},{32,40},{40,48},{48,56},{56,64},{64,7... | collective-permute-start | bytes 430088 | tf_op jit(solution)/shard_map/ppermute | solution.py:341
  5.8 5.1 %collective-permute-start.1 = (bf16[32,320]{1,0:T(8,128)(2,1)S(1)}, bf16[32,320]{1,0:T(8,128)(2,1)S(1)}, u32[]{:S(2)}, u32[]{:S(2)}) collective-permute-start(bf16[32,320]{1,0:T(8,128)(2,1)S(1)} %pad_maximum_fusion.1), channel_id=1, source_target_pairs={{8,0},{16,8},{24,16},{32,24},{40,32},{48,40},{56,48},{64,56},{72,6... | collective-permute-start | bytes 61448 | tf_op jit(solution)/shard_map/ppermute | solution.py:341
  11.3 31.3 %copy-start.2 = (bf16[1888,128]{1,0:T(8,128)(2,1)}, bf16[1888,128]{1,0:T(8,128)(2,1)S(1)}, u32[]{:S(2)}) copy-start(bf16[1888,128]{1,0:T(8,128)(2,1)S(1)} %get-tuple-element.16.refs_0_) | copy-start | bytes 1449988
  11.3 19.3 %collective-permute-start.2 = (bf16[1888,128]{1,0:T(8,128)(2,1)S(1)}, bf16[1888,128]{1,0:T(8,128)(2,1)S(1)}, u32[]{:S(2)}, u32[]{:S(2)}) collective-permute-start(bf16[1888,128]{1,0:T(8,128)(2,1)S(1)} %get-tuple-element.16.refs_0_), channel_id=1, source_target_pairs={{0,1},{1,0},{2,3},{3,2},{4,5},{5,4},{6,7},{7,6},{8,9},{9,8},{10,11... | collective-permute-start | bytes 1449992 | tf_op jit(solution)/shard_map/ppermute | solution.py:346
  12.6 13.3 %collective-permute-start.5 = (bf16[1488,128]{1,0:T(8,128)(2,1)S(1)}, bf16[1488,128]{1,0:T(8,128)(2,1)S(1)}, u32[]{:S(2)}, u32[]{:S(2)}) collective-permute-start(bf16[1488,128]{1,0:T(8,128)(2,1)S(1)} %get-tuple-element.19), channel_id=1, source_target_pairs={{0,4},{1,5},{2,6},{3,7},{4,0},{5,1},{6,2},{7,3},{8,12},{9,13},{10,... | collective-permute-start | bytes 1142792 | tf_op jit(solution)/shard_map/ppermute | solution.py:346
  25.9 16.7 %copy-start.3 = (bf16[1488,128]{1,0:T(8,128)(2,1)}, bf16[1488,128]{1,0:T(8,128)(2,1)S(1)}, u32[]{:S(2)}) copy-start(bf16[1488,128]{1,0:T(8,128)(2,1)S(1)} %collective-permute-done.5.refs_4_) | copy-start | bytes 1142788
  25.9 17.3 %collective-permute-start.8 = (bf16[1488,128]{1,0:T(8,128)(2,1)S(1)}, bf16[1488,128]{1,0:T(8,128)(2,1)S(1)}, u32[]{:S(2)}, u32[]{:S(2)}) collective-permute-start(bf16[1488,128]{1,0:T(8,128)(2,1)S(1)} %collective-permute-done.5.refs_4_), channel_id=1, source_target_pairs={{0,1},{1,0},{2,3},{3,2},{4,5},{5,4},{6,7},{7,6},{8,9},{9,8},{10,11... | collective-permute-start | bytes 1142792 | tf_op jit(solution)/shard_map/ppermute | solution.py:346
  26.6 16.5 %collective-permute-start.3 = (bf16[1408,128]{1,0:T(8,128)(2,1)S(1)}, bf16[1408,128]{1,0:T(8,128)(2,1)}, u32[]{:S(2)}, u32[]{:S(2)}) collective-permute-start(bf16[1408,128]{1,0:T(8,128)(2,1)S(1)} %get-tuple-element.17), channel_id=1, source_target_pairs={{0,2},{1,3},{2,4},{3,5},{4,6},{5,7},{6,0},{7,1},{8,10},{9,11},{10,... | collective-permute-start | bytes 1081352 | tf_op jit(solution)/shard_map/ppermute | solution.py:346
  28.5 14.7 %collective-permute-start.4 = (bf16[1408,128]{1,0:T(8,128)(2,1)S(1)}, bf16[1408,128]{1,0:T(8,128)(2,1)}, u32[]{:S(2)}, u32[]{:S(2)}) collective-permute-start(bf16[1408,128]{1,0:T(8,128)(2,1)S(1)} %get-tuple-element.18), channel_id=1, source_target_pairs={{0,6},{1,7},{2,0},{3,1},{4,2},{5,3},{6,4},{7,5},{8,14},{9,15},{10,... | collective-permute-start | bytes 1081352 | tf_op jit(solution)/shard_map/ppermute | solution.py:346
  30.6 11.9 %copy-start.1 = (bf16[1888,128]{1,0:T(8,128)(2,1)}, bf16[1888,128]{1,0:T(8,128)(2,1)S(1)}, u32[]{:S(2)}) copy-start(bf16[1888,128]{1,0:T(8,128)(2,1)S(1)} %collective-permute-done.2.got.refs_1_) | copy-start | bytes 1449988
  30.8 16.0 %collective-permute-start.6 = (bf16[1408,128]{1,0:T(8,128)(2,1)S(1)}, bf16[1408,128]{1,0:T(8,128)(2,1)}, u32[]{:S(2)}, u32[]{:S(2)}) collective-permute-start(bf16[1408,128]{1,0:T(8,128)(2,1)S(1)} %get-tuple-element.20), channel_id=1, source_target_pairs={{0,2},{1,3},{2,4},{3,5},{4,6},{5,7},{6,0},{7,1},{8,10},{9,11},{10,... | collective-permute-start | bytes 1081352 | tf_op jit(solution)/shard_map/ppermute | solution.py:346
  30.9 16.0 %collective-permute-start.7 = (bf16[1408,128]{1,0:T(8,128)(2,1)S(1)}, bf16[1408,128]{1,0:T(8,128)(2,1)}, u32[]{:S(2)}, u32[]{:S(2)}) collective-permute-start(bf16[1408,128]{1,0:T(8,128)(2,1)S(1)} %get-tuple-element.21), channel_id=1, source_target_pairs={{0,6},{1,7},{2,0},{3,1},{4,2},{5,3},{6,4},{7,5},{8,14},{9,15},{10,... | collective-permute-start | bytes 1081352 | tf_op jit(solution)/shard_map/ppermute | solution.py:346
  43.1 3.7 %copy-start.4 = (bf16[1488,128]{1,0:T(8,128)(2,1)}, bf16[1488,128]{1,0:T(8,128)(2,1)S(1)}, u32[]{:S(2)}) copy-start(bf16[1488,128]{1,0:T(8,128)(2,1)S(1)} %collective-permute-done.8.refs_7_) | copy-start | bytes 1142788

commit v6 on v5

--- a/solution.py
+++ b/solution.py
@@ -359,7 +359,7 @@
     across = to_band(full, 0, 1)
     above, below, twice = to_band(up, 1, 0), to_band(down, 3, 0), to_band(far, 2, 0)
     up, down = small_call(relay_kernel, k[None], (across,), (EXACT, EXACT), (FULL,), "relay_rows")
-    rows = [full, across, above, below, twice, to_band(up, 1, 0), to_band(down, 3, 0), to_band(twice, 0, 1)]
+    rows = [full, across, above, below, twice, to_band(up, 1, 0), to_band(down, 3, 0), to_band(far, 2, 1)]
     return main_call(jnp.stack([k, base]), rows, weights, taps)
 
 

time: 102 us -> 112 us (1.098)
  the two profiles are of different devices: /device:TPU:20 before, /device:TPU:15 now
where the time goes in v6:
time: 112 us
  Pallas kernels  64 us (57%)
  waiting for transfers between devices  25.7 us (23%)
  starting transfers between devices  16 us (14%)
  local copies, waits for them, and re-layouts  2.83 us (3%)
  matrix products  2.54 us (2%)
    pallas_call x1, Pallas kernels, main_call(): pl.pallas_call(main_kernel, out_shape=jax.ShapeDtypeStruct((F, BD, H, WL)...  55.1 us
    ppermute x7, waiting for transfers between devices, to_band(): return lax.ppermute(x, 'band', [(i, (i + 2 * z) % n ^ y) for i in range(n)])  18.7 us
    ppermute x7, starting transfers between devices, to_band(): return lax.ppermute(x, 'band', [(i, (i + 2 * z) % n ^ y) for i in range(n)])  9.7 us
    pallas_call x1, Pallas kernels, weights_call(): pl.pallas_call(weights_kernel, out_shape=[bf(3, 960, 256), bf(960, 192),...  8.43 us
    ppermute x2, waiting for transfers between devices, from_col(): lax.ppermute(x, 'col', [(i, i + by) for i in range(n) if 0 <= i + by < n])  6.94 us
    ppermute x2, starting transfers between devices, from_col(): lax.ppermute(x, 'col', [(i, i + by) for i in range(n) if 0 <= i + by < n])  6.32 us
    dot_general x2, matrix products, dot_on(): lax.dot_general(x, y, (((i,), (j,)), ((), ())), preferred_element_type=jn...  2.54 us
    unnamed x12, local copies, waits for them, and re-layouts  2.48 us
  transfers between devices with their start and end apart: 9, of which 3 were waited for; matrix products, arithmetic and copies ran while one was open for 1% of the time, Pallas kernels for 8%

profile of v6, /device:TPU:15, one launch (start us, length us, event | category | flops | bytes accessed | tf_op | source)
XLA Modules:
  0.0 111.8 jit_solution(2731768648034009375)
XLA Ops:
  0.0 0.0 copy-start
  0.0 0.9 copy-done
  0.9 1.2 %convolution_convert_fusion.1 = bf16[320,256]{1,0:T(8,128)(2,1)S(1)} fusion(bf16[320,320]{1,0:T(8,128)(2,1)} %constant.13.clone.order, bf16[320,1,256]{2,0,1:T(8,128)(2,1)S(1)} %copy-done), kind=kOutput, calls=%fused_computation.1 | convolution fusion | flops 52510720 | bytes 532480 | tf_op jit(solution)/shard_map/dot_general | solution.py:26
  2.1 0.2 copy.9
  2.3 1.3 %convolution_convert_fusion = bf16[320,256]{1,0:T(8,128)(2,1)S(1)} fusion(bf16[320,320]{1,0:T(8,128)(2,1)} %constant.13.clone.order, bf16[320,1,256]{2,0,1:T(8,128)(2,1)} %param.7), kind=kOutput, calls=%fused_computation | convolution fusion | flops 52510720 | bytes 532480 | tf_op jit(solution)/shard_map/dot_general | solution.py:26
  3.7 0.2 copy.10
  3.9 4.4 %collective-permute-start = (bf16[224,320]{1,0:T(8,128)(2,1)S(1)}, bf16[224,320]{1,0:T(8,128)(2,1)S(1)}, u32[]{:S(2)}, u32[]{:S(2)}) collective-permute-start(bf16[224,320]{1,0:T(8,128)(2,1)S(1)} %pad_maximum_fusion), channel_id=1, source_target_pairs={{0,8},{8,16},{16,24},{24,32},{32,40},{40,48},{48,56},{56,64},{64,7... | collective-permute-start | bytes 430088 | tf_op jit(solution)/shard_map/ppermute | solution.py:341
  8.3 1.9 %collective-permute-start.1 = (bf16[32,320]{1,0:T(8,128)(2,1)S(1)}, bf16[32,320]{1,0:T(8,128)(2,1)S(1)}, u32[]{:S(2)}, u32[]{:S(2)}) collective-permute-start(bf16[32,320]{1,0:T(8,128)(2,1)S(1)} %pad_maximum_fusion.1), channel_id=1, source_target_pairs={{8,0},{16,8},{24,16},{32,24},{40,32},{48,40},{56,48},{64,56},{72,6... | collective-permute-start | bytes 61448 | tf_op jit(solution)/shard_map/ppermute | solution.py:341
  10.2 6.9 %collective-permute-done.1.after = bf16[32,320]{1,0:T(8,128)(2,1)S(1)} collective-permute-done((bf16[32,320]{1,0:T(8,128)(2,1)S(1)}, bf16[32,320]{1,0:T(8,128)(2,1)S(1)}, u32[]{:S(2)}, u32[]{:S(2)}) %collective-permute-start.1) | collective-permute-done | bytes 20512 | tf_op jit(solution)/shard_map/ppermute | solution.py:341
  17.2 0.0 collective-permute-done.before
  17.2 0.3 pack_rows.1
  17.5 0.0 copy-start.2
  17.5 1.1 %collective-permute-start.2 = (bf16[1888,128]{1,0:T(8,128)(2,1)S(1)}, bf16[1888,128]{1,0:T(8,128)(2,1)S(1)}, u32[]{:S(2)}, u32[]{:S(2)}) collective-permute-start(bf16[1888,128]{1,0:T(8,128)(2,1)S(1)} %get-tuple-element.16.refs_0_), channel_id=1, source_target_pairs={{0,1},{1,0},{2,3},{3,2},{4,5},{5,4},{6,7},{7,6},{8,9},{9,8},{10,11... | collective-permute-start | bytes 1449992 | tf_op jit(solution)/shard_map/ppermute | solution.py:346
  18.6 1.6 %collective-permute-start.3 = (bf16[1408,128]{1,0:T(8,128)(2,1)S(1)}, bf16[1408,128]{1,0:T(8,128)(2,1)S(1)}, u32[]{:S(2)}, u32[]{:S(2)}) collective-permute-start(bf16[1408,128]{1,0:T(8,128)(2,1)S(1)} %get-tuple-element.17), channel_id=1, source_target_pairs={{0,2},{1,3},{2,4},{3,5},{4,6},{5,7},{6,0},{7,1},{8,10},{9,11},{10,... | collective-permute-start | bytes 1081352 | tf_op jit(solution)/shard_map/ppermute | solution.py:346
  20.3 3.4 %collective-permute-start.8 = (bf16[1488,128]{1,0:T(8,128)(2,1)S(1)}, bf16[1488,128]{1,0:T(8,128)(2,1)S(1)}, u32[]{:S(2)}, u32[]{:S(2)}) collective-permute-start(bf16[1488,128]{1,0:T(8,128)(2,1)S(1)} %get-tuple-element.19), channel_id=1, source_target_pairs={{0,5},{1,4},{2,7},{3,6},{4,1},{5,0},{6,3},{7,2},{8,13},{9,12},{10,... | collective-permute-start | bytes 1142792 | tf_op jit(solution)/shard_map/ppermute | solution.py:346
  23.7 0.0 collective-permute-start.5
  23.7 1.8 %collective-permute-start.4 = (bf16[1408,128]{1,0:T(8,128)(2,1)S(1)}, bf16[1408,128]{1,0:T(8,128)(2,1)}, u32[]{:S(2)}, u32[]{:S(2)}) collective-permute-start(bf16[1408,128]{1,0:T(8,128)(2,1)S(1)} %get-tuple-element.18), channel_id=1, source_target_pairs={{0,6},{1,7},{2,0},{3,1},{4,2},{5,3},{6,4},{7,5},{8,14},{9,15},{10,... | collective-permute-start | bytes 1081352 | tf_op jit(solution)/shard_map/ppermute | solution.py:346
  25.5 4.3 %collective-permute-done.2.got.refs_1_ = bf16[1888,128]{1,0:T(8,128)(2,1)S(1)} collective-permute-done((bf16[1888,128]{1,0:T(8,128)(2,1)S(1)}, bf16[1888,128]{1,0:T(8,128)(2,1)S(1)}, u32[]{:S(2)}, u32[]{:S(2)}) %collective-permute-start.2) | collective-permute-done | bytes 483360 | tf_op jit(solution)/shard_map/ppermute | solution.py:346
  29.7 0.0 copy-start.1
  29.7 0.2 relay_rows.1
  29.9 1.7 %collective-permute-start.6 = (bf16[1408,128]{1,0:T(8,128)(2,1)S(1)}, bf16[1408,128]{1,0:T(8,128)(2,1)}, u32[]{:S(2)}, u32[]{:S(2)}) collective-permute-start(bf16[1408,128]{1,0:T(8,128)(2,1)S(1)} %get-tuple-element.20), channel_id=1, source_target_pairs={{0,2},{1,3},{2,4},{3,5},{4,6},{5,7},{6,0},{7,1},{8,10},{9,11},{10,... | collective-permute-start | bytes 1081352 | tf_op jit(solution)/shard_map/ppermute | solution.py:346
  31.6 14.4 %collective-permute-done.3.refs_2_ = bf16[1408,128]{1,0:T(8,128)(2,1)S(1)} collective-permute-done((bf16[1408,128]{1,0:T(8,128)(2,1)S(1)}, bf16[1408,128]{1,0:T(8,128)(2,1)S(1)}, u32[]{:S(2)}, u32[]{:S(2)}) %collective-permute-start.3) | collective-permute-done | bytes 360480 | tf_op jit(solution)/shard_map/ppermute | solution.py:346
  46.1 0.0 copy-start.5
  46.1 0.7 copy-done.5
  46.8 0.0 collective-permute-start.7
  46.8 8.4 %pack_weights.1 = (bf16[3,960,256]{2,1,0:T(8,128)(2,1)}, bf16[960,192]{1,0:T(8,128)(2,1)}, bf16[3,960,256]{2,1,0:T(8,128)(2,1)}, bf16[960,192]{1,0:T(8,128)(2,1)}, bf16[3072,256]{1,0:T(8,128)(2,1)}) custom-call(bf16[9,320,320]{2,1,0:T(8,128)(2,1)} %bitcast.22, bf16[9,320,320]{2,1,0:T(8,128)(2,1)} %bitcast.23, bf16[27,32,40]{2,1,0:T(8,128)(2,1)} %bitcast.24, ...), custom_call_target="tpu_custom_call" | custom-call | flops 10000000 | bytes 10000000 | tf_op jit(solution)/shard_map/pack_weights/pallas_call | solution.py:230
  55.3 0.0 copy-done.2
  55.3 0.0 copy-done.1
  55.3 0.6 pad_add_fusion.s_ref
  55.9 0.0 collective-permute-done.4.refs_3_
  55.9 0.0 collective-permute-done.8.refs_7_
  55.9 0.0 copy-start.3
  55.9 0.0 collective-permute-done.5.refs_4_
  55.9 0.0 copy-start.4
  55.9 0.0 collective-permute-done.6.refs_5_
  55.9 0.0 collective-permute-done.7.refs_6_
  55.9 0.7 copy-done.3
  56.6 0.1 copy-done.4
  56.7 55.1 %features_volume_aggregate.1 = bf16[32,24,8,256]{3,2,1,0:T(8,128)(2,1)} custom-call(s32[2]{0:T(128)} %pad_add_fusion.s_ref, bf16[1888,128]{1,0:T(8,128)(2,1)} %copy-done.2, bf16[1888,128]{1,0:T(8,128)(2,1)} %copy-done.1, bf16[1408,128]{1,0:T(8,128)(2,1)} %copy-done.5, bf16[1408,128]{1,0:T(8,128)(2,1)} %collective-permute-done.4.refs_3_, ...), custom_call_target="tpu_custom_call" | custom-call | tf_op jit(solution)/shard_map/features_volume_aggregate/pallas_call | solution.py:326
  (5 shorter events, 0.1 us)
Async XLA Ops:
  0.0 0.9 copy-start
  3.9 13.3 %collective-permute-start = (bf16[224,320]{1,0:T(8,128)(2,1)S(1)}, bf16[224,320]{1,0:T(8,128)(2,1)S(1)}, u32[]{:S(2)}, u32[]{:S(2)}) collective-permute-start(bf16[224,320]{1,0:T(8,128)(2,1)S(1)} %pad_maximum_fusion), channel_id=1, source_target_pairs={{0,8},{8,16},{16,24},{24,32},{32,40},{40,48},{48,56},{56,64},{64,7... | collective-permute-start | bytes 430088 | tf_op jit(solution)/shard_map/ppermute | solution.py:341
  8.3 8.9 %collective-permute-start.1 = (bf16[32,320]{1,0:T(8,128)(2,1)S(1)}, bf16[32,320]{1,0:T(8,128)(2,1)S(1)}, u32[]{:S(2)}, u32[]{:S(2)}) collective-permute-start(bf16[32,320]{1,0:T(8,128)(2,1)S(1)} %pad_maximum_fusion.1), channel_id=1, source_target_pairs={{8,0},{16,8},{24,16},{32,24},{40,32},{48,40},{56,48},{64,56},{72,6... | collective-permute-start | bytes 61448 | tf_op jit(solution)/shard_map/ppermute | solution.py:341
  17.5 37.8 %copy-start.2 = (bf16[1888,128]{1,0:T(8,128)(2,1)}, bf16[1888,128]{1,0:T(8,128)(2,1)S(1)}, u32[]{:S(2)}) copy-start(bf16[1888,128]{1,0:T(8,128)(2,1)S(1)} %get-tuple-element.16.refs_0_) | copy-start | bytes 1449988
  17.5 12.3 %collective-permute-start.2 = (bf16[1888,128]{1,0:T(8,128)(2,1)S(1)}, bf16[1888,128]{1,0:T(8,128)(2,1)S(1)}, u32[]{:S(2)}, u32[]{:S(2)}) collective-permute-start(bf16[1888,128]{1,0:T(8,128)(2,1)S(1)} %get-tuple-element.16.refs_0_), channel_id=1, source_target_pairs={{0,1},{1,0},{2,3},{3,2},{4,5},{5,4},{6,7},{7,6},{8,9},{9,8},{10,11... | collective-permute-start | bytes 1449992 | tf_op jit(solution)/shard_map/ppermute | solution.py:346
  18.6 27.5 %collective-permute-start.3 = (bf16[1408,128]{1,0:T(8,128)(2,1)S(1)}, bf16[1408,128]{1,0:T(8,128)(2,1)S(1)}, u32[]{:S(2)}, u32[]{:S(2)}) collective-permute-start(bf16[1408,128]{1,0:T(8,128)(2,1)S(1)} %get-tuple-element.17), channel_id=1, source_target_pairs={{0,2},{1,3},{2,4},{3,5},{4,6},{5,7},{6,0},{7,1},{8,10},{9,11},{10,... | collective-permute-start | bytes 1081352 | tf_op jit(solution)/shard_map/ppermute | solution.py:346
  20.3 35.6 %collective-permute-start.8 = (bf16[1488,128]{1,0:T(8,128)(2,1)S(1)}, bf16[1488,128]{1,0:T(8,128)(2,1)S(1)}, u32[]{:S(2)}, u32[]{:S(2)}) collective-permute-start(bf16[1488,128]{1,0:T(8,128)(2,1)S(1)} %get-tuple-element.19), channel_id=1, source_target_pairs={{0,5},{1,4},{2,7},{3,6},{4,1},{5,0},{6,3},{7,2},{8,13},{9,12},{10,... | collective-permute-start | bytes 1142792 | tf_op jit(solution)/shard_map/ppermute | solution.py:346
  23.7 32.2 %collective-permute-start.5 = (bf16[1488,128]{1,0:T(8,128)(2,1)S(1)}, bf16[1488,128]{1,0:T(8,128)(2,1)S(1)}, u32[]{:S(2)}, u32[]{:S(2)}) collective-permute-start(bf16[1488,128]{1,0:T(8,128)(2,1)S(1)} %get-tuple-element.19), channel_id=1, source_target_pairs={{0,4},{1,5},{2,6},{3,7},{4,0},{5,1},{6,2},{7,3},{8,12},{9,13},{10,... | collective-permute-start | bytes 1142792 | tf_op jit(solution)/shard_map/ppermute | solution.py:346
  23.7 32.2 %collective-permute-start.4 = (bf16[1408,128]{1,0:T(8,128)(2,1)S(1)}, bf16[1408,128]{1,0:T(8,128)(2,1)}, u32[]{:S(2)}, u32[]{:S(2)}) collective-permute-start(bf16[1408,128]{1,0:T(8,128)(2,1)S(1)} %get-tuple-element.18), channel_id=1, source_target_pairs={{0,6},{1,7},{2,0},{3,1},{4,2},{5,3},{6,4},{7,5},{8,14},{9,15},{10,... | collective-permute-start | bytes 1081352 | tf_op jit(solution)/shard_map/ppermute | solution.py:346
  29.7 25.5 %copy-start.1 = (bf16[1888,128]{1,0:T(8,128)(2,1)}, bf16[1888,128]{1,0:T(8,128)(2,1)S(1)}, u32[]{:S(2)}) copy-start(bf16[1888,128]{1,0:T(8,128)(2,1)S(1)} %collective-permute-done.2.got.refs_1_) | copy-start | bytes 1449988
  29.9 26.0 %collective-permute-start.6 = (bf16[1408,128]{1,0:T(8,128)(2,1)S(1)}, bf16[1408,128]{1,0:T(8,128)(2,1)}, u32[]{:S(2)}, u32[]{:S(2)}) collective-permute-start(bf16[1408,128]{1,0:T(8,128)(2,1)S(1)} %get-tuple-element.20), channel_id=1, source_target_pairs={{0,2},{1,3},{2,4},{3,5},{4,6},{5,7},{6,0},{7,1},{8,10},{9,11},{10,... | collective-permute-start | bytes 1081352 | tf_op jit(solution)/shard_map/ppermute | solution.py:346
  46.1 0.7 copy-start.5
  46.8 9.1 %collective-permute-start.7 = (bf16[1408,128]{1,0:T(8,128)(2,1)S(1)}, bf16[1408,128]{1,0:T(8,128)(2,1)}, u32[]{:S(2)}, u32[]{:S(2)}) collective-permute-start(bf16[1408,128]{1,0:T(8,128)(2,1)S(1)} %get-tuple-element.21), channel_id=1, source_target_pairs={{0,6},{1,7},{2,0},{3,1},{4,2},{5,3},{6,4},{7,5},{8,14},{9,15},{10,... | collective-permute-start | bytes 1081352 | tf_op jit(solution)/shard_map/ppermute | solution.py:346
  55.9 0.7 copy-start.3
  55.9 0.9 copy-start.4
